TPU v7x, 128 devices: a whole 4x4x4 slice. The times are simulated.
128 devices in a mesh: dp: 32 (over x, z, core), tp: 4 (over y).
Axes of the slice: x: 4, y: 4, z: 4, core: 2. Of those that a mesh axis runs over, the one named last changes fastest.
Arguments:
- node_embed: bfloat16 [3, 32, 8, 7168], P(None, 'dp', None, 'tp'), may hold values from -8 to 8
- embed_gain: float32 [7168], P('tp'), may hold values from 0.3 to 4.5
- root_hidden: bfloat16 [32, 7168], P('dp', 'tp'), may hold values from -6 to 6
- parents: int32 [2, 32, 8], P(None, 'dp'), may hold values from 0 to 7
- queries: bfloat16 [3, 32, 8, 128, 576], P(None, 'dp', None, 'tp'), may hold values from -24 to 24
- cache: bfloat16 [32, 4096, 576], P('dp'), may hold values from -4 to 4
- cache_len: int32 [32], P('dp'), may hold values from 512 to 4096, as said below
- value_up: bfloat16 [128, 512, 128], P('tp'), may hold values from -1 to 1
- out_proj: bfloat16 [16384, 7168], P('tp', 'dp'), may hold values from -0.046875 to 0.046875
- moe_gain: float32 [7168], P('tp'), may hold values from 0.1 to 1.9
- router: bfloat16 [7168, 32], P('tp'), may hold values from -0.0625 to 0.0625
- expert_ids: int32 [3, 32, 8, 8], P(None, 'dp'), may hold values from 0 to 31, all different within a row; in each aligned block of 8 rows (0 to 7, 8 to 15, ..., all dimensions but the last counted through in order) at most 4 rows name the same one
- w_gate: bfloat16 [32, 7168, 1024], P('dp', None, 'tp'), may hold values from -0.0625 to 0.0625
- w_up: bfloat16 [32, 7168, 1024], P('dp', None, 'tp'), may hold values from -0.0625 to 0.0625
- w_down: bfloat16 [32, 1024, 7168], P('dp', 'tp'), may hold values from -0.1875 to 0.1875
Outputs:
- drafted: bfloat16 [3, 32, 8, 7168], P(None, 'dp', None, 'tp')
Inputs may be any that keep to these rules, and one draw needn't show every extreme that they name: `cache_len`: request 0 holds exactly 4096 cached tokens. `expert_ids`: each node names 8 different experts. At one depth the nodes of the 1 request of one index of dp name no expert more than 4 times, and in some of these blocks an expert is named exactly 4 times.
All inputs are finite; a program needn't handle non-finite values.
Results may differ from a plain program's by a relative error of at most 0.017.
Values may be sent and summed in bfloat16 or wider, within the bound.
No kernel may reach another device: no remote copies, remote signals or barrier semaphores. Data moves between devices by JAX's collectives and lax.ppermute only.
A program may use at most 128 MiB of HBM per device.

v0:
```python
import jax
import jax.numpy as jnp
from jax import lax
from jax.sharding import PartitionSpec as P

EPS = 1e-06
ROUTE_SCALE = 2.5


def attend_request(query_block, cache_block, length, value_up, score_scale):
    depths, nodes, heads_dev, width_qk = query_block.shape
    latent = value_up.shape[1]
    query_rows = query_block.reshape(-1, width_qk)
    scores = (
        jnp.einsum("qk,ck->qc", query_rows, cache_block, preferred_element_type=jnp.float32)
        * score_scale
    )
    valid = jnp.arange(cache_block.shape[0], dtype=jnp.int32) < length
    scores = jnp.where(valid[None, :], scores, -jnp.inf)
    highest = jnp.max(scores, axis=1, keepdims=True)
    weights = jnp.exp(scores - highest)
    probs = (weights / jnp.sum(weights, axis=1, keepdims=True)).astype(jnp.bfloat16)
    latent_out = jnp.dot(probs, cache_block[:, :latent], preferred_element_type=jnp.float32).astype(
        jnp.bfloat16
    )
    latent_out = latent_out.reshape(depths * nodes, heads_dev, latent)
    mixed = jnp.einsum("nhl,hld->nhd", latent_out, value_up, preferred_element_type=jnp.float32)
    return mixed.astype(jnp.bfloat16).reshape(depths, nodes, -1)


def expert_core(full_rows, w_gate, w_up, down_local):
    sources, count, width = full_rows.shape
    input_rows = full_rows.reshape(-1, width)
    gate = jnp.dot(input_rows, w_gate[0], preferred_element_type=jnp.float32)
    upward = jnp.dot(input_rows, w_up[0], preferred_element_type=jnp.float32)
    activation = (jax.nn.silu(gate) * upward).astype(jnp.bfloat16)
    partial_out = jnp.dot(activation, down_local[0], preferred_element_type=jnp.float32)
    summed = lax.psum_scatter(
        partial_out.astype(jnp.bfloat16), "tp", scatter_dimension=1, tiled=True
    )
    return summed.reshape(sources, count, -1)


def local(
    node_embed,
    embed_gain,
    root_hidden,
    parents,
    queries,
    cache,
    cache_len,
    value_up,
    out_proj,
    moe_gain,
    router,
    expert_ids,
    w_gate,
    w_up,
    w_down,
):
    depths, req_dev, nodes, quarter = node_embed.shape
    groups = lax.axis_size("dp")
    width = quarter * lax.axis_size("tp")
    top_routes = expert_ids.shape[3]
    node_rows = req_dev * nodes
    capacity = min(node_rows, 2 * node_rows * top_routes // groups)
    latent = value_up.shape[1]
    score_scale = (value_up.shape[2] + cache.shape[2] - latent) ** (-0.5)
    heads_all = lax.map(
        lambda item: attend_request(item[0], item[1], item[2], value_up, score_scale),
        (jnp.moveaxis(queries, 1, 0), cache, cache_len),
    )
    heads_all = jnp.moveaxis(heads_all, 0, 1)
    embed = node_embed.astype(jnp.float32)
    embed_sq = lax.psum(jnp.sum(embed * embed, axis=-1), "tp")
    embed_inv = 1.0 / jnp.sqrt(embed_sq / width + EPS)
    normed = embed * embed_inv[..., None] * embed_gain
    slot_index = jnp.arange(groups * capacity, dtype=jnp.int32)
    expert_index = jnp.arange(groups, dtype=jnp.int32)
    node_index = jnp.arange(nodes, dtype=jnp.int32)
    router_wide = router.astype(jnp.float32)
    previous = jnp.broadcast_to(root_hidden[:, None, :], (req_dev, nodes, quarter))
    drafted = []
    for depth in range(depths):
        if depth > 0:
            picker = (parents[depth - 1][:, :, None] == node_index).astype(jnp.bfloat16)
            previous = jnp.einsum(
                "rnm,rmd->rnd", picker, drafted[-1], preferred_element_type=jnp.float32
            )
        head_local = heads_all[depth].reshape(node_rows, -1)
        columns = jnp.dot(
            lax.all_gather(head_local, "dp", axis=0, tiled=True),
            out_proj,
            preferred_element_type=jnp.float32,
        )
        spread = lax.all_to_all(columns, "dp", split_axis=0, concat_axis=1, tiled=True)
        attn_out = lax.psum_scatter(spread, "tp", scatter_dimension=1, tiled=True).astype(
            jnp.bfloat16
        )
        hidden_state = (
            normed[depth]
            + previous.astype(jnp.float32)
            + attn_out.reshape(req_dev, nodes, quarter).astype(jnp.float32)
        ).astype(jnp.bfloat16)
        state_rows = hidden_state.reshape(node_rows, quarter).astype(jnp.float32)
        partial_sq = jnp.sum(state_rows * state_rows, axis=1)
        partial_logits = jnp.dot(
            state_rows * moe_gain, router_wide, precision=lax.Precision.HIGHEST
        )
        total_sq = lax.psum(partial_sq, "tp")
        inv_rms = 1.0 / jnp.sqrt(total_sq / width + EPS)
        logits = lax.psum(partial_logits * inv_rms[:, None], "tp")
        moe_in = (state_rows * inv_rms[:, None] * moe_gain).astype(jnp.bfloat16)
        chosen_ids = expert_ids[depth].reshape(node_rows, top_routes)
        named = chosen_ids[:, :, None] == expert_index
        chosen = jax.nn.sigmoid(jnp.sum(jnp.where(named, logits[:, None, :], 0.0), axis=2))
        route_w = chosen / jnp.sum(chosen, axis=1, keepdims=True) * ROUTE_SCALE
        named_count = named.reshape(node_rows * top_routes, groups).astype(jnp.int32)
        ranking = jnp.sum((jnp.cumsum(named_count, axis=0) - named_count) * named_count, axis=1)
        target = chosen_ids.reshape(-1) * capacity + ranking
        placed = (target[:, None] == slot_index).reshape(node_rows, top_routes, groups * capacity)
        table = jnp.sum(placed.astype(jnp.float32), axis=1).astype(jnp.bfloat16)
        mixing = jnp.sum(jnp.where(placed, route_w[:, :, None], 0.0), axis=1)
        full_in = lax.all_gather(moe_in, "tp", axis=1, tiled=True)
        outgoing = jnp.einsum("rs,rd->sd", table, full_in, preferred_element_type=jnp.float32)
        outgoing = outgoing.astype(jnp.bfloat16).reshape(groups, capacity, width)
        answered = expert_core(
            lax.all_to_all(outgoing, "dp", split_axis=0, concat_axis=0, tiled=True),
            w_gate,
            w_up,
            w_down,
        )
        returned = lax.all_to_all(answered, "dp", split_axis=0, concat_axis=0, tiled=True)
        moe_out = jnp.dot(
            mixing,
            returned.reshape(groups * capacity, quarter).astype(jnp.float32),
            precision=lax.Precision.HIGHEST,
        )
        drafted.append((state_rows + moe_out).astype(jnp.bfloat16).reshape(req_dev, nodes, quarter))
    return jnp.stack(drafted)


def solution(mesh):
    placed = (
        P(None, "dp", None, "tp"),
        P("tp"),
        P("dp", "tp"),
        P(None, "dp", None),
        P(None, "dp", None, "tp", None),
        P("dp", None, None),
        P("dp"),
        P("tp", None, None),
        P("tp", "dp"),
        P("tp"),
        P("tp", None),
        P(None, "dp", None, None),
        P("dp", None, "tp"),
        P("dp", None, "tp"),
        P("dp", "tp", None),
    )
    return jax.shard_map(
        local, mesh=mesh, in_specs=placed, out_specs=P(None, "dp", None, "tp"), check_vma=False
    )
```

profile of v0, /device:TPU:1, one launch (start us, length us, event | category | flops | bytes accessed | tf_op | source)
XLA Modules:
  0.0 513.8 jit_solution(9748893064171476430)
XLA Ops:
  7.3 7.5 %fusion = (f32[768]{0:T(1024)S(1)}, f32[768,4096]{1,0:T(8,128)S(1)}) fusion(pred[4096]{0:T(1024)(128)(4,1)S(1)} %iota_compare_fusion.9, bf16[768,576]{1,0:T(8,128)(2,1)} %bitcast.147, bf16[1,4096,576]{1,2,0:T(8,128)(2,1)} %param.20), kind=kOutput, calls=%fused_computation.3 | convolution fusion | flops 3633315072 | bytes 18193408 | tf_op jit(solution)/shard_map/while/body/eval_jaxpr/qk,ck->qc/dot_general | solution.py:15
  23.6 47.7 %all-gather.4.cloned.1.call-done = bf16[256,4096]{1,0:T(8,128)(2,1)} async-done(((bf16[8,4096]{1,0:T(8,128)(2,1)}), bf16[256,4096]{1,0:T(8,128)(2,1)}) %all-gather.4.cloned.1.call-update) | async-done | bytes 2097168 | tf_op jit(solution)/shard_map/all_gather | solution.py:92
  73.6 14.0 %all_to_all.87 = f32[32,8,224]{2,1,0:T(8,128)S(1)} all-to-all(f32[32,8,224]{2,1,0:T(8,128)S(1)} %convolution_bitcast_fusion.2), channel_id=1, replica_groups=mesh['dp'=32,'tp'=4] {'dp'}, dimensions={0} | all-to-all | bytes 458752 | tf_op jit(solution)/shard_map/all_to_all | solution.py:96
  89.5 8.4 %psum.49 = f32[3,1,8]{2,0,1:T(4,128)S(1)} all-reduce(f32[3,1,8]{2,0,1:T(4,128)S(1)} %bitcast.145), channel_id=1, replica_groups=mesh['dp'=32,'tp'=4] {'tp'}, use_global_device_ids=true, to_apply=%region_1.2 | all-reduce | flops 24 | bytes 192 | tf_op jit(solution)/shard_map/psum | solution.py:75
  99.7 4.7 reduce-scatter.7.cloned.1.call-done
  105.4 7.0 %psum.50 = f32[8]{0:T(128)S(1)} all-reduce(f32[8]{0:T(128)S(1)} %get-tuple-element.29), channel_id=1, replica_groups=mesh['dp'=32,'tp'=4] {'tp'}, use_global_device_ids=true, to_apply=%region_8.9 | all-reduce | flops 8 | bytes 64 | tf_op jit(solution)/shard_map/psum | solution.py:110
  112.6 6.5 %psum.51 = f32[8,32]{1,0:T(8,128)S(1)} all-reduce(f32[8,32]{1,0:T(8,128)S(1)} %convolution_multiply_fusion.2), channel_id=1, replica_groups=mesh['dp'=32,'tp'=4] {'tp'}, use_global_device_ids=true, to_apply=%region_9.10 | all-reduce | flops 256 | bytes 2048 | tf_op jit(solution)/shard_map/psum | solution.py:112
  119.2 9.6 %all_gather.19 = bf16[8,7168]{1,0:T(8,128)(2,1)S(1)} all-gather(bf16[8,1792]{1,0:T(8,128)(2,1)S(1)} %fusion.80), channel_id=1, replica_groups=mesh['dp'=32,'tp'=4] {'tp'}, dimensions={1}, use_global_device_ids=true | all-gather | bytes 143360 | tf_op jit(solution)/shard_map/all_gather | solution.py:124
  131.2 4.1 reshape.328
  135.3 41.8 %all_to_all.88 = bf16[32,4,7168]{2,1,0:T(4,128)(2,1)} all-to-all(bf16[32,4,7168]{2,1,0:T(4,128)(2,1)} %reshape.328), channel_id=1, replica_groups=mesh['dp'=32,'tp'=4] {'dp'}, dimensions={0} | all-to-all | bytes 3670016 | tf_op jit(solution)/shard_map/all_to_all | solution.py:128
  184.2 7.1 %convolution_convert_fusion.4 = bf16[128,7168]{1,0:T(8,128)(2,1)} fusion(bf16[1,256,7168]{2,1,0:T(8,128)(2,1)} %param.29, bf16[128,7168]{1,0:T(8,128)(2,1)} %reshape.329, bf16[1,7168,256]{2,1,0:T(8,128)(2,1)} %param.28, f32[128,256]{1,0:T(8,128)S(1)} %fusion.17), kind=kOutput, calls=%fused_computation.9 | convolution fusion | flops 940638208 | bytes 11141120 | tf_op jit(solution)/shard_map/dot_general | solution.py:37
  193.8 12.6 %all_to_all.89 = f32[32,8,224]{2,1,0:T(8,128)S(1)} all-to-all(f32[32,8,224]{2,1,0:T(8,128)S(1)} %convolution_bitcast_fusion.1), channel_id=1, replica_groups=mesh['dp'=32,'tp'=4] {'dp'}, dimensions={0} | all-to-all | bytes 458752 | tf_op jit(solution)/shard_map/all_to_all | solution.py:96
  207.4 7.7 %reduce-scatter.9.cloned.1.call-done = bf16[128,1792]{1,0:T(8,128)(2,1)} async-done(((bf16[128,7168]{1,0:T(8,128)(2,1)}), bf16[128,1792]{1,0:T(8,128)(2,1)}) %reduce-scatter.9.cloned.1.call-update) | async-done | bytes 458768 | tf_op jit(solution)/shard_map/reduce_scatter | solution.py:38
  217.0 7.6 %all-to-all-start.2 = ((bf16[32,4,1792]{2,1,0:T(4,128)(2,1)}), bf16[32,4,1792]{2,1,0:T(4,128)(2,1)S(1)}, u32[]{:S(2)}, u32[]{:S(2)}) async-start(bf16[32,4,1792]{2,1,0:T(4,128)(2,1)} %reshape.330), calls=%async_computation.4 | async-start | bytes 917504 | tf_op jit(solution)/shard_map/all_to_all | solution.py:133
  225.3 10.3 %all-to-all-done.2 = bf16[32,4,1792]{2,1,0:T(4,128)(2,1)S(1)} async-done(((bf16[32,4,1792]{2,1,0:T(4,128)(2,1)}), bf16[32,4,1792]{2,1,0:T(4,128)(2,1)S(1)}, u32[]{:S(2)}, u32[]{:S(2)}) %all-to-all-start.2) | async-done | bytes 458784 | tf_op jit(solution)/shard_map/all_to_all | solution.py:133
  237.1 6.8 %psum.52 = f32[8]{0:T(128)S(1)} all-reduce(f32[8]{0:T(128)S(1)} %get-tuple-element.47), channel_id=1, replica_groups=mesh['dp'=32,'tp'=4] {'tp'}, use_global_device_ids=true, to_apply=%region_19.20 | all-reduce | flops 8 | bytes 64 | tf_op jit(solution)/shard_map/psum | solution.py:110
  244.1 6.6 %psum.53 = f32[8,32]{1,0:T(8,128)S(1)} all-reduce(f32[8,32]{1,0:T(8,128)S(1)} %convolution_multiply_fusion.1), channel_id=1, replica_groups=mesh['dp'=32,'tp'=4] {'tp'}, use_global_device_ids=true, to_apply=%region_20.21 | all-reduce | flops 256 | bytes 2048 | tf_op jit(solution)/shard_map/psum | solution.py:112
  250.8 9.5 %all_gather.21 = bf16[8,7168]{1,0:T(8,128)(2,1)S(1)} all-gather(bf16[8,1792]{1,0:T(8,128)(2,1)S(1)} %multiply_convert_fusion.1), channel_id=1, replica_groups=mesh['dp'=32,'tp'=4] {'tp'}, dimensions={1}, use_global_device_ids=true | all-gather | bytes 143360 | tf_op jit(solution)/shard_map/all_gather | solution.py:124
  266.8 41.4 %all_to_all.90 = bf16[32,4,7168]{2,1,0:T(4,128)(2,1)} all-to-all(bf16[32,4,7168]{2,1,0:T(4,128)(2,1)} %reshape.332), channel_id=1, replica_groups=mesh['dp'=32,'tp'=4] {'dp'}, dimensions={0} | all-to-all | bytes 3670016 | tf_op jit(solution)/shard_map/all_to_all | solution.py:128
  315.4 7.1 %convolution_convert_fusion.2 = bf16[128,7168]{1,0:T(8,128)(2,1)} fusion(bf16[1,256,7168]{2,1,0:T(8,128)(2,1)} %param.29, bf16[128,7168]{1,0:T(8,128)(2,1)} %reshape.333, bf16[1,7168,256]{2,1,0:T(8,128)(2,1)} %param.28, f32[128,256]{1,0:T(8,128)S(1)} %fusion.15), kind=kOutput, calls=%fused_computation.7 | convolution fusion | flops 940638208 | bytes 11141120 | tf_op jit(solution)/shard_map/dot_general | solution.py:37
  329.4 16.7 %reduce-scatter.13.cloned.1.call-done = bf16[128,1792]{1,0:T(8,128)(2,1)} async-done(((bf16[128,7168]{1,0:T(8,128)(2,1)}), bf16[128,1792]{1,0:T(8,128)(2,1)}) %reduce-scatter.13.cloned.1.call-update) | async-done | bytes 458768 | tf_op jit(solution)/shard_map/reduce_scatter | solution.py:38
  348.0 7.6 %all-to-all-start.5 = ((bf16[32,4,1792]{2,1,0:T(4,128)(2,1)}), bf16[32,4,1792]{2,1,0:T(4,128)(2,1)S(1)}, u32[]{:S(2)}, u32[]{:S(2)}) async-start(bf16[32,4,1792]{2,1,0:T(4,128)(2,1)} %reshape.334), calls=%async_computation.9 | async-start | bytes 917504 | tf_op jit(solution)/shard_map/all_to_all | solution.py:133
  356.7 9.9 %all-to-all-done.5 = bf16[32,4,1792]{2,1,0:T(4,128)(2,1)S(1)} async-done(((bf16[32,4,1792]{2,1,0:T(4,128)(2,1)}), bf16[32,4,1792]{2,1,0:T(4,128)(2,1)S(1)}, u32[]{:S(2)}, u32[]{:S(2)}) %all-to-all-start.5) | async-done | bytes 458784 | tf_op jit(solution)/shard_map/all_to_all | solution.py:133
  367.0 9.7 %reduce-scatter.15.cloned.1.call-done = f32[8,1792]{1,0:T(8,128)} async-done(((f32[8,7168]{1,0:T(8,128)}), f32[8,1792]{1,0:T(8,128)}) %reduce-scatter.15.cloned.1.call-update) | async-done | bytes 57360 | tf_op jit(solution)/shard_map/reduce_scatter | solution.py:97
  377.7 7.0 %psum.54 = f32[8]{0:T(128)S(1)} all-reduce(f32[8]{0:T(128)S(1)} %get-tuple-element.49), channel_id=1, replica_groups=mesh['dp'=32,'tp'=4] {'tp'}, use_global_device_ids=true, to_apply=%region_30.31 | all-reduce | flops 8 | bytes 64 | tf_op jit(solution)/shard_map/psum | solution.py:110
  385.0 9.1 %all_gather.23 = bf16[8,7168]{1,0:T(8,128)(2,1)S(1)} all-gather(bf16[8,1792]{1,0:T(8,128)(2,1)S(1)} %multiply_convert_fusion), channel_id=1, replica_groups=mesh['dp'=32,'tp'=4] {'tp'}, dimensions={1}, use_global_device_ids=true | all-gather | bytes 143360 | tf_op jit(solution)/shard_map/all_gather | solution.py:124
  394.1 6.4 %psum.55 = f32[8,32]{1,0:T(8,128)S(1)} all-reduce(f32[8,32]{1,0:T(8,128)S(1)} %convolution_multiply_fusion), channel_id=1, replica_groups=mesh['dp'=32,'tp'=4] {'tp'}, use_global_device_ids=true, to_apply=%region_31.32 | all-reduce | flops 256 | bytes 2048 | tf_op jit(solution)/shard_map/psum | solution.py:112
  402.9 4.1 reshape.336
  407.0 42.4 %all_to_all.91 = bf16[32,4,7168]{2,1,0:T(4,128)(2,1)} all-to-all(bf16[32,4,7168]{2,1,0:T(4,128)(2,1)} %reshape.336), channel_id=1, replica_groups=mesh['dp'=32,'tp'=4] {'dp'}, dimensions={0} | all-to-all | bytes 3670016 | tf_op jit(solution)/shard_map/all_to_all | solution.py:128
  456.6 7.1 %convolution_convert_fusion = bf16[128,7168]{1,0:T(8,128)(2,1)} fusion(bf16[1,256,7168]{2,1,0:T(8,128)(2,1)} %param.29, bf16[128,7168]{1,0:T(8,128)(2,1)} %reshape.337, bf16[1,7168,256]{2,1,0:T(8,128)(2,1)} %param.28, f32[128,256]{1,0:T(8,128)S(1)} %fusion.13), kind=kOutput, calls=%fused_computation.5 | convolution fusion | flops 940638208 | bytes 11141120 | tf_op jit(solution)/shard_map/dot_general | solution.py:37
  463.7 23.0 %reduce-scatter.17.cloned.1.call-done = bf16[128,1792]{1,0:T(8,128)(2,1)} async-done(((bf16[128,7168]{1,0:T(8,128)(2,1)}), bf16[128,1792]{1,0:T(8,128)(2,1)}) %reduce-scatter.17.cloned.1.call-update) | async-done | bytes 458768 | tf_op jit(solution)/shard_map/reduce_scatter | solution.py:38
  487.8 18.4 %all_to_all.92 = bf16[32,4,1792]{2,1,0:T(4,128)(2,1)S(1)} all-to-all(bf16[32,4,1792]{2,1,0:T(4,128)(2,1)S(1)} %reshape.338), channel_id=1, replica_groups=mesh['dp'=32,'tp'=4] {'dp'}, dimensions={0} | all-to-all | bytes 917504 | tf_op jit(solution)/shard_map/all_to_all | solution.py:133
  (123 shorter events, 70.0 us)
Async XLA Ops:
  6.5 64.8 %copy-start = (bf16[4096,224]{0,1:T(8,128)(2,1)S(1)}, bf16[4096,224]{0,1:T(8,128)(2,1)}, u32[]{:S(2)}) copy-start(bf16[4096,224]{0,1:T(8,128)(2,1)} %param.23) | copy-start | bytes 5505028
  6.5 64.8 %all-gather.4.cloned.1.call-start = ((), (), s32[]{:S(2)}) async-start(), calls=%async_computation.15 | async-start | bytes 2162688 | tf_op jit(solution)/shard_map/all_gather | solution.py:92
  14.8 3.2 copy-start.9
  18.1 3.6 copy-start.1
  22.8 66.6 %copy-start.3 = (bf16[3,1,8,1792]{3,2,1,0:T(8,128)(2,1)S(1)}, bf16[3,1,8,1792]{3,2,1,0:T(8,128)(2,1)}, u32[]{:S(2)}) copy-start(bf16[3,1,8,1792]{3,2,1,0:T(8,128)(2,1)} %param.15) | copy-start | bytes 258052
  22.8 75.2 %copy-start.7 = (bf16[1,1792]{1,0:T(2,128)(2,1)S(1)}, bf16[1,1792]{1,0:T(2,128)(2,1)}, u32[]{:S(2)}) copy-start(bf16[1,1792]{1,0:T(2,128)(2,1)} %param.17) | copy-start | bytes 10756
  22.8 75.2 %copy-start.5 = (s32[3,1,8,8]{3,2,1,0:T(8,128)S(1)}, s32[3,1,8,8]{3,2,1,0:T(8,128)}, u32[]{:S(2)}) copy-start(s32[3,1,8,8]{3,2,1,0:T(8,128)} %param.26) | copy-start | bytes 2308
  22.8 76.8 %copy-start.6 = (f32[1792]{0:T(1024)S(1)}, f32[1792]{0:T(1024)}, u32[]{:S(2)}) copy-start(f32[1792]{0:T(1024)} %param.16) | copy-start | bytes 21508
  23.5 88.9 %copy-start.2 = (bf16[1792,32]{0,1:T(8,128)(2,1)S(1)}, bf16[1792,32]{0,1:T(8,128)(2,1)}, u32[]{:S(2)}) copy-start(bf16[1792,32]{0,1:T(8,128)(2,1)} %param.25) | copy-start | bytes 344068
  23.5 88.9 %copy-start.4 = (f32[1792]{0:T(1024)S(1)}, f32[1792]{0:T(1024)}, u32[]{:S(2)}) copy-start(f32[1792]{0:T(1024)} %param.24) | copy-start | bytes 21508
  23.5 80.9 %reduce-scatter.7.cloned.1.call-start = ((), (), s32[]{:S(2)}) async-start(), calls=%async_computation.16 | async-start | bytes 286720 | tf_op jit(solution)/shard_map/reduce_scatter | solution.py:97
  88.6 102.8 %all-gather.6.cloned.1.call-start = ((), (), s32[]{:S(2)}) async-start(), calls=%async_computation.18 | async-start | bytes 2162688 | tf_op jit(solution)/shard_map/all_gather | solution.py:92
  89.4 125.7 %reduce-scatter.9.cloned.1.call-start = ((), (), s32[]{:S(2)}) async-start(), calls=%async_computation.17 | async-start | bytes 2293760 | tf_op jit(solution)/shard_map/reduce_scatter | solution.py:38
  191.4 33.9 %copy-start.8 = (s32[2,1,8]{2,1,0:T(1,128)S(1)}, s32[2,1,8]{2,1,0:T(1,128)}, u32[]{:S(2)}) copy-start(s32[2,1,8]{2,1,0:T(1,128)} %param.18) | copy-start | bytes 196
  191.4 44.6 %reduce-scatter.11.cloned.1.call-start = ((), (), s32[]{:S(2)}) async-start(), calls=%async_computation.19 | async-start | bytes 286720 | tf_op jit(solution)/shard_map/reduce_scatter | solution.py:97
  217.0 18.6 %all-to-all-start.2 = ((bf16[32,4,1792]{2,1,0:T(4,128)(2,1)}), bf16[32,4,1792]{2,1,0:T(4,128)(2,1)S(1)}, u32[]{:S(2)}, u32[]{:S(2)}) async-start(bf16[32,4,1792]{2,1,0:T(4,128)(2,1)} %reshape.330), calls=%async_computation.4 | async-start | bytes 917504 | tf_op jit(solution)/shard_map/all_to_all | solution.py:133
  224.6 97.9 %all-gather.8.cloned.1.call-start = ((), (), s32[]{:S(2)}) async-start(), calls=%async_computation.21 | async-start | bytes 2162688 | tf_op jit(solution)/shard_map/all_gather | solution.py:92
  225.2 120.9 %reduce-scatter.13.cloned.1.call-start = ((), (), s32[]{:S(2)}) async-start(), calls=%async_computation.20 | async-start | bytes 2293760 | tf_op jit(solution)/shard_map/reduce_scatter | solution.py:38
  325.5 22.5 %all-to-all-start.6 = ((f32[32,8,224]{2,1,0:T(8,128)}), f32[32,8,224]{2,1,0:T(8,128)S(1)}, u32[]{:S(2)}, u32[]{:S(2)}) async-start(f32[32,8,224]{2,1,0:T(8,128)} %convolution_bitcast_fusion), calls=%async_computation.10 | async-start | bytes 524288 | tf_op jit(solution)/shard_map/all_to_all | solution.py:96
  348.0 18.6 %all-to-all-start.5 = ((bf16[32,4,1792]{2,1,0:T(4,128)(2,1)}), bf16[32,4,1792]{2,1,0:T(4,128)(2,1)S(1)}, u32[]{:S(2)}, u32[]{:S(2)}) async-start(bf16[32,4,1792]{2,1,0:T(4,128)(2,1)} %reshape.334), calls=%async_computation.9 | async-start | bytes 917504 | tf_op jit(solution)/shard_map/all_to_all | solution.py:133
  355.6 21.0 %reduce-scatter.15.cloned.1.call-start = ((), (), s32[]{:S(2)}) async-start(), calls=%async_computation.22 | async-start | bytes 286720 | tf_op jit(solution)/shard_map/reduce_scatter | solution.py:97
  356.6 130.1 %reduce-scatter.17.cloned.1.call-start = ((), (), s32[]{:S(2)}) async-start(), calls=%async_computation.23 | async-start | bytes 2293760 | tf_op jit(solution)/shard_map/reduce_scatter | solution.py:38
Sparse Core Ops, SparseCore 0:
  23.7 47.5 all-gather.3
  88.8 15.6 reduce-scatter.6
  107.0 46.4 all-gather.5
  191.5 23.5 reduce-scatter.8
  217.4 18.5 reduce-scatter.10
  238.1 45.7 all-gather.7
  322.6 23.4 reduce-scatter.12
  358.8 17.7 reduce-scatter.14
  463.8 22.8 reduce-scatter.16
where the time goes:
time: 516 us; the launch traced here: 514 us
  blocking collectives  248 us (48%)
  waiting for transfers between devices  131 us (25%)
  matrix products  60.1 us (12%)
  local copies, waits for them, and re-layouts  33.3 us (6%)
  starting transfers between devices  19.4 us (4%)
  between operations  14.4 us (3%)
  other arithmetic  7.8 us (2%)
    all_to_all x3, blocking collectives, local(): lax.all_to_all(outgoing, 'dp', split_axis=0, concat_axis=0, tiled=True)  126 us
    all_gather x3, waiting for transfers between devices, local(): lax.all_gather(head_local, 'dp', axis=0, tiled=True)  47.7 us
    reduce_scatter x3, waiting for transfers between devices, expert_core(): lax.psum_scatter(partial_out.astype(jnp.bfloat16), 'tp', scatter_dimensio...  47.5 us
    all_gather x3, blocking collectives, local(): full_in = lax.all_gather(moe_in, 'tp', axis=1, tiled=True)  28.2 us
    all_to_all x2, blocking collectives, local(): lax.all_to_all(columns, 'dp', split_axis=0, concat_axis=1, tiled=True)  26.6 us
    dot_general x3, matrix products, expert_core(): jnp.dot(activation, down_local[0], preferred_element_type=jnp.float32)  21.2 us
    psum x3, blocking collectives, local(): total_sq = lax.psum(partial_sq, 'tp')  20.9 us
    all_to_all x2, waiting for transfers between devices, local(): lax.all_to_all(answered, 'dp', split_axis=0, concat_axis=0, tiled=True)  20.2 us
  transfers between devices with their start and end apart: 12, of which 8 were waited for; matrix products, arithmetic and copies ran while one was open for 11% of the time, Pallas kernels for 0%

commit v1 on v0

v1 whole, which is shorter than its diff:
```python
import functools

import jax
import jax.numpy as jnp
from jax import lax
from jax.experimental import pallas as pl
from jax.experimental.pallas import tpu as pltpu
from jax.sharding import PartitionSpec as P

EPS = 1e-06
ROUTE_SCALE = 2.5
SLOTS = 4
HALVES = 2
F32 = jnp.float32
BF16 = jnp.bfloat16
VMEM_BYTES = 48 * 1024 * 1024


def iota(shape, dim):
    return lax.broadcasted_iota(jnp.int32, shape, dim)


def split3(value):
    high = value.astype(BF16)
    rest = value - high.astype(F32)
    middle = rest.astype(BF16)
    low = (rest - middle.astype(F32)).astype(BF16)
    return high, middle, low


def pack_matrix(rows, forward):
    shape = (rows, rows)
    packed, mixed = iota(shape, 0 if forward else 1), iota(shape, 1 if forward else 0)
    per_half = rows // HALVES
    half = packed // per_half
    place = packed - half * per_half
    request = place // SLOTS
    source = request * (HALVES * SLOTS) + half * SLOTS + (place - request * SLOTS)
    return (source == mixed).astype(BF16)


def routing(ids, experts):
    nodes, top = ids.shape
    lane = iota((nodes, experts), 1)
    named = jnp.zeros((nodes, experts), F32)
    for route in range(top):
        named = named + (ids[:, route : route + 1] == lane).astype(F32)
    above = (iota((nodes, nodes), 1) < iota((nodes, nodes), 0)).astype(BF16)
    rank = jnp.dot(above, named.astype(BF16), preferred_element_type=F32)
    columns = experts * HALVES * SLOTS
    spread = (iota((experts, columns), 1) // (HALVES * SLOTS) == iota((experts, columns), 0)).astype(BF16)
    order = jnp.dot(((rank + 1.0) * named).astype(BF16), spread, preferred_element_type=F32)
    column = iota((nodes, columns), 1)
    slot = column - (column // SLOTS) * SLOTS
    placed = order == (slot + 1).astype(F32)
    half = (column // SLOTS) - (column // (HALVES * SLOTS)) * HALVES
    return named, spread, placed, half


def combine(rec, state, stats, ids, experts, width):
    nodes = ids.shape[0]
    named, spread, placed, half = routing(ids, experts)
    logits = stats[:, :experts]
    inv_rms = 1.0 / jnp.sqrt(stats[:, experts : experts + 1] / width + EPS)
    chosen = named / (1.0 + jnp.exp(-(logits * inv_rms)))
    weight = chosen / jnp.sum(chosen, axis=1, keepdims=True) * ROUTE_SCALE
    wide = jnp.dot(
        jnp.concatenate(split3(weight), axis=0), spread, preferred_element_type=F32
    )
    zero = jnp.zeros_like(placed, dtype=F32)
    pieces = []
    for h in range(HALVES):
        for piece in range(3):
            part = wide[piece * nodes : (piece + 1) * nodes]
            pieces.append(jnp.where(placed & (half == h), part, zero))
    mixing = jnp.concatenate(pieces, axis=0).astype(BF16)
    mixed = jnp.dot(mixing, rec, preferred_element_type=F32)
    outs = []
    for h in range(HALVES):
        base = h * 3 * nodes
        outs.append(
            mixed[base : base + nodes]
            + mixed[base + nodes : base + 2 * nodes]
            + mixed[base + 2 * nodes : base + 3 * nodes]
        )
    moe_out = jnp.concatenate(outs, axis=1)
    return (state.astype(F32) + moe_out).astype(BF16)


def owner_kernel(first, last, experts, width, copies, *refs):
    refs = list(refs)
    if not first:
        rec = refs.pop(0)[...]
        state_ref = refs.pop(0)
        stats = refs.pop(0)[...]
        for _ in range(3):
            stats = stats + refs.pop(0)[...]
        ids = refs.pop(0)[...]
        if not last:
            parents = refs.pop(0)[...]
    if first:
        root = refs.pop(0)[...]
    if not last:
        normed = refs.pop(0)[...]
        attn = refs.pop(0)[...]
        next_ids = refs.pop(0)[...]
        router = refs.pop(0)
    if not first:
        drafted_ref = refs.pop(0)
        drafted = combine(rec, state_ref[...], stats, ids, experts, width)
        drafted_ref[...] = drafted
    if last:
        return
    out_state, out_stats, outgoing = refs
    if first:
        previous = root.astype(F32)
    else:
        wide = drafted.astype(F32)
        previous = jnp.zeros_like(wide)
        for node in range(wide.shape[0]):
            previous = previous + jnp.where(parents == node, wide[node : node + 1, :], 0.0)
    state = (normed + previous + attn.astype(BF16).astype(F32)).astype(BF16)
    out_state[...] = state
    wide = state.astype(F32)
    square = jnp.sum(wide * wide, axis=1, keepdims=True)
    parts = jnp.dot(state, router[...], preferred_element_type=F32)
    logits = parts[:, :experts] + parts[:, experts : 2 * experts] + parts[:, 2 * experts : 3 * experts]
    pad = jnp.zeros((wide.shape[0], 128 - experts - 1), F32)
    out_stats[...] = jnp.concatenate([logits, square, pad], axis=1)
    _, _, placed, half = routing(next_ids, experts)
    table = jnp.concatenate(
        [(placed & (half == h)).astype(F32) for h in range(HALVES)], axis=0
    ).astype(BF16)
    part = wide.shape[1] // HALVES
    halves = jnp.concatenate(
        [wide[:, h * part : (h + 1) * part] for h in range(HALVES)], axis=0
    ).astype(BF16)
    sent = lax.dot_general(table, halves, (((0,), (0,)), ((), ())), preferred_element_type=F32)
    sent = sent.reshape(experts, HALVES * SLOTS, part).astype(BF16)
    for copy in range(copies):
        outgoing[:, copy] = sent


def owner_call(first, last, experts, width, copies, args, nodes, quarter):
    outs = []
    if not first:
        outs.append(jax.ShapeDtypeStruct((nodes, quarter), BF16))
    if not last:
        outs.append(jax.ShapeDtypeStruct((nodes, quarter), BF16))
        outs.append(jax.ShapeDtypeStruct((nodes, 128), F32))
        outs.append(
            jax.ShapeDtypeStruct((experts, copies, HALVES * SLOTS, quarter // HALVES), BF16)
        )
    return pl.pallas_call(
        functools.partial(owner_kernel, first, last, experts, width, copies),
        out_shape=outs,
        compiler_params=pltpu.CompilerParams(vmem_limit_bytes=VMEM_BYTES),
    )(*args)


def expert_kernel(width, x_ref, gain_ref, gate_ref, up_ref, act_ref, pack, inv, total):
    step = pl.program_id(0)
    sources, quarters, group, part = x_ref.shape
    rows = sources * group

    def block(index):
        return x_ref[:, index].astype(F32).reshape(rows, part)

    row_half = (iota((rows, 1), 0) // SLOTS) - (iota((rows, 1), 0) // group) * HALVES

    @pl.when(step == 0)
    def _():
        pack[...] = pack_matrix(rows, True)
        square = jnp.zeros((rows, part), F32)
        for index in range(quarters):
            value = block(index)
            square = square + value * value
        summed = jnp.broadcast_to(jnp.sum(square, axis=1, keepdims=True), (rows, 128))
        other = jnp.where(
            row_half == 0, pltpu.roll(summed, rows - SLOTS, 0), pltpu.roll(summed, SLOTS, 0)
        )
        inv[...] = 1.0 / jnp.sqrt((summed + other) / width + EPS)
        total[...] = jnp.zeros_like(total)

    gain = gain_ref[step]
    scaled = block(step) * inv[:, :1]
    scaled = (scaled * jnp.where(row_half == 0, gain[0:1, :], gain[1:2, :])).astype(BF16)
    packed = jnp.dot(pack[...], scaled, preferred_element_type=F32).astype(BF16)
    per_half = rows // HALVES
    hidden = gate_ref.shape[1]
    for h in range(HALVES):
        piece = packed[h * per_half : (h + 1) * per_half]
        span = slice(h * part, (h + 1) * part)
        total[:, :hidden] += jnp.dot(piece, gate_ref[span, :], preferred_element_type=F32)
        total[:, hidden:] += jnp.dot(piece, up_ref[span, :], preferred_element_type=F32)

    @pl.when(step == pl.num_programs(0) - 1)
    def _():
        gate = total[:, :hidden]
        act_ref[...] = (gate / (1.0 + jnp.exp(-gate)) * total[:, hidden:]).astype(BF16)


def expert_call(width, x, gain, gate, up):
    sources, quarters, group, part = x.shape
    rows = sources * group
    hidden = gate.shape[1]
    block = gate.shape[0] // quarters
    return pl.pallas_call(
        functools.partial(expert_kernel, width),
        grid=(quarters,),
        in_specs=[
            pl.BlockSpec(x.shape, lambda i: (0, 0, 0, 0)),
            pl.BlockSpec(gain.shape, lambda i: (0, 0, 0)),
            pl.BlockSpec((block, hidden), lambda i: (i, 0)),
            pl.BlockSpec((block, hidden), lambda i: (i, 0)),
        ],
        out_specs=pl.BlockSpec((rows // HALVES, hidden), lambda i: (0, 0)),
        out_shape=jax.ShapeDtypeStruct((rows // HALVES, hidden), BF16),
        scratch_shapes=[
            pltpu.VMEM((rows, rows), BF16),
            pltpu.VMEM((rows, 128), F32),
            pltpu.VMEM((rows // HALVES, 2 * hidden), F32),
        ],
        compiler_params=pltpu.CompilerParams(vmem_limit_bytes=VMEM_BYTES),
    )(x, gain, gate, up)


def down_kernel(count, *refs):
    acts, weights, out_ref = refs[:count], refs[count : 2 * count], refs[2 * count]
    total = jnp.dot(acts[0][...], weights[0][...], preferred_element_type=F32)
    for index in range(1, count):
        total = total + jnp.dot(acts[index][...], weights[index][...], preferred_element_type=F32)
    part = total.shape[1] // HALVES
    stacked = jnp.concatenate(
        [total[:, h * part : (h + 1) * part] for h in range(HALVES)], axis=0
    ).astype(BF16)
    unpack = pack_matrix(stacked.shape[0], False)
    out_ref[...] = jnp.dot(unpack, stacked, preferred_element_type=F32).astype(BF16)


def down_call(acts, weights):
    rows = acts[0].shape[0]
    quarter = weights[0].shape[1]
    return pl.pallas_call(
        functools.partial(down_kernel, len(acts)),
        out_shape=jax.ShapeDtypeStruct((rows * HALVES, quarter // HALVES), BF16),
        compiler_params=pltpu.CompilerParams(vmem_limit_bytes=VMEM_BYTES),
    )(*acts, *weights)


def attend_request(query_block, cache_block, length, value_up, score_scale):
    depths, nodes, heads_dev, width_qk = query_block.shape
    latent = value_up.shape[1]
    query_rows = query_block.reshape(-1, width_qk)
    scores = (
        jnp.einsum("qk,ck->qc", query_rows, cache_block, preferred_element_type=F32)
        * score_scale
    )
    valid = jnp.arange(cache_block.shape[0], dtype=jnp.int32) < length
    scores = jnp.where(valid[None, :], scores, -jnp.inf)
    highest = jnp.max(scores, axis=1, keepdims=True)
    weights = jnp.exp(scores - highest)
    probs = (weights / jnp.sum(weights, axis=1, keepdims=True)).astype(BF16)
    latent_out = jnp.dot(probs, cache_block[:, :latent], preferred_element_type=F32).astype(BF16)
    latent_out = latent_out.reshape(depths * nodes, heads_dev, latent)
    mixed = jnp.einsum("nhl,hld->nhd", latent_out, value_up, preferred_element_type=F32)
    return mixed.astype(BF16).reshape(depths, nodes, -1)


def local(
    node_embed,
    embed_gain,
    root_hidden,
    parents,
    queries,
    cache,
    cache_len,
    value_up,
    out_proj,
    moe_gain,
    router,
    expert_ids,
    w_gate,
    w_up,
    w_down,
):
    depths, _, nodes, quarter = node_embed.shape
    groups = lax.axis_size("dp")
    tp = lax.axis_size("tp")
    mine = lax.axis_index("tp")
    width = quarter * tp
    part = quarter // HALVES
    experts = router.shape[1]
    latent = value_up.shape[1]
    score_scale = (value_up.shape[2] + cache.shape[2] - latent) ** (-0.5)
    shifts = {k: [(i, (i + k) % tp) for i in range(tp)] for k in range(1, tp)}

    def share(value):
        return [value] + [lax.ppermute(value, "tp", shifts[k]) for k in range(1, tp)]

    def deal(pick):
        return [pick(mine)] + [
            lax.ppermute(pick((mine + k) % tp), "tp", shifts[k]) for k in range(1, tp)
        ]

    down = deal(lambda i: lax.dynamic_slice(w_down[0], (0, i * quarter), (w_down.shape[1], quarter)))
    embed = node_embed[:, 0].astype(F32)
    embed_sq = sum(share(jnp.sum(embed * embed, axis=-1)))
    normed = embed * (1.0 / jnp.sqrt(embed_sq / width + EPS))[..., None] * embed_gain
    gains = jnp.stack(share(moe_gain.reshape(HALVES, part)))
    gains = gains[(mine - jnp.arange(tp, dtype=jnp.int32)) % tp]
    product = router.astype(F32) * moe_gain[:, None]
    high = lax.reduce_precision(product, 8, 7)
    middle = lax.reduce_precision(product - high, 8, 7)
    low = product - high - middle
    routed = jnp.concatenate(
        [high, middle, low, jnp.zeros((quarter, 128 - 3 * experts), F32)], axis=1
    ).astype(BF16)

    heads_all = attend_request(queries[:, 0], cache[0], cache_len[0], value_up, score_scale)

    def attention_out(depth):
        rows = lax.all_gather(heads_all[depth], "dp", axis=0, tiled=True)
        columns = jnp.dot(rows, out_proj, preferred_element_type=F32).astype(BF16)
        columns = columns.reshape(groups, nodes, -1)
        columns = lax.all_to_all(columns, "dp", split_axis=0, concat_axis=0, tiled=True)
        columns = columns.reshape(tp, groups // tp, nodes, columns.shape[2])
        pieces = deal(lambda i: lax.dynamic_index_in_dim(columns, i, 0, keepdims=False))
        summed = sum(piece.astype(F32) for piece in pieces)
        return jnp.moveaxis(summed, 0, 1).reshape(nodes, quarter)

    attn = [attention_out(depth) for depth in range(depths)]

    drafted = []
    carried = None
    for depth in range(depths + 1):
        first, last = depth == 0, depth == depths
        args = []
        if not first:
            args += list(carried) + [expert_ids[depth - 1, 0]]
            if not last:
                args += [parents[depth - 1, 0][:, None]]
        if first:
            args += [root_hidden]
        if not last:
            args += [normed[depth], attn[depth], expert_ids[depth, 0], routed]
        result = list(owner_call(first, last, experts, width, tp, args, nodes, quarter))
        if not first:
            drafted.append(result.pop(0))
        if last:
            break
        state, stats, outgoing = result
        all_stats = share(stats)
        outgoing = outgoing.reshape(experts * tp, HALVES * SLOTS, part)
        arrived = lax.all_to_all(outgoing, ("dp", "tp"), split_axis=0, concat_axis=0, tiled=True)
        arrived = arrived.reshape(groups, tp, HALVES * SLOTS, part)
        act = expert_call(width, arrived, gains, w_gate[0], w_up[0])
        answer = down_call(share(act), down)
        answer = answer.reshape(groups, HALVES * SLOTS, part)
        returned = lax.all_to_all(answer, "dp", split_axis=0, concat_axis=0, tiled=True)
        carried = [returned.reshape(groups * HALVES * SLOTS, part), state] + all_stats
    return jnp.stack(drafted)[:, None]


def solution(mesh):
    placed = (
        P(None, "dp", None, "tp"),
        P("tp"),
        P("dp", "tp"),
        P(None, "dp", None),
        P(None, "dp", None, "tp", None),
        P("dp", None, None),
        P("dp"),
        P("tp", None, None),
        P("tp", "dp"),
        P("tp"),
        P("tp", None),
        P(None, "dp", None, None),
        P("dp", None, "tp"),
        P("dp", None, "tp"),
        P("dp", "tp", None),
    )
    return jax.shard_map(
        local, mesh=mesh, in_specs=placed, out_specs=P(None, "dp", None, "tp"), check_vma=False
    )
```

time: 516 us -> 423 us (0.82)
  blocking collectives: 248 us -> 71.6 us
  starting transfers between devices: 19.4 us -> 105 us
  matrix products: 60.1 us -> 20 us
  Pallas kernels: 0 us -> 31.1 us
  waiting for transfers between devices: 131 us -> 146 us
  local copies, waits for them, and re-layouts: 33.3 us -> 22.3 us
    all_to_all x6 -> x2, blocking collectives: 171 us -> 71.6 us  [local(): lax.all_to_all(outgoing, ('dp', 'tp'), split_axis=0, concat_axis=0, tiled...]
    reduce_scatter x6 -> x0, waiting for transfers between devices: 61.9 us -> none  [the longest x3 47.5 us: expert_core(): lax.psum_scatter(partial_out.astype(jnp.bfloat16), 'tp', scatter_dimensio...]
    ppermute x0 -> x36, starting transfers between devices: none -> 59.4 us  [the longest x24 43.3 us: share(): lax.ppermute(value, 'tp', shifts[k])]
    ppermute x0 -> x36, waiting for transfers between devices: none -> 59.3 us  [the longest x24 59.2 us: share(): lax.ppermute(value, 'tp', shifts[k])]
    psum x7 -> x0, blocking collectives: 48.8 us -> none  [the longest x3 20.9 us: local(): total_sq = lax.psum(partial_sq, 'tp')]
    dot_general x23 -> x6, matrix products: 60.1 us -> 20 us  [the longest x3 7.8 us: attention_out(): columns = jnp.dot(rows, out_proj, preferred_element_type=F32).astype(BF16)]
    pallas_call x0 -> x10, Pallas kernels: none -> 31.1 us  [the longest x3 16.6 us: expert_call(): pl.pallas_call(functools.partial(expert_kernel, width), grid=(quarters,),...]
    all_gather x3 -> x0, blocking collectives: 28.2 us -> none  [local(): full_in = lax.all_gather(moe_in, 'tp', axis=1, tiled=True)]
  transfers between devices with their start and end apart: 12 -> 46, of which waited for: 8 -> 18; matrix products, arithmetic and copies ran while one was open for 11% -> 6% of each run, Pallas kernels for 0% -> 2%
where the time goes in v1:
time: 423 us; the launch traced here: 418 us
  waiting for transfers between devices  146 us (35%)
  starting transfers between devices  105 us (25%)
  blocking collectives  71.6 us (17%)
  Pallas kernels  31.1 us (7%)
  local copies, waits for them, and re-layouts  22.3 us (5%)
  matrix products  20 us (5%)
  between operations  14.8 us (3%)
  other arithmetic  6.45 us (2%)
    all_to_all x2, blocking collectives, local(): lax.all_to_all(outgoing, ('dp', 'tp'), split_axis=0, concat_axis=0, tiled...  71.6 us
    all_gather x3, waiting for transfers between devices, attention_out(): rows = lax.all_gather(heads_all[depth], 'dp', axis=0, tiled=True)  63.4 us
    ppermute x24, waiting for transfers between devices, share(): lax.ppermute(value, 'tp', shifts[k])  59.2 us
    ppermute x24, starting transfers between devices, share(): lax.ppermute(value, 'tp', shifts[k])  43.3 us
    all_to_all x3, starting transfers between devices, local(): lax.all_to_all(answer, 'dp', split_axis=0, concat_axis=0, tiled=True)  20.1 us
    all_to_all x3, starting transfers between devices, attention_out(): lax.all_to_all(columns, 'dp', split_axis=0, concat_axis=0, tiled=True)  19.6 us
    pallas_call x3, Pallas kernels, expert_call(): pl.pallas_call(functools.partial(expert_kernel, width), grid=(quarters,),...  16.6 us
    ppermute x12, starting transfers between devices, deal(): lax.ppermute(pick((mine + k) % tp), 'tp', shifts[k])  16 us
  transfers between devices with their start and end apart: 46, of which 18 were waited for; matrix products, arithmetic and copies ran while one was open for 6% of the time, Pallas kernels for 2%

profile of v1, /device:TPU:1, one launch (start us, length us, event | category | flops | bytes accessed | tf_op | source)
XLA Modules:
  0.0 417.7 jit_solution(5944488777368657736)
XLA Ops:
  7.3 7.5 %fusion = (f32[768]{0:T(1024)S(1)}, f32[768,4096]{1,0:T(8,128)S(1)}) fusion(pred[4096]{0:T(1024)(128)(4,1)S(1)} %iota_compare_fusion, bf16[768,576]{1,0:T(8,128)(2,1)} %bitcast.147, bf16[1,4096,576]{1,2,0:T(8,128)(2,1)} %param.20), kind=kOutput, calls=%fused_computation.4 | convolution fusion | flops 3633315072 | bytes 18193408 | tf_op jit(solution)/shard_map/qk,ck->qc/dot_general | solution.py:256
  14.8 3.2 fusion.1
  18.1 3.7 fusion.4
  32.3 39.1 %all-gather.4.cloned.1.call-done = bf16[256,4096]{1,0:T(8,128)(2,1)} async-done(((bf16[8,4096]{1,0:T(8,128)(2,1)}), bf16[256,4096]{1,0:T(8,128)(2,1)}) %all-gather.4.cloned.1.call-update) | async-done | bytes 2097168 | tf_op jit(solution)/shard_map/all_gather | solution.py:323
  74.5 5.2 %all-to-all-start = ((bf16[32,8,224]{2,1,0:T(8,128)(2,1)}), bf16[32,8,224]{2,1,0:T(8,128)(2,1)S(1)}, u32[]{:S(2)}, u32[]{:S(2)}) async-start(bf16[32,8,224]{2,1,0:T(8,128)(2,1)} %bitcast.10), calls=%async_computation | async-start | bytes 262144 | tf_op jit(solution)/shard_map/all_to_all | solution.py:326
  79.8 7.7 %all-to-all-done = bf16[32,8,224]{2,1,0:T(8,128)(2,1)S(1)} async-done(((bf16[32,8,224]{2,1,0:T(8,128)(2,1)}), bf16[32,8,224]{2,1,0:T(8,128)(2,1)S(1)}, u32[]{:S(2)}, u32[]{:S(2)}) %all-to-all-start) | async-done | bytes 114720 | tf_op jit(solution)/shard_map/all_to_all | solution.py:326
  92.6 24.3 %all-gather.6.cloned.1.call-done = bf16[256,4096]{1,0:T(8,128)(2,1)} async-done(((bf16[8,4096]{1,0:T(8,128)(2,1)}), bf16[256,4096]{1,0:T(8,128)(2,1)}) %all-gather.6.cloned.1.call-update) | async-done | bytes 2097168 | tf_op jit(solution)/shard_map/all_gather | solution.py:323
  120.0 5.3 %all-to-all-start.3 = ((bf16[32,8,224]{2,1,0:T(8,128)(2,1)}), bf16[32,8,224]{2,1,0:T(8,128)(2,1)S(1)}, u32[]{:S(2)}, u32[]{:S(2)}) async-start(bf16[32,8,224]{2,1,0:T(8,128)(2,1)} %bitcast.35), calls=%async_computation.3 | async-start | bytes 262144 | tf_op jit(solution)/shard_map/all_to_all | solution.py:326
  127.4 5.6 %all-to-all-done.3 = bf16[32,8,224]{2,1,0:T(8,128)(2,1)S(1)} async-done(((bf16[32,8,224]{2,1,0:T(8,128)(2,1)}), bf16[32,8,224]{2,1,0:T(8,128)(2,1)S(1)}, u32[]{:S(2)}, u32[]{:S(2)}) %all-to-all-start.3) | async-done | bytes 114720 | tf_op jit(solution)/shard_map/all_to_all | solution.py:326
  133.0 6.0 %all-to-all-start.1 = ((bf16[128,8,896]{2,1,0:T(8,128)(2,1)}), bf16[128,8,896]{2,1,0:T(8,128)(2,1)}, u32[]{:S(2)}, u32[]{:S(2)}) async-start(bf16[128,8,896]{2,1,0:T(8,128)(2,1)} %bitcast.127), calls=%async_computation.1 | async-start | bytes 3670016 | tf_op jit(solution)/shard_map/all_to_all | solution.py:355
  139.1 3.6 dynamic-slice_bitcast_fusion
  149.0 47.6 %collective-permute-done.6 = f32[2,896]{1,0:T(2,128)S(1)} collective-permute-done((f32[2,896]{1,0:T(2,128)S(1)}, f32[2,896]{1,0:T(2,128)S(1)}, u32[]{:S(2)}, u32[]{:S(2)}) %collective-permute-start.6) | collective-permute-done | bytes 7200 | tf_op jit(solution)/shard_map/ppermute | solution.py:299
  196.5 4.6 %collective-permute-start.8 = (f32[2,896]{1,0:T(2,128)S(1)}, f32[2,896]{1,0:T(2,128)S(1)}, u32[]{:S(2)}, u32[]{:S(2)}) collective-permute-start(f32[2,896]{1,0:T(2,128)S(1)} %reshape.152), channel_id=1, source_target_pairs={{0,3},{1,0},{2,1},{3,2},{4,7},{5,4},{6,5},{7,6},{8,11},{9,8},{10,9... | collective-permute-start | bytes 21512 | tf_op jit(solution)/shard_map/ppermute | solution.py:299
  202.6 3.0 convolution_convert_fusion.1
  207.3 9.1 %all-to-all-start.6 = ((bf16[32,8,224]{2,1,0:T(8,128)(2,1)}), bf16[32,8,224]{2,1,0:T(8,128)(2,1)}, u32[]{:S(2)}, u32[]{:S(2)}) async-start(bf16[32,8,224]{2,1,0:T(8,128)(2,1)} %bitcast.142), calls=%async_computation.6 | async-start | bytes 262144 | tf_op jit(solution)/shard_map/all_to_all | solution.py:326
  219.5 5.9 %shard_map.146.refs_0_ = bf16[128,256]{1,0:T(8,128)(2,1)S(1)} custom-call(bf16[32,4,8,896]{3,2,1,0:T(8,128)(2,1)} %bitcast.19.x_ref, f32[4,2,896]{2,1,0:T(2,128)S(1)} %gather_fusion, bf16[7168,256]{1,0:T(8,128)(2,1)S(1)} %bitcast.120, bf16[7168,256]{1,0:T(8,128)(2,1)} %bitcast.134), custom_call_target="tpu_custom_call" | custom-call | tf_op jit(solution)/shard_map/pallas_call | solution.py:208
  225.4 4.1 collective-permute-start.10
  236.9 2.8 shard_map.147
  240.4 9.7 %all-to-all-start.2 = ((bf16[32,8,896]{2,1,0:T(8,128)(2,1)}), bf16[32,8,896]{2,1,0:T(8,128)(2,1)}, u32[]{:S(2)}, u32[]{:S(2)}) async-start(bf16[32,8,896]{2,1,0:T(8,128)(2,1)} %bitcast.125), calls=%async_computation.2 | async-start | bytes 917504 | tf_op jit(solution)/shard_map/all_to_all | solution.py:360
  252.5 9.9 %collective-permute-start.15 = (f32[8,128]{1,0:T(8,128)}, f32[8,128]{1,0:T(8,128)S(1)}, u32[]{:S(2)}, u32[]{:S(2)}) collective-permute-start(f32[8,128]{1,0:T(8,128)} %copy-done.14), channel_id=1, source_target_pairs={{0,1},{1,2},{2,3},{3,0},{4,5},{5,6},{6,7},{7,4},{8,9},{9,10},{10,1... | collective-permute-start | bytes 12296 | tf_op jit(solution)/shard_map/ppermute | solution.py:299
  272.7 38.7 %all_to_all.45 = bf16[128,8,896]{2,1,0:T(8,128)(2,1)S(1)} all-to-all(bf16[128,8,896]{2,1,0:T(8,128)(2,1)S(1)} %bitcast.129), channel_id=1, replica_groups=mesh['dp'=32,'tp'=4] {'dp','tp'}, dimensions={0} | all-to-all | bytes 3670016 | tf_op jit(solution)/shard_map/all_to_all | solution.py:355
  311.4 5.3 %shard_map.149.refs_0_ = bf16[128,256]{1,0:T(8,128)(2,1)S(1)} custom-call(bf16[32,4,8,896]{3,2,1,0:T(8,128)(2,1)S(1)} %bitcast.124, f32[4,2,896]{2,1,0:T(2,128)S(1)} %gather_fusion, bf16[7168,256]{1,0:T(8,128)(2,1)S(1)} %bitcast.121, bf16[7168,256]{1,0:T(8,128)(2,1)} %bitcast.135), custom_call_target="tpu_custom_call" | custom-call | tf_op jit(solution)/shard_map/pallas_call | solution.py:208
  323.2 2.8 shard_map.150
  326.7 5.6 %all-to-all-start.5 = ((bf16[32,8,896]{2,1,0:T(8,128)(2,1)}), bf16[32,8,896]{2,1,0:T(8,128)(2,1)}, u32[]{:S(2)}, u32[]{:S(2)}) async-start(bf16[32,8,896]{2,1,0:T(8,128)(2,1)} %bitcast.126), calls=%async_computation.5 | async-start | bytes 917504 | tf_op jit(solution)/shard_map/all_to_all | solution.py:360
  333.0 2.8 collective-permute-start.25
  338.7 4.8 %all-to-all-done.5 = bf16[32,8,896]{2,1,0:T(8,128)(2,1)} async-done(((bf16[32,8,896]{2,1,0:T(8,128)(2,1)}), bf16[32,8,896]{2,1,0:T(8,128)(2,1)}, u32[]{:S(2)}, u32[]{:S(2)}) %all-to-all-start.5) | async-done | bytes 458784 | tf_op jit(solution)/shard_map/all_to_all | solution.py:360
  345.7 32.9 %all_to_all.46 = bf16[128,8,896]{2,1,0:T(8,128)(2,1)S(1)} all-to-all(bf16[128,8,896]{2,1,0:T(8,128)(2,1)S(1)} %bitcast.128), channel_id=1, replica_groups=mesh['dp'=32,'tp'=4] {'dp','tp'}, dimensions={0} | all-to-all | bytes 3670016 | tf_op jit(solution)/shard_map/all_to_all | solution.py:355
  378.6 5.3 %shard_map.152.refs_0_ = bf16[128,256]{1,0:T(8,128)(2,1)S(1)} custom-call(bf16[32,4,8,896]{3,2,1,0:T(8,128)(2,1)S(1)} %bitcast.123, f32[4,2,896]{2,1,0:T(2,128)S(1)} %gather_fusion, bf16[7168,256]{1,0:T(8,128)(2,1)S(1)} %bitcast.122, bf16[7168,256]{1,0:T(8,128)(2,1)} %bitcast.136), custom_call_target="tpu_custom_call" | custom-call | tf_op jit(solution)/shard_map/pallas_call | solution.py:208
  390.3 3.5 shard_map.153
  393.9 4.9 %all-to-all-start.8 = ((bf16[32,8,896]{2,1,0:T(8,128)(2,1)}), bf16[32,8,896]{2,1,0:T(8,128)(2,1)S(1)}, u32[]{:S(2)}, u32[]{:S(2)}) async-start(bf16[32,8,896]{2,1,0:T(8,128)(2,1)} %bitcast.62), calls=%async_computation.8 | async-start | bytes 917504 | tf_op jit(solution)/shard_map/all_to_all | solution.py:360
  399.5 2.8 collective-permute-start.34
  405.1 4.8 %all-to-all-done.8 = bf16[32,8,896]{2,1,0:T(8,128)(2,1)S(1)} async-done(((bf16[32,8,896]{2,1,0:T(8,128)(2,1)}), bf16[32,8,896]{2,1,0:T(8,128)(2,1)S(1)}, u32[]{:S(2)}, u32[]{:S(2)}) %all-to-all-start.8) | async-done | bytes 458784 | tf_op jit(solution)/shard_map/all_to_all | solution.py:360
  (171 shorter events, 80.8 us)
Async XLA Ops:
  6.5 64.8 %all-gather.4.cloned.1.call-start = ((), (), s32[]{:S(2)}) async-start(), calls=%async_computation.9 | async-start | bytes 2162688 | tf_op jit(solution)/shard_map/all_gather | solution.py:323
  23.6 93.3 %all-gather.6.cloned.1.call-start = ((), (), s32[]{:S(2)}) async-start(), calls=%async_computation.10 | async-start | bytes 2162688 | tf_op jit(solution)/shard_map/all_gather | solution.py:323
  24.4 178.2 %all-gather.8.cloned.1.call-start = ((), (), s32[]{:S(2)}) async-start(), calls=%async_computation.11 | async-start | bytes 2162688 | tf_op jit(solution)/shard_map/all_gather | solution.py:323
  24.6 7.6 %collective-permute-start = (f32[3,8]{1,0:T(4,128)S(1)}, f32[3,8]{1,0:T(4,128)S(1)}, u32[]{:S(2)}, u32[]{:S(2)}) collective-permute-start(f32[3,8]{1,0:T(4,128)S(1)} %fusion.10), channel_id=1, source_target_pairs={{0,1},{1,2},{2,3},{3,0},{4,5},{5,6},{6,7},{7,4},{8,9},{9,10},{10,1... | collective-permute-start | bytes 296 | tf_op jit(solution)/shard_map/ppermute | solution.py:299
  26.7 5.5 %collective-permute-start.1 = (f32[3,8]{1,0:T(4,128)S(1)}, f32[3,8]{1,0:T(4,128)S(1)}, u32[]{:S(2)}, u32[]{:S(2)}) collective-permute-start(f32[3,8]{1,0:T(4,128)S(1)} %fusion.10), channel_id=1, source_target_pairs={{0,2},{1,3},{2,0},{3,1},{4,6},{5,7},{6,4},{7,5},{8,10},{9,11},{10,... | collective-permute-start | bytes 296 | tf_op jit(solution)/shard_map/ppermute | solution.py:299
  74.5 12.9 %all-to-all-start = ((bf16[32,8,224]{2,1,0:T(8,128)(2,1)}), bf16[32,8,224]{2,1,0:T(8,128)(2,1)S(1)}, u32[]{:S(2)}, u32[]{:S(2)}) async-start(bf16[32,8,224]{2,1,0:T(8,128)(2,1)} %bitcast.10), calls=%async_computation | async-start | bytes 262144 | tf_op jit(solution)/shard_map/all_to_all | solution.py:326
  87.5 37.8 %collective-permute-start.3 = (bf16[8,8,224]{2,1,0:T(8,128)(2,1)S(1)}, bf16[8,8,224]{2,1,0:T(8,128)(2,1)S(1)}, u32[]{:S(2)}, u32[]{:S(2)}) collective-permute-start(bf16[8,8,224]{2,1,0:T(8,128)(2,1)S(1)} %get-tuple-element.46), channel_id=1, source_target_pairs={{0,1},{1,2},{2,3},{3,0},{4,5},{5,6},{6,7},{7,4},{8,9},{9,10},{10,1... | collective-permute-start | bytes 86024 | tf_op jit(solution)/shard_map/ppermute | solution.py:303
  88.8 36.5 %collective-permute-start.4 = (bf16[8,8,224]{2,1,0:T(8,128)(2,1)S(1)}, bf16[8,8,224]{2,1,0:T(8,128)(2,1)S(1)}, u32[]{:S(2)}, u32[]{:S(2)}) collective-permute-start(bf16[8,8,224]{2,1,0:T(8,128)(2,1)S(1)} %get-tuple-element.48), channel_id=1, source_target_pairs={{0,2},{1,3},{2,0},{3,1},{4,6},{5,7},{6,4},{7,5},{8,10},{9,11},{10,... | collective-permute-start | bytes 86024 | tf_op jit(solution)/shard_map/ppermute | solution.py:303
  91.2 34.1 %collective-permute-start.5 = (bf16[8,8,224]{2,1,0:T(8,128)(2,1)S(1)}, bf16[8,8,224]{2,1,0:T(8,128)(2,1)S(1)}, u32[]{:S(2)}, u32[]{:S(2)}) collective-permute-start(bf16[8,8,224]{2,1,0:T(8,128)(2,1)S(1)} %get-tuple-element.47), channel_id=1, source_target_pairs={{0,3},{1,0},{2,1},{3,2},{4,7},{5,4},{6,5},{7,6},{8,11},{9,8},{10,9... | collective-permute-start | bytes 86024 | tf_op jit(solution)/shard_map/ppermute | solution.py:303
  120.0 13.0 %all-to-all-start.3 = ((bf16[32,8,224]{2,1,0:T(8,128)(2,1)}), bf16[32,8,224]{2,1,0:T(8,128)(2,1)S(1)}, u32[]{:S(2)}, u32[]{:S(2)}) async-start(bf16[32,8,224]{2,1,0:T(8,128)(2,1)} %bitcast.35), calls=%async_computation.3 | async-start | bytes 262144 | tf_op jit(solution)/shard_map/all_to_all | solution.py:326
  133.0 74.3 %all-to-all-start.1 = ((bf16[128,8,896]{2,1,0:T(8,128)(2,1)}), bf16[128,8,896]{2,1,0:T(8,128)(2,1)}, u32[]{:S(2)}, u32[]{:S(2)}) async-start(bf16[128,8,896]{2,1,0:T(8,128)(2,1)} %bitcast.127), calls=%async_computation.1 | async-start | bytes 3670016 | tf_op jit(solution)/shard_map/all_to_all | solution.py:355
  142.7 86.8 %collective-permute-start.12 = (bf16[256,1792]{1,0:T(8,128)(2,1)}, bf16[256,1792]{1,0:T(8,128)(2,1)}, u32[]{:S(2)}, u32[]{:S(2)}) collective-permute-start(bf16[256,1792]{1,0:T(8,128)(2,1)} %get-tuple-element.28), channel_id=1, source_target_pairs={{0,1},{1,2},{2,3},{3,0},{4,5},{5,6},{6,7},{7,4},{8,9},{9,10},{10,1... | collective-permute-start | bytes 2752520 | tf_op jit(solution)/shard_map/ppermute | solution.py:303
  144.1 85.4 %collective-permute-start.13 = (bf16[256,1792]{1,0:T(8,128)(2,1)}, bf16[256,1792]{1,0:T(8,128)(2,1)}, u32[]{:S(2)}, u32[]{:S(2)}) collective-permute-start(bf16[256,1792]{1,0:T(8,128)(2,1)} %get-tuple-element.30), channel_id=1, source_target_pairs={{0,2},{1,3},{2,0},{3,1},{4,6},{5,7},{6,4},{7,5},{8,10},{9,11},{10,... | collective-permute-start | bytes 2752520 | tf_op jit(solution)/shard_map/ppermute | solution.py:303
  146.6 85.8 %collective-permute-start.14 = (bf16[256,1792]{1,0:T(8,128)(2,1)}, bf16[256,1792]{1,0:T(8,128)(2,1)}, u32[]{:S(2)}, u32[]{:S(2)}) collective-permute-start(bf16[256,1792]{1,0:T(8,128)(2,1)} %get-tuple-element.27), channel_id=1, source_target_pairs={{0,3},{1,0},{2,1},{3,2},{4,7},{5,4},{6,5},{7,6},{8,11},{9,8},{10,9... | collective-permute-start | bytes 2752520 | tf_op jit(solution)/shard_map/ppermute | solution.py:303
  147.7 48.8 %collective-permute-start.6 = (f32[2,896]{1,0:T(2,128)S(1)}, f32[2,896]{1,0:T(2,128)S(1)}, u32[]{:S(2)}, u32[]{:S(2)}) collective-permute-start(f32[2,896]{1,0:T(2,128)S(1)} %reshape.152), channel_id=1, source_target_pairs={{0,1},{1,2},{2,3},{3,0},{4,5},{5,6},{6,7},{7,4},{8,9},{9,10},{10,1... | collective-permute-start | bytes 21512 | tf_op jit(solution)/shard_map/ppermute | solution.py:299
  148.0 53.2 %collective-permute-start.7 = (f32[2,896]{1,0:T(2,128)S(1)}, f32[2,896]{1,0:T(2,128)S(1)}, u32[]{:S(2)}, u32[]{:S(2)}) collective-permute-start(f32[2,896]{1,0:T(2,128)S(1)} %reshape.152), channel_id=1, source_target_pairs={{0,2},{1,3},{2,0},{3,1},{4,6},{5,7},{6,4},{7,5},{8,10},{9,11},{10,... | collective-permute-start | bytes 21512 | tf_op jit(solution)/shard_map/ppermute | solution.py:299
  196.5 5.4 %collective-permute-start.8 = (f32[2,896]{1,0:T(2,128)S(1)}, f32[2,896]{1,0:T(2,128)S(1)}, u32[]{:S(2)}, u32[]{:S(2)}) collective-permute-start(f32[2,896]{1,0:T(2,128)S(1)} %reshape.152), channel_id=1, source_target_pairs={{0,3},{1,0},{2,1},{3,2},{4,7},{5,4},{6,5},{7,6},{8,11},{9,8},{10,9... | collective-permute-start | bytes 21512 | tf_op jit(solution)/shard_map/ppermute | solution.py:299
  207.3 23.7 %all-to-all-start.6 = ((bf16[32,8,224]{2,1,0:T(8,128)(2,1)}), bf16[32,8,224]{2,1,0:T(8,128)(2,1)}, u32[]{:S(2)}, u32[]{:S(2)}) async-start(bf16[32,8,224]{2,1,0:T(8,128)(2,1)} %bitcast.142), calls=%async_computation.6 | async-start | bytes 262144 | tf_op jit(solution)/shard_map/all_to_all | solution.py:326
  217.0 33.1 %collective-permute-start.18 = (bf16[8,8,224]{2,1,0:T(8,128)(2,1)}, bf16[8,8,224]{2,1,0:T(8,128)(2,1)}, u32[]{:S(2)}, u32[]{:S(2)}) collective-permute-start(bf16[8,8,224]{2,1,0:T(8,128)(2,1)} %get-tuple-element.43), channel_id=1, source_target_pairs={{0,1},{1,2},{2,3},{3,0},{4,5},{5,6},{6,7},{7,4},{8,9},{9,10},{10,1... | collective-permute-start | bytes 86024 | tf_op jit(solution)/shard_map/ppermute | solution.py:303
  225.4 7.1 %collective-permute-start.10 = (bf16[128,256]{1,0:T(8,128)(2,1)S(1)}, bf16[128,256]{1,0:T(8,128)(2,1)S(1)}, u32[]{:S(2)}, u32[]{:S(2)}) collective-permute-start(bf16[128,256]{1,0:T(8,128)(2,1)S(1)} %shard_map.146.refs_0_), channel_id=1, source_target_pairs={{0,2},{1,3},{2,0},{3,1},{4,6},{5,7},{6,4},{7,5},{8,10},{9,11},{10,... | collective-permute-start | bytes 196616 | tf_op jit(solution)/shard_map/ppermute | solution.py:299
  229.5 5.3 %collective-permute-start.11 = (bf16[128,256]{1,0:T(8,128)(2,1)S(1)}, bf16[128,256]{1,0:T(8,128)(2,1)S(1)}, u32[]{:S(2)}, u32[]{:S(2)}) collective-permute-start(bf16[128,256]{1,0:T(8,128)(2,1)S(1)} %shard_map.146.refs_0_), channel_id=1, source_target_pairs={{0,3},{1,0},{2,1},{3,2},{4,7},{5,4},{6,5},{7,6},{8,11},{9,8},{10,9... | collective-permute-start | bytes 196616 | tf_op jit(solution)/shard_map/ppermute | solution.py:299
  232.4 20.1 %collective-permute-start.19 = (bf16[8,8,224]{2,1,0:T(8,128)(2,1)}, bf16[8,8,224]{2,1,0:T(8,128)(2,1)}, u32[]{:S(2)}, u32[]{:S(2)}) collective-permute-start(bf16[8,8,224]{2,1,0:T(8,128)(2,1)} %get-tuple-element.45), channel_id=1, source_target_pairs={{0,2},{1,3},{2,0},{3,1},{4,6},{5,7},{6,4},{7,5},{8,10},{9,11},{10,... | collective-permute-start | bytes 86024 | tf_op jit(solution)/shard_map/ppermute | solution.py:303
  232.5 29.9 %collective-permute-start.20 = (bf16[8,8,224]{2,1,0:T(8,128)(2,1)}, bf16[8,8,224]{2,1,0:T(8,128)(2,1)}, u32[]{:S(2)}, u32[]{:S(2)}) collective-permute-start(bf16[8,8,224]{2,1,0:T(8,128)(2,1)} %get-tuple-element.44), channel_id=1, source_target_pairs={{0,3},{1,0},{2,1},{3,2},{4,7},{5,4},{6,5},{7,6},{8,11},{9,8},{10,9... | collective-permute-start | bytes 86024 | tf_op jit(solution)/shard_map/ppermute | solution.py:303
  234.8 29.0 %collective-permute-start.27 = (bf16[8,8,224]{2,1,0:T(8,128)(2,1)}, bf16[8,8,224]{2,1,0:T(8,128)(2,1)}, u32[]{:S(2)}, u32[]{:S(2)}) collective-permute-start(bf16[8,8,224]{2,1,0:T(8,128)(2,1)} %get-tuple-element.40), channel_id=1, source_target_pairs={{0,1},{1,2},{2,3},{3,0},{4,5},{5,6},{6,7},{7,4},{8,9},{9,10},{10,1... | collective-permute-start | bytes 86024 | tf_op jit(solution)/shard_map/ppermute | solution.py:303
  234.8 31.0 %collective-permute-start.28 = (bf16[8,8,224]{2,1,0:T(8,128)(2,1)}, bf16[8,8,224]{2,1,0:T(8,128)(2,1)}, u32[]{:S(2)}, u32[]{:S(2)}) collective-permute-start(bf16[8,8,224]{2,1,0:T(8,128)(2,1)} %get-tuple-element.42), channel_id=1, source_target_pairs={{0,2},{1,3},{2,0},{3,1},{4,6},{5,7},{6,4},{7,5},{8,10},{9,11},{10,... | collective-permute-start | bytes 86024 | tf_op jit(solution)/shard_map/ppermute | solution.py:303
  240.4 27.0 %all-to-all-start.2 = ((bf16[32,8,896]{2,1,0:T(8,128)(2,1)}), bf16[32,8,896]{2,1,0:T(8,128)(2,1)}, u32[]{:S(2)}, u32[]{:S(2)}) async-start(bf16[32,8,896]{2,1,0:T(8,128)(2,1)} %bitcast.125), calls=%async_computation.2 | async-start | bytes 917504 | tf_op jit(solution)/shard_map/all_to_all | solution.py:360
  250.1 15.7 %collective-permute-start.29 = (bf16[8,8,224]{2,1,0:T(8,128)(2,1)}, bf16[8,8,224]{2,1,0:T(8,128)(2,1)S(1)}, u32[]{:S(2)}, u32[]{:S(2)}) collective-permute-start(bf16[8,8,224]{2,1,0:T(8,128)(2,1)} %get-tuple-element.41), channel_id=1, source_target_pairs={{0,3},{1,0},{2,1},{3,2},{4,7},{5,4},{6,5},{7,6},{8,11},{9,8},{10,9... | collective-permute-start | bytes 86024 | tf_op jit(solution)/shard_map/ppermute | solution.py:303
  252.5 14.9 %collective-permute-start.15 = (f32[8,128]{1,0:T(8,128)}, f32[8,128]{1,0:T(8,128)S(1)}, u32[]{:S(2)}, u32[]{:S(2)}) collective-permute-start(f32[8,128]{1,0:T(8,128)} %copy-done.14), channel_id=1, source_target_pairs={{0,1},{1,2},{2,3},{3,0},{4,5},{5,6},{6,7},{7,4},{8,9},{9,10},{10,1... | collective-permute-start | bytes 12296 | tf_op jit(solution)/shard_map/ppermute | solution.py:299
  317.2 5.6 %collective-permute-start.22 = (bf16[128,256]{1,0:T(8,128)(2,1)S(1)}, bf16[128,256]{1,0:T(8,128)(2,1)S(1)}, u32[]{:S(2)}, u32[]{:S(2)}) collective-permute-start(bf16[128,256]{1,0:T(8,128)(2,1)S(1)} %shard_map.149.refs_0_), channel_id=1, source_target_pairs={{0,2},{1,3},{2,0},{3,1},{4,6},{5,7},{6,4},{7,5},{8,10},{9,11},{10,... | collective-permute-start | bytes 196616 | tf_op jit(solution)/shard_map/ppermute | solution.py:299
  326.7 16.7 %all-to-all-start.5 = ((bf16[32,8,896]{2,1,0:T(8,128)(2,1)}), bf16[32,8,896]{2,1,0:T(8,128)(2,1)}, u32[]{:S(2)}, u32[]{:S(2)}) async-start(bf16[32,8,896]{2,1,0:T(8,128)(2,1)} %bitcast.126), calls=%async_computation.5 | async-start | bytes 917504 | tf_op jit(solution)/shard_map/all_to_all | solution.py:360
  384.4 5.6 %collective-permute-start.31 = (bf16[128,256]{1,0:T(8,128)(2,1)S(1)}, bf16[128,256]{1,0:T(8,128)(2,1)S(1)}, u32[]{:S(2)}, u32[]{:S(2)}) collective-permute-start(bf16[128,256]{1,0:T(8,128)(2,1)S(1)} %shard_map.152.refs_0_), channel_id=1, source_target_pairs={{0,2},{1,3},{2,0},{3,1},{4,6},{5,7},{6,4},{7,5},{8,10},{9,11},{10,... | collective-permute-start | bytes 196616 | tf_op jit(solution)/shard_map/ppermute | solution.py:299
  393.9 16.0 %all-to-all-start.8 = ((bf16[32,8,896]{2,1,0:T(8,128)(2,1)}), bf16[32,8,896]{2,1,0:T(8,128)(2,1)S(1)}, u32[]{:S(2)}, u32[]{:S(2)}) async-start(bf16[32,8,896]{2,1,0:T(8,128)(2,1)} %bitcast.62), calls=%async_computation.8 | async-start | bytes 917504 | tf_op jit(solution)/shard_map/all_to_all | solution.py:360
  (40 other events, 620.6 us)
Sparse Core Ops, SparseCore 0:
  23.8 47.5 all-gather.3
  73.6 43.2 all-gather.5
  119.2 54.2 all-gather.7

commit v2 on v1

--- a/solution.py
+++ b/solution.py
@@ -87,47 +87,58 @@
     return (state.astype(F32) + moe_out).astype(BF16)
 
 
-def owner_kernel(first, last, experts, width, copies, *refs):
+def owner_kernel(depth, depths, experts, width, copies, *refs):
+    first, last = depth == 0, depth == depths
     refs = list(refs)
-    if not first:
+    ids_ref = refs.pop(0)
+    if first:
+        root = refs.pop(0)[...]
+        base = refs.pop(0)[...]
+        attn = refs.pop(0)[...].astype(F32)
+        for _ in range(3):
+            attn = attn + refs.pop(0)[...].astype(F32)
+        base = base + attn.astype(BF16).astype(F32).reshape(base.shape)
+    else:
         rec = refs.pop(0)[...]
         state_ref = refs.pop(0)
         stats = refs.pop(0)[...]
         for _ in range(3):
             stats = stats + refs.pop(0)[...]
-        ids = refs.pop(0)[...]
-        if not last:
-            parents = refs.pop(0)[...]
-    if first:
-        root = refs.pop(0)[...]
     if not last:
-        normed = refs.pop(0)[...]
-        attn = refs.pop(0)[...]
-        next_ids = refs.pop(0)[...]
-        router = refs.pop(0)
+        router = refs.pop(0)[...]
+        gain = refs.pop(0)[...]
+    if not first and not last:
+        parents = refs.pop(0)[depth - 1]
+        base_ref = refs.pop(0)
     if not first:
         drafted_ref = refs.pop(0)
-        drafted = combine(rec, state_ref[...], stats, ids, experts, width)
+        drafted = combine(rec, state_ref[...], stats, ids_ref[depth - 1], experts, width)
         drafted_ref[...] = drafted
     if last:
         return
-    out_state, out_stats, outgoing = refs
+    out_state, out_stats, outgoing = refs[:3]
     if first:
+        refs[3][...] = base[1:]
+        start = base[0]
         previous = root.astype(F32)
     else:
+        start = base_ref[depth - 1]
         wide = drafted.astype(F32)
         previous = jnp.zeros_like(wide)
         for node in range(wide.shape[0]):
             previous = previous + jnp.where(parents == node, wide[node : node + 1, :], 0.0)
-    state = (normed + previous + attn.astype(BF16).astype(F32)).astype(BF16)
+    state = (start + previous).astype(BF16)
     out_state[...] = state
     wide = state.astype(F32)
     square = jnp.sum(wide * wide, axis=1, keepdims=True)
-    parts = jnp.dot(state, router[...], preferred_element_type=F32)
-    logits = parts[:, :experts] + parts[:, experts : 2 * experts] + parts[:, 2 * experts : 3 * experts]
+    product = split3(router.astype(F32) * gain)
+    contract = (((1,), (1,)), ((), ()))
+    logits = lax.dot_general(state, product[0], contract, preferred_element_type=F32)
+    for piece in product[1:]:
+        logits = logits + lax.dot_general(state, piece, contract, preferred_element_type=F32)
     pad = jnp.zeros((wide.shape[0], 128 - experts - 1), F32)
     out_stats[...] = jnp.concatenate([logits, square, pad], axis=1)
-    _, _, placed, half = routing(next_ids, experts)
+    _, _, placed, half = routing(ids_ref[depth], experts)
     table = jnp.concatenate(
         [(placed & (half == h)).astype(F32) for h in range(HALVES)], axis=0
     ).astype(BF16)
@@ -141,18 +152,20 @@
         outgoing[:, copy] = sent
 
 
-def owner_call(first, last, experts, width, copies, args, nodes, quarter):
+def owner_call(depth, depths, experts, width, copies, args, nodes, quarter):
     outs = []
-    if not first:
+    if depth > 0:
         outs.append(jax.ShapeDtypeStruct((nodes, quarter), BF16))
-    if not last:
+    if depth < depths:
         outs.append(jax.ShapeDtypeStruct((nodes, quarter), BF16))
         outs.append(jax.ShapeDtypeStruct((nodes, 128), F32))
         outs.append(
             jax.ShapeDtypeStruct((experts, copies, HALVES * SLOTS, quarter // HALVES), BF16)
         )
+    if depth == 0:
+        outs.append(jax.ShapeDtypeStruct((depths - 1, nodes, quarter), F32))
     return pl.pallas_call(
-        functools.partial(owner_kernel, first, last, experts, width, copies),
+        functools.partial(owner_kernel, depth, depths, experts, width, copies),
         out_shape=outs,
         compiler_params=pltpu.CompilerParams(vmem_limit_bytes=VMEM_BYTES),
     )(*args)
@@ -246,6 +259,57 @@
         out_shape=jax.ShapeDtypeStruct((rows * HALVES, quarter // HALVES), BF16),
         compiler_params=pltpu.CompilerParams(vmem_limit_bytes=VMEM_BYTES),
     )(*acts, *weights)
+
+
+def project_kernel(rows_ref, weight_ref, out_ref):
+    columns = lax.dot_general(
+        rows_ref[...], weight_ref[...], (((1,), (1,)), ((), ())), preferred_element_type=F32
+    )
+    out_ref[...] = columns.reshape(out_ref.shape).astype(BF16)
+
+
+def project(rows, weight, owners):
+    steps = 4
+    group = rows.shape[0] // owners
+    return pl.pallas_call(
+        project_kernel,
+        grid=(steps,),
+        in_specs=[
+            pl.BlockSpec((rows.shape[0] // steps, rows.shape[1]), lambda i: (i, 0)),
+            pl.BlockSpec(weight.shape, lambda i: (0, 0)),
+        ],
+        out_specs=pl.BlockSpec((owners // steps, group, weight.shape[0]), lambda i: (i, 0, 0)),
+        out_shape=jax.ShapeDtypeStruct((owners, group, weight.shape[0]), BF16),
+        compiler_params=pltpu.CompilerParams(vmem_limit_bytes=VMEM_BYTES),
+    )(rows, weight)
+
+
+def settle_kernel(place_ref, x_ref, *refs):
+    outs, wide = refs[:-1], refs[-1]
+    quarters = len(outs)
+    blocks, _, columns = x_ref.shape
+    value = x_ref[...].astype(F32)
+    per = blocks // quarters
+    for block in range(blocks):
+        at = (block % per) * columns
+        wide[block // per, :, at : at + columns] = value[block]
+    for k in range(quarters):
+        outs[k][...] = wide[lax.rem(place_ref[0] + k, quarters)].astype(BF16)
+
+
+def settle(place, x, quarters):
+    blocks, rows, columns = x.shape
+    width = blocks // quarters * columns
+    return pl.pallas_call(
+        settle_kernel,
+        in_specs=[
+            pl.BlockSpec(memory_space=pltpu.SMEM),
+            pl.BlockSpec(memory_space=pltpu.VMEM),
+        ],
+        out_shape=[jax.ShapeDtypeStruct((rows, width), BF16) for _ in range(quarters)],
+        scratch_shapes=[pltpu.VMEM((quarters, rows, width), F32)],
+        compiler_params=pltpu.CompilerParams(vmem_limit_bytes=VMEM_BYTES),
+    )(place, x)
 
 
 def attend_request(query_block, cache_block, length, value_up, score_scale):
@@ -298,57 +362,59 @@
     def share(value):
         return [value] + [lax.ppermute(value, "tp", shifts[k]) for k in range(1, tp)]
 
-    def deal(pick):
-        return [pick(mine)] + [
-            lax.ppermute(pick((mine + k) % tp), "tp", shifts[k]) for k in range(1, tp)
+    def deal(values):
+        return [values[0]] + [lax.ppermute(values[k], "tp", shifts[k]) for k in range(1, tp)]
+
+    heads = attend_request(queries[:, 0], cache[0], cache_len[0], value_up, score_scale)
+    heads = heads.reshape(depths * nodes, -1)
+    gathered = lax.all_gather(heads, "dp", axis=0, tiled=True)
+
+    w_down, node_embed, heads = lax.optimization_barrier((w_down, node_embed, heads))
+    down = deal(
+        [
+            lax.dynamic_slice(
+                w_down[0], (0, (mine + k) % tp * quarter), (w_down.shape[1], quarter)
+            )
+            for k in range(tp)
         ]
-
-    down = deal(lambda i: lax.dynamic_slice(w_down[0], (0, i * quarter), (w_down.shape[1], quarter)))
+    )
     embed = node_embed[:, 0].astype(F32)
-    embed_sq = sum(share(jnp.sum(embed * embed, axis=-1)))
+    squares = jnp.sum(embed * embed, axis=-1).reshape(1, depths * nodes)
+    gain_rows = quarter // 128
+    notes = jnp.concatenate(
+        [
+            moe_gain.reshape(gain_rows, 128),
+            jnp.pad(squares, ((0, 1), (0, 128 - depths * nodes))),
+        ]
+    )
+    notes = jnp.stack(share(notes))
+    embed_sq = jnp.sum(notes[:, gain_rows, : depths * nodes], axis=0).reshape(depths, nodes)
     normed = embed * (1.0 / jnp.sqrt(embed_sq / width + EPS))[..., None] * embed_gain
-    gains = jnp.stack(share(moe_gain.reshape(HALVES, part)))
-    gains = gains[(mine - jnp.arange(tp, dtype=jnp.int32)) % tp]
-    product = router.astype(F32) * moe_gain[:, None]
-    high = lax.reduce_precision(product, 8, 7)
-    middle = lax.reduce_precision(product - high, 8, 7)
-    low = product - high - middle
-    routed = jnp.concatenate(
-        [high, middle, low, jnp.zeros((quarter, 128 - 3 * experts), F32)], axis=1
-    ).astype(BF16)
-
-    heads_all = attend_request(queries[:, 0], cache[0], cache_len[0], value_up, score_scale)
-
-    def attention_out(depth):
-        rows = lax.all_gather(heads_all[depth], "dp", axis=0, tiled=True)
-        columns = jnp.dot(rows, out_proj, preferred_element_type=F32).astype(BF16)
-        columns = columns.reshape(groups, nodes, -1)
-        columns = lax.all_to_all(columns, "dp", split_axis=0, concat_axis=0, tiled=True)
-        columns = columns.reshape(tp, groups // tp, nodes, columns.shape[2])
-        pieces = deal(lambda i: lax.dynamic_index_in_dim(columns, i, 0, keepdims=False))
-        summed = sum(piece.astype(F32) for piece in pieces)
-        return jnp.moveaxis(summed, 0, 1).reshape(nodes, quarter)
-
-    attn = [attention_out(depth) for depth in range(depths)]
+    gains = notes[(mine - jnp.arange(tp, dtype=jnp.int32)) % tp, :gain_rows].reshape(tp, HALVES, part)
+    gathered, normed, gains, *down = lax.optimization_barrier((gathered, normed, gains, *down))
+
+    columns = project(gathered, out_proj.T, groups)
+    columns = lax.all_to_all(columns, "dp", split_axis=0, concat_axis=0, tiled=True)
+    attn = deal(settle(mine.reshape(1).astype(jnp.int32), columns, tp))
 
     drafted = []
     carried = None
+    ids = expert_ids[:, 0]
+    parent_columns = parents[:, 0, :, None]
     for depth in range(depths + 1):
-        first, last = depth == 0, depth == depths
-        args = []
-        if not first:
-            args += list(carried) + [expert_ids[depth - 1, 0]]
-            if not last:
-                args += [parents[depth - 1, 0][:, None]]
-        if first:
-            args += [root_hidden]
-        if not last:
-            args += [normed[depth], attn[depth], expert_ids[depth, 0], routed]
-        result = list(owner_call(first, last, experts, width, tp, args, nodes, quarter))
-        if not first:
+        args = [ids]
+        args += [root_hidden, normed, *attn] if depth == 0 else carried
+        if depth < depths:
+            args += [router.T, moe_gain[None]]
+        if 0 < depth < depths:
+            args += [parent_columns, base]
+        result = list(owner_call(depth, depths, experts, width, tp, args, nodes, quarter))
+        if depth > 0:
             drafted.append(result.pop(0))
-        if last:
+        if depth == depths:
             break
+        if depth == 0:
+            base = result.pop()
         state, stats, outgoing = result
         all_stats = share(stats)
         outgoing = outgoing.reshape(experts * tp, HALVES * SLOTS, part)

time: 423 us -> 327 us (0.77)
  waiting for transfers between devices: 146 us -> 73.2 us
  starting transfers between devices: 105 us -> 47.4 us
  blocking collectives: 71.6 us -> 118 us
  matrix products: 20 us -> 12 us
    all_gather x3 -> x1, waiting for transfers between devices: 63.4 us -> 1.43 us  [local(): gathered = lax.all_gather(heads, 'dp', axis=0, tiled=True)]
    ppermute x24 -> x21, waiting for transfers between devices: 59.2 us -> 16.8 us  [share(): lax.ppermute(value, 'tp', shifts[k])]
    ppermute x12 -> x6, waiting for transfers between devices: 0.03 us -> 42 us  [deal(): lax.ppermute(values[k], 'tp', shifts[k])]
    all_to_all x2 -> x3, blocking collectives: 71.6 us -> 100 us  [local(): lax.all_to_all(outgoing, ('dp', 'tp'), split_axis=0, concat_axis=0, tiled...]
    all_to_all x4 -> x0, starting transfers between devices: 25.6 us -> none  [the longest x3 19.6 us: attention_out(): lax.all_to_all(columns, 'dp', split_axis=0, concat_axis=0, tiled=True)]
    ppermute x24 -> x21, starting transfers between devices: 43.3 us -> 24.1 us  [share(): lax.ppermute(value, 'tp', shifts[k])]
    all_to_all x0 -> x1, blocking collectives: none -> 18.2 us  [local(): lax.all_to_all(columns, 'dp', split_axis=0, concat_axis=0, tiled=True)]
    all_to_all x4 -> x0, waiting for transfers between devices: 13.3 us -> none  [the longest x3 13.3 us: attention_out(): lax.all_to_all(columns, 'dp', split_axis=0, concat_axis=0, tiled=True)]
  transfers between devices with their start and end apart: 46 -> 31, of which waited for: 18 -> 26; matrix products, arithmetic and copies ran while one was open for 6% -> 2% of each run, Pallas kernels for 2% -> 0%
where the time goes in v2:
time: 327 us; the launch traced here: 325 us
  blocking collectives  118 us (36%)
  waiting for transfers between devices  73.2 us (22%)
  starting transfers between devices  47.4 us (14%)
  Pallas kernels  35.1 us (11%)
  local copies, waits for them, and re-layouts  19.9 us (6%)
  between operations  14.5 us (4%)
  matrix products  12 us (4%)
  other arithmetic  4.91 us (2%)
    all_to_all x3, blocking collectives, local(): lax.all_to_all(outgoing, ('dp', 'tp'), split_axis=0, concat_axis=0, tiled...  100 us
    ppermute x6, waiting for transfers between devices, deal(): lax.ppermute(values[k], 'tp', shifts[k])  42 us
    ppermute x21, starting transfers between devices, share(): lax.ppermute(value, 'tp', shifts[k])  24.1 us
    all_to_all x1, blocking collectives, local(): lax.all_to_all(columns, 'dp', split_axis=0, concat_axis=0, tiled=True)  18.2 us
    ppermute x21, waiting for transfers between devices, share(): lax.ppermute(value, 'tp', shifts[k])  16.8 us
    pallas_call x3, Pallas kernels, expert_call(): pl.pallas_call(functools.partial(expert_kernel, width), grid=(quarters,),...  16 us
    all_to_all x3, starting transfers between devices, local(): lax.all_to_all(answer, 'dp', split_axis=0, concat_axis=0, tiled=True)  14.7 us
    unnamed x72, local copies, waits for them, and re-layouts  13.4 us
  transfers between devices with their start and end apart: 31, of which 26 were waited for; matrix products, arithmetic and copies ran while one was open for 2% of the time, Pallas kernels for 0%

profile of v2, /device:TPU:1, one launch (start us, length us, event | category | flops | bytes accessed | tf_op | source)
XLA Modules:
  0.0 325.5 jit_solution(13823461320158750260)
XLA Ops:
  7.8 7.2 %fusion = (f32[768]{0:T(1024)S(1)}, f32[768,4096]{1,0:T(8,128)S(1)}) fusion(pred[4096]{0:T(1024)(128)(4,1)S(1)} %iota_compare_fusion, bf16[768,576]{1,0:T(8,128)(2,1)S(1)} %bitcast.70, bf16[1,4096,576]{1,2,0:T(8,128)(2,1)} %param.20), kind=kOutput, calls=%fused_computation.4 | convolution fusion | flops 3633315072 | bytes 18193408 | tf_op jit(solution)/shard_map/qk,ck->qc/dot_general | solution.py:320
  15.0 3.2 fusion.1
  18.3 3.7 %fusion.4 = bf16[768,512]{1,0:T(8,128)(2,1)S(1)} fusion(bf16[4096,576]{0,1:T(8,128)(2,1)S(1)} %bitcast.105, f32[768,4096]{1,0:T(8,128)S(1)} %get-tuple-element.60, f32[768]{0:T(1024)S(1)} %fusion.1, f32[768]{0:T(1024)S(1)} %get-tuple-element.59, pred[4096]{0:T(1024)(128)(4,1)S(1)} %iota_compare_fusion), kind=kOutput, calls=%fused_computation.8 | convolution fusion | flops 3237347328 | bytes 17575936 | tf_op jit(solution)/shard_map/dot_general | solution.py:328
  24.0 3.6 %collective-permute-start.2 = (f32[16,128]{1,0:T(8,128)S(1)}, f32[16,128]{1,0:T(8,128)S(1)}, u32[]{:S(2)}, u32[]{:S(2)}) collective-permute-start(f32[16,128]{1,0:T(8,128)S(1)} %select_maximum_fusion), channel_id=1, source_target_pairs={{0,3},{1,0},{2,1},{3,2},{4,7},{5,4},{6,5},{7,6},{8,11},{9,8},{10,9... | collective-permute-start | bytes 24584 | tf_op jit(solution)/shard_map/ppermute | solution.py:363
  28.7 3.6 %dynamic-slice_bitcast_fusion = (bf16[256,1792]{1,0:T(8,128)(2,1)}, bf16[256,1792]{1,0:T(8,128)(2,1)}, bf16[256,1792]{1,0:T(8,128)(2,1)}, bf16[256,1792]{1,0:T(8,128)(2,1)S(1)}) fusion(bf16[1,256,7168]{2,1,0:T(8,128)(2,1)} %param.29, s32[]{:T(128)S(6)} %select_n.68, s32[]{:T(128)S(6)} %select_n.66, s32[]{:T(128)S(6)} %select_n.64, s32[]{:T(128)S(6)} %select_n.62), kind=kLoop, calls=%fused_computation.11 | loop fusion | bytes 7340048 | tf_op jit(solution)/shard_map/dynamic_slice | solution.py:375
  37.5 16.7 %collective-permute-done.3.refs_5_ = bf16[256,1792]{1,0:T(8,128)(2,1)S(1)} collective-permute-done((bf16[256,1792]{1,0:T(8,128)(2,1)}, bf16[256,1792]{1,0:T(8,128)(2,1)S(1)}, u32[]{:S(2)}, u32[]{:S(2)}) %collective-permute-start.3) | collective-permute-done | bytes 917536 | tf_op jit(solution)/shard_map/ppermute | solution.py:366
  54.2 20.3 %collective-permute-done.4.refs_6_ = bf16[256,1792]{1,0:T(8,128)(2,1)} collective-permute-done((bf16[256,1792]{1,0:T(8,128)(2,1)}, bf16[256,1792]{1,0:T(8,128)(2,1)}, u32[]{:S(2)}, u32[]{:S(2)}) %collective-permute-start.4) | collective-permute-done | bytes 917536 | tf_op jit(solution)/shard_map/ppermute | solution.py:366
  78.4 5.3 %shard_map.145 = bf16[32,24,224]{2,1,0:T(8,128)(2,1)S(1)} custom-call(bf16[768,4096]{1,0:T(8,128)(2,1)} %all-gather.2.cloned.1.call-done.rows_ref, bf16[224,4096]{1,0:T(8,128)(2,1)S(1)} %bitcast.83), custom_call_target="tpu_custom_call" | custom-call | tf_op jit(solution)/shard_map/pallas_call | solution.py:274
  83.6 18.2 %all_to_all.35.x_ref = bf16[32,24,224]{2,1,0:T(8,128)(2,1)S(1)} all-to-all(bf16[32,24,224]{2,1,0:T(8,128)(2,1)S(1)} %shard_map.145), channel_id=1, replica_groups=mesh['dp'=32,'tp'=4] {'dp'}, dimensions={0} | all-to-all | bytes 688128 | tf_op jit(solution)/shard_map/all_to_all | solution.py:397
  103.6 2.2 collective-permute-start.7
  107.7 2.7 collective-permute-done.7.refs_5_
  112.3 33.3 %all_to_all.36 = bf16[128,8,896]{2,1,0:T(8,128)(2,1)S(1)} all-to-all(bf16[128,8,896]{2,1,0:T(8,128)(2,1)S(1)} %bitcast.79), channel_id=1, replica_groups=mesh['dp'=32,'tp'=4] {'dp','tp'}, dimensions={0} | all-to-all | bytes 3670016 | tf_op jit(solution)/shard_map/all_to_all | solution.py:421
  145.6 5.3 %shard_map.148.refs_0_ = bf16[128,256]{1,0:T(8,128)(2,1)S(1)} custom-call(bf16[32,4,8,896]{3,2,1,0:T(8,128)(2,1)S(1)} %bitcast.75, f32[4,2,896]{2,1,0:T(2,128)S(1)} %reshape.129.gain_ref, bf16[7168,256]{1,0:T(8,128)(2,1)S(1)} %bitcast.71, bf16[7168,256]{1,0:T(8,128)(2,1)} %bitcast.94), custom_call_target="tpu_custom_call" | custom-call | tf_op jit(solution)/shard_map/pallas_call | solution.py:221
  153.9 2.0 collective-permute-done.9.refs_1_
  157.3 3.3 shard_map.149
  160.6 4.9 %all-to-all-start.2 = ((bf16[32,8,896]{2,1,0:T(8,128)(2,1)}), bf16[32,8,896]{2,1,0:T(8,128)(2,1)S(1)}, u32[]{:S(2)}, u32[]{:S(2)}) async-start(bf16[32,8,896]{2,1,0:T(8,128)(2,1)} %bitcast.29), calls=%async_computation.2 | async-start | bytes 917504 | tf_op jit(solution)/shard_map/all_to_all | solution.py:426
  166.2 2.8 collective-permute-start.13
  172.0 4.6 %all-to-all-done.2 = bf16[32,8,896]{2,1,0:T(8,128)(2,1)S(1)} async-done(((bf16[32,8,896]{2,1,0:T(8,128)(2,1)}), bf16[32,8,896]{2,1,0:T(8,128)(2,1)S(1)}, u32[]{:S(2)}, u32[]{:S(2)}) %all-to-all-start.2) | async-done | bytes 458784 | tf_op jit(solution)/shard_map/all_to_all | solution.py:426
  180.8 32.9 %all_to_all.37 = bf16[128,8,896]{2,1,0:T(8,128)(2,1)S(1)} all-to-all(bf16[128,8,896]{2,1,0:T(8,128)(2,1)S(1)} %bitcast.78), channel_id=1, replica_groups=mesh['dp'=32,'tp'=4] {'dp','tp'}, dimensions={0} | all-to-all | bytes 3670016 | tf_op jit(solution)/shard_map/all_to_all | solution.py:421
  213.7 5.3 %shard_map.151.refs_0_ = bf16[128,256]{1,0:T(8,128)(2,1)S(1)} custom-call(bf16[32,4,8,896]{3,2,1,0:T(8,128)(2,1)S(1)} %bitcast.76, f32[4,2,896]{2,1,0:T(2,128)S(1)} %reshape.129.gain_ref, bf16[7168,256]{1,0:T(8,128)(2,1)S(1)} %bitcast.72, bf16[7168,256]{1,0:T(8,128)(2,1)} %bitcast.95), custom_call_target="tpu_custom_call" | custom-call | tf_op jit(solution)/shard_map/pallas_call | solution.py:221
  222.0 2.0 collective-permute-done.15.refs_1_
  225.5 3.2 shard_map.152
  228.7 4.9 %all-to-all-start.4 = ((bf16[32,8,896]{2,1,0:T(8,128)(2,1)}), bf16[32,8,896]{2,1,0:T(8,128)(2,1)S(1)}, u32[]{:S(2)}, u32[]{:S(2)}) async-start(bf16[32,8,896]{2,1,0:T(8,128)(2,1)} %bitcast.35), calls=%async_computation.4 | async-start | bytes 917504 | tf_op jit(solution)/shard_map/all_to_all | solution.py:426
  234.5 2.8 collective-permute-start.19
  240.9 3.8 %all-to-all-done.4 = bf16[32,8,896]{2,1,0:T(8,128)(2,1)S(1)} async-done(((bf16[32,8,896]{2,1,0:T(8,128)(2,1)}), bf16[32,8,896]{2,1,0:T(8,128)(2,1)S(1)}, u32[]{:S(2)}, u32[]{:S(2)}) %all-to-all-start.4) | async-done | bytes 458784 | tf_op jit(solution)/shard_map/all_to_all | solution.py:426
  250.2 34.1 %all_to_all.38 = bf16[128,8,896]{2,1,0:T(8,128)(2,1)S(1)} all-to-all(bf16[128,8,896]{2,1,0:T(8,128)(2,1)S(1)} %bitcast.77), channel_id=1, replica_groups=mesh['dp'=32,'tp'=4] {'dp','tp'}, dimensions={0} | all-to-all | bytes 3670016 | tf_op jit(solution)/shard_map/all_to_all | solution.py:421
  284.3 5.3 %shard_map.154.refs_0_ = bf16[128,256]{1,0:T(8,128)(2,1)S(1)} custom-call(bf16[32,4,8,896]{3,2,1,0:T(8,128)(2,1)S(1)} %bitcast.74, f32[4,2,896]{2,1,0:T(2,128)S(1)} %reshape.129.gain_ref, bf16[7168,256]{1,0:T(8,128)(2,1)S(1)} %bitcast.73, bf16[7168,256]{1,0:T(8,128)(2,1)} %bitcast.96), custom_call_target="tpu_custom_call" | custom-call | tf_op jit(solution)/shard_map/pallas_call | solution.py:221
  292.6 2.0 collective-permute-done.21.refs_1_
  296.1 3.2 shard_map.155
  299.3 4.9 %all-to-all-start.6 = ((bf16[32,8,896]{2,1,0:T(8,128)(2,1)}), bf16[32,8,896]{2,1,0:T(8,128)(2,1)S(1)}, u32[]{:S(2)}, u32[]{:S(2)}) async-start(bf16[32,8,896]{2,1,0:T(8,128)(2,1)} %bitcast.40), calls=%async_computation.6 | async-start | bytes 917504 | tf_op jit(solution)/shard_map/all_to_all | solution.py:426
  304.9 2.8 collective-permute-start.25
  310.7 4.6 %all-to-all-done.6 = bf16[32,8,896]{2,1,0:T(8,128)(2,1)S(1)} async-done(((bf16[32,8,896]{2,1,0:T(8,128)(2,1)}), bf16[32,8,896]{2,1,0:T(8,128)(2,1)S(1)}, u32[]{:S(2)}, u32[]{:S(2)}) %all-to-all-start.6) | async-done | bytes 458784 | tf_op jit(solution)/shard_map/all_to_all | solution.py:426
  (141 shorter events, 56.2 us)
Async XLA Ops:
  6.5 70.3 %all-gather.2.cloned.1.call-start = ((), (), s32[]{:S(2)}) async-start(), calls=%async_computation.7 | async-start | bytes 6488064 | tf_op jit(solution)/shard_map/all_gather | solution.py:370
  24.0 11.5 %collective-permute-start.2 = (f32[16,128]{1,0:T(8,128)S(1)}, f32[16,128]{1,0:T(8,128)S(1)}, u32[]{:S(2)}, u32[]{:S(2)}) collective-permute-start(f32[16,128]{1,0:T(8,128)S(1)} %select_maximum_fusion), channel_id=1, source_target_pairs={{0,3},{1,0},{2,1},{3,2},{4,7},{5,4},{6,5},{7,6},{8,11},{9,8},{10,9... | collective-permute-start | bytes 24584 | tf_op jit(solution)/shard_map/ppermute | solution.py:363
  27.7 8.9 %collective-permute-start.1 = (f32[16,128]{1,0:T(8,128)S(1)}, f32[16,128]{1,0:T(8,128)S(1)}, u32[]{:S(2)}, u32[]{:S(2)}) collective-permute-start(f32[16,128]{1,0:T(8,128)S(1)} %select_maximum_fusion), channel_id=1, source_target_pairs={{0,2},{1,3},{2,0},{3,1},{4,6},{5,7},{6,4},{7,5},{8,10},{9,11},{10,... | collective-permute-start | bytes 24584 | tf_op jit(solution)/shard_map/ppermute | solution.py:363
  28.0 8.5 %collective-permute-start = (f32[16,128]{1,0:T(8,128)S(1)}, f32[16,128]{1,0:T(8,128)S(1)}, u32[]{:S(2)}, u32[]{:S(2)}) collective-permute-start(f32[16,128]{1,0:T(8,128)S(1)} %select_maximum_fusion), channel_id=1, source_target_pairs={{0,1},{1,2},{2,3},{3,0},{4,5},{5,6},{6,7},{7,4},{8,9},{9,10},{10,1... | collective-permute-start | bytes 24584 | tf_op jit(solution)/shard_map/ppermute | solution.py:363
  32.3 78.1 %copy-start.18 = (bf16[1,1792]{1,0:T(2,128)(2,1)S(1)}, bf16[1,1792]{1,0:T(2,128)(2,1)}, u32[]{:S(2)}) copy-start(bf16[1,1792]{1,0:T(2,128)(2,1)} %refs_1_.1) | copy-start | bytes 10756
  32.3 21.8 %collective-permute-start.3 = (bf16[256,1792]{1,0:T(8,128)(2,1)}, bf16[256,1792]{1,0:T(8,128)(2,1)S(1)}, u32[]{:S(2)}, u32[]{:S(2)}) collective-permute-start(bf16[256,1792]{1,0:T(8,128)(2,1)} %get-tuple-element.57), channel_id=1, source_target_pairs={{0,1},{1,2},{2,3},{3,0},{4,5},{5,6},{6,7},{7,4},{8,9},{9,10},{10,1... | collective-permute-start | bytes 2752520 | tf_op jit(solution)/shard_map/ppermute | solution.py:366
  34.0 40.4 %collective-permute-start.4 = (bf16[256,1792]{1,0:T(8,128)(2,1)}, bf16[256,1792]{1,0:T(8,128)(2,1)}, u32[]{:S(2)}, u32[]{:S(2)}) collective-permute-start(bf16[256,1792]{1,0:T(8,128)(2,1)} %get-tuple-element.56), channel_id=1, source_target_pairs={{0,2},{1,3},{2,0},{3,1},{4,6},{5,7},{6,4},{7,5},{8,10},{9,11},{10,... | collective-permute-start | bytes 2752520 | tf_op jit(solution)/shard_map/ppermute | solution.py:366
  35.6 39.8 %collective-permute-start.5 = (bf16[256,1792]{1,0:T(8,128)(2,1)}, bf16[256,1792]{1,0:T(8,128)(2,1)}, u32[]{:S(2)}, u32[]{:S(2)}) collective-permute-start(bf16[256,1792]{1,0:T(8,128)(2,1)} %get-tuple-element.55), channel_id=1, source_target_pairs={{0,3},{1,0},{2,1},{3,2},{4,7},{5,4},{6,5},{7,6},{8,11},{9,8},{10,9... | collective-permute-start | bytes 2752520 | tf_op jit(solution)/shard_map/ppermute | solution.py:366
  102.0 5.7 %collective-permute-start.6 = (bf16[24,1792]{1,0:T(8,128)(2,1)S(1)}, bf16[24,1792]{1,0:T(8,128)(2,1)S(1)}, u32[]{:S(2)}, u32[]{:S(2)}) collective-permute-start(bf16[24,1792]{1,0:T(8,128)(2,1)S(1)} %get-tuple-element.35), channel_id=1, source_target_pairs={{0,1},{1,2},{2,3},{3,0},{4,5},{5,6},{6,7},{7,4},{8,9},{9,10},{10,1... | collective-permute-start | bytes 258056 | tf_op jit(solution)/shard_map/ppermute | solution.py:366
  103.6 6.7 %collective-permute-start.7 = (bf16[24,1792]{1,0:T(8,128)(2,1)S(1)}, bf16[24,1792]{1,0:T(8,128)(2,1)S(1)}, u32[]{:S(2)}, u32[]{:S(2)}) collective-permute-start(bf16[24,1792]{1,0:T(8,128)(2,1)S(1)} %get-tuple-element.36), channel_id=1, source_target_pairs={{0,2},{1,3},{2,0},{3,1},{4,6},{5,7},{6,4},{7,5},{8,10},{9,11},{10,... | collective-permute-start | bytes 258056 | tf_op jit(solution)/shard_map/ppermute | solution.py:366
  105.8 4.6 %collective-permute-start.8 = (bf16[24,1792]{1,0:T(8,128)(2,1)S(1)}, bf16[24,1792]{1,0:T(8,128)(2,1)S(1)}, u32[]{:S(2)}, u32[]{:S(2)}) collective-permute-start(bf16[24,1792]{1,0:T(8,128)(2,1)S(1)} %get-tuple-element.37), channel_id=1, source_target_pairs={{0,3},{1,0},{2,1},{3,2},{4,7},{5,4},{6,5},{7,6},{8,11},{9,8},{10,9... | collective-permute-start | bytes 258056 | tf_op jit(solution)/shard_map/ppermute | solution.py:366
  150.9 4.9 %collective-permute-start.9 = (bf16[128,256]{1,0:T(8,128)(2,1)S(1)}, bf16[128,256]{1,0:T(8,128)(2,1)S(1)}, u32[]{:S(2)}, u32[]{:S(2)}) collective-permute-start(bf16[128,256]{1,0:T(8,128)(2,1)S(1)} %shard_map.148.refs_0_), channel_id=1, source_target_pairs={{0,1},{1,2},{2,3},{3,0},{4,5},{5,6},{6,7},{7,4},{8,9},{9,10},{10,1... | collective-permute-start | bytes 196616 | tf_op jit(solution)/shard_map/ppermute | solution.py:363
  151.4 5.6 %collective-permute-start.10 = (bf16[128,256]{1,0:T(8,128)(2,1)S(1)}, bf16[128,256]{1,0:T(8,128)(2,1)S(1)}, u32[]{:S(2)}, u32[]{:S(2)}) collective-permute-start(bf16[128,256]{1,0:T(8,128)(2,1)S(1)} %shard_map.148.refs_0_), channel_id=1, source_target_pairs={{0,2},{1,3},{2,0},{3,1},{4,6},{5,7},{6,4},{7,5},{8,10},{9,11},{10,... | collective-permute-start | bytes 196616 | tf_op jit(solution)/shard_map/ppermute | solution.py:363
  152.3 5.1 %collective-permute-start.11 = (bf16[128,256]{1,0:T(8,128)(2,1)S(1)}, bf16[128,256]{1,0:T(8,128)(2,1)S(1)}, u32[]{:S(2)}, u32[]{:S(2)}) collective-permute-start(bf16[128,256]{1,0:T(8,128)(2,1)S(1)} %shard_map.148.refs_0_), channel_id=1, source_target_pairs={{0,3},{1,0},{2,1},{3,2},{4,7},{5,4},{6,5},{7,6},{8,11},{9,8},{10,9... | collective-permute-start | bytes 196616 | tf_op jit(solution)/shard_map/ppermute | solution.py:363
  160.6 16.0 %all-to-all-start.2 = ((bf16[32,8,896]{2,1,0:T(8,128)(2,1)}), bf16[32,8,896]{2,1,0:T(8,128)(2,1)S(1)}, u32[]{:S(2)}, u32[]{:S(2)}) async-start(bf16[32,8,896]{2,1,0:T(8,128)(2,1)} %bitcast.29), calls=%async_computation.2 | async-start | bytes 917504 | tf_op jit(solution)/shard_map/all_to_all | solution.py:426
  165.5 4.9 %collective-permute-start.12 = (f32[8,128]{1,0:T(8,128)}, f32[8,128]{1,0:T(8,128)}, u32[]{:S(2)}, u32[]{:S(2)}) collective-permute-start(f32[8,128]{1,0:T(8,128)} %copy-done.23), channel_id=1, source_target_pairs={{0,1},{1,2},{2,3},{3,0},{4,5},{5,6},{6,7},{7,4},{8,9},{9,10},{10,1... | collective-permute-start | bytes 12296 | tf_op jit(solution)/shard_map/ppermute | solution.py:363
  166.2 4.3 %collective-permute-start.13 = (f32[8,128]{1,0:T(8,128)}, f32[8,128]{1,0:T(8,128)}, u32[]{:S(2)}, u32[]{:S(2)}) collective-permute-start(f32[8,128]{1,0:T(8,128)} %copy-done.23), channel_id=1, source_target_pairs={{0,2},{1,3},{2,0},{3,1},{4,6},{5,7},{6,4},{7,5},{8,10},{9,11},{10,... | collective-permute-start | bytes 12296 | tf_op jit(solution)/shard_map/ppermute | solution.py:363
  169.0 3.0 collective-permute-start.14
  219.1 4.9 %collective-permute-start.15 = (bf16[128,256]{1,0:T(8,128)(2,1)S(1)}, bf16[128,256]{1,0:T(8,128)(2,1)S(1)}, u32[]{:S(2)}, u32[]{:S(2)}) collective-permute-start(bf16[128,256]{1,0:T(8,128)(2,1)S(1)} %shard_map.151.refs_0_), channel_id=1, source_target_pairs={{0,1},{1,2},{2,3},{3,0},{4,5},{5,6},{6,7},{7,4},{8,9},{9,10},{10,1... | collective-permute-start | bytes 196616 | tf_op jit(solution)/shard_map/ppermute | solution.py:363
  219.5 5.6 %collective-permute-start.16 = (bf16[128,256]{1,0:T(8,128)(2,1)S(1)}, bf16[128,256]{1,0:T(8,128)(2,1)S(1)}, u32[]{:S(2)}, u32[]{:S(2)}) collective-permute-start(bf16[128,256]{1,0:T(8,128)(2,1)S(1)} %shard_map.151.refs_0_), channel_id=1, source_target_pairs={{0,2},{1,3},{2,0},{3,1},{4,6},{5,7},{6,4},{7,5},{8,10},{9,11},{10,... | collective-permute-start | bytes 196616 | tf_op jit(solution)/shard_map/ppermute | solution.py:363
  220.4 5.1 %collective-permute-start.17 = (bf16[128,256]{1,0:T(8,128)(2,1)S(1)}, bf16[128,256]{1,0:T(8,128)(2,1)S(1)}, u32[]{:S(2)}, u32[]{:S(2)}) collective-permute-start(bf16[128,256]{1,0:T(8,128)(2,1)S(1)} %shard_map.151.refs_0_), channel_id=1, source_target_pairs={{0,3},{1,0},{2,1},{3,2},{4,7},{5,4},{6,5},{7,6},{8,11},{9,8},{10,9... | collective-permute-start | bytes 196616 | tf_op jit(solution)/shard_map/ppermute | solution.py:363
  228.7 16.0 %all-to-all-start.4 = ((bf16[32,8,896]{2,1,0:T(8,128)(2,1)}), bf16[32,8,896]{2,1,0:T(8,128)(2,1)S(1)}, u32[]{:S(2)}, u32[]{:S(2)}) async-start(bf16[32,8,896]{2,1,0:T(8,128)(2,1)} %bitcast.35), calls=%async_computation.4 | async-start | bytes 917504 | tf_op jit(solution)/shard_map/all_to_all | solution.py:426
  233.6 4.5 %collective-permute-start.18 = (f32[8,128]{1,0:T(8,128)}, f32[8,128]{1,0:T(8,128)S(1)}, u32[]{:S(2)}, u32[]{:S(2)}) collective-permute-start(f32[8,128]{1,0:T(8,128)} %copy-done.21), channel_id=1, source_target_pairs={{0,1},{1,2},{2,3},{3,0},{4,5},{5,6},{6,7},{7,4},{8,9},{9,10},{10,1... | collective-permute-start | bytes 12296 | tf_op jit(solution)/shard_map/ppermute | solution.py:363
  234.5 4.5 %collective-permute-start.19 = (f32[8,128]{1,0:T(8,128)}, f32[8,128]{1,0:T(8,128)S(1)}, u32[]{:S(2)}, u32[]{:S(2)}) collective-permute-start(f32[8,128]{1,0:T(8,128)} %copy-done.21), channel_id=1, source_target_pairs={{0,2},{1,3},{2,0},{3,1},{4,6},{5,7},{6,4},{7,5},{8,10},{9,11},{10,... | collective-permute-start | bytes 12296 | tf_op jit(solution)/shard_map/ppermute | solution.py:363
  237.4 3.0 collective-permute-start.20
  289.7 4.9 %collective-permute-start.21 = (bf16[128,256]{1,0:T(8,128)(2,1)S(1)}, bf16[128,256]{1,0:T(8,128)(2,1)S(1)}, u32[]{:S(2)}, u32[]{:S(2)}) collective-permute-start(bf16[128,256]{1,0:T(8,128)(2,1)S(1)} %shard_map.154.refs_0_), channel_id=1, source_target_pairs={{0,1},{1,2},{2,3},{3,0},{4,5},{5,6},{6,7},{7,4},{8,9},{9,10},{10,1... | collective-permute-start | bytes 196616 | tf_op jit(solution)/shard_map/ppermute | solution.py:363
  290.1 5.6 %collective-permute-start.22 = (bf16[128,256]{1,0:T(8,128)(2,1)S(1)}, bf16[128,256]{1,0:T(8,128)(2,1)S(1)}, u32[]{:S(2)}, u32[]{:S(2)}) collective-permute-start(bf16[128,256]{1,0:T(8,128)(2,1)S(1)} %shard_map.154.refs_0_), channel_id=1, source_target_pairs={{0,2},{1,3},{2,0},{3,1},{4,6},{5,7},{6,4},{7,5},{8,10},{9,11},{10,... | collective-permute-start | bytes 196616 | tf_op jit(solution)/shard_map/ppermute | solution.py:363
  291.0 5.1 %collective-permute-start.23 = (bf16[128,256]{1,0:T(8,128)(2,1)S(1)}, bf16[128,256]{1,0:T(8,128)(2,1)S(1)}, u32[]{:S(2)}, u32[]{:S(2)}) collective-permute-start(bf16[128,256]{1,0:T(8,128)(2,1)S(1)} %shard_map.154.refs_0_), channel_id=1, source_target_pairs={{0,3},{1,0},{2,1},{3,2},{4,7},{5,4},{6,5},{7,6},{8,11},{9,8},{10,9... | collective-permute-start | bytes 196616 | tf_op jit(solution)/shard_map/ppermute | solution.py:363
  299.3 16.0 %all-to-all-start.6 = ((bf16[32,8,896]{2,1,0:T(8,128)(2,1)}), bf16[32,8,896]{2,1,0:T(8,128)(2,1)S(1)}, u32[]{:S(2)}, u32[]{:S(2)}) async-start(bf16[32,8,896]{2,1,0:T(8,128)(2,1)} %bitcast.40), calls=%async_computation.6 | async-start | bytes 917504 | tf_op jit(solution)/shard_map/all_to_all | solution.py:426
  304.2 4.2 %collective-permute-start.24 = (f32[8,128]{1,0:T(8,128)}, f32[8,128]{1,0:T(8,128)S(1)}, u32[]{:S(2)}, u32[]{:S(2)}) collective-permute-start(f32[8,128]{1,0:T(8,128)} %copy-done.19), channel_id=1, source_target_pairs={{0,1},{1,2},{2,3},{3,0},{4,5},{5,6},{6,7},{7,4},{8,9},{9,10},{10,1... | collective-permute-start | bytes 12296 | tf_op jit(solution)/shard_map/ppermute | solution.py:363
  304.9 4.2 %collective-permute-start.25 = (f32[8,128]{1,0:T(8,128)}, f32[8,128]{1,0:T(8,128)S(1)}, u32[]{:S(2)}, u32[]{:S(2)}) collective-permute-start(f32[8,128]{1,0:T(8,128)} %copy-done.19), channel_id=1, source_target_pairs={{0,2},{1,3},{2,0},{3,1},{4,6},{5,7},{6,4},{7,5},{8,10},{9,11},{10,... | collective-permute-start | bytes 12296 | tf_op jit(solution)/shard_map/ppermute | solution.py:363
  307.7 3.0 collective-permute-start.26
  (35 other events, 608.8 us)
Sparse Core Ops, SparseCore 0:
  24.0 52.8 all-gather.1

commit v3 on v2

--- a/solution.py
+++ b/solution.py
@@ -1,4 +1,5 @@
 import functools
+import math
 
 import jax
 import jax.numpy as jnp
@@ -90,39 +91,42 @@
 def owner_kernel(depth, depths, experts, width, copies, *refs):
     first, last = depth == 0, depth == depths
     refs = list(refs)
-    ids_ref = refs.pop(0)
+    tables = refs.pop(0)
+    top = tables.shape[2] - 1
     if first:
         root = refs.pop(0)[...]
-        base = refs.pop(0)[...]
+        start = refs.pop(0)[...]
         attn = refs.pop(0)[...].astype(F32)
         for _ in range(3):
             attn = attn + refs.pop(0)[...].astype(F32)
-        base = base + attn.astype(BF16).astype(F32).reshape(base.shape)
+        start = start + attn.astype(BF16).astype(F32).reshape(start.shape)
+        base, start = start[1:], start[0]
+        router = refs.pop(0)[...].astype(F32)
+        product = split3(router * refs.pop(0)[...])
+        blank = jnp.zeros((128 - 3 * experts, router.shape[1]), BF16)
+        routed = jnp.concatenate([*product, blank], axis=0)
     else:
         rec = refs.pop(0)[...]
         state_ref = refs.pop(0)
         stats = refs.pop(0)[...]
         for _ in range(3):
             stats = stats + refs.pop(0)[...]
-    if not last:
-        router = refs.pop(0)[...]
-        gain = refs.pop(0)[...]
     if not first and not last:
-        parents = refs.pop(0)[depth - 1]
-        base_ref = refs.pop(0)
+        routed = refs.pop(0)[...]
+        start = refs.pop(0)[depth - 1]
     if not first:
         drafted_ref = refs.pop(0)
-        drafted = combine(rec, state_ref[...], stats, ids_ref[depth - 1], experts, width)
+        drafted = combine(rec, state_ref[...], stats, tables[depth - 1][:, :top], experts, width)
         drafted_ref[...] = drafted
     if last:
         return
     out_state, out_stats, outgoing = refs[:3]
     if first:
-        refs[3][...] = base[1:]
-        start = base[0]
+        refs[3][...] = routed
+        refs[4][...] = base
         previous = root.astype(F32)
     else:
-        start = base_ref[depth - 1]
+        parents = tables[depth][:, top : top + 1]
         wide = drafted.astype(F32)
         previous = jnp.zeros_like(wide)
         for node in range(wide.shape[0]):
@@ -131,14 +135,13 @@
     out_state[...] = state
     wide = state.astype(F32)
     square = jnp.sum(wide * wide, axis=1, keepdims=True)
-    product = split3(router.astype(F32) * gain)
-    contract = (((1,), (1,)), ((), ()))
-    logits = lax.dot_general(state, product[0], contract, preferred_element_type=F32)
-    for piece in product[1:]:
-        logits = logits + lax.dot_general(state, piece, contract, preferred_element_type=F32)
+    parts = lax.dot_general(
+        state, routed, (((1,), (1,)), ((), ())), preferred_element_type=F32
+    )
+    logits = parts[:, :experts] + parts[:, experts : 2 * experts] + parts[:, 2 * experts : 3 * experts]
     pad = jnp.zeros((wide.shape[0], 128 - experts - 1), F32)
     out_stats[...] = jnp.concatenate([logits, square, pad], axis=1)
-    _, _, placed, half = routing(ids_ref[depth], experts)
+    _, _, placed, half = routing(tables[depth][:, :top], experts)
     table = jnp.concatenate(
         [(placed & (half == h)).astype(F32) for h in range(HALVES)], axis=0
     ).astype(BF16)
@@ -163,6 +166,7 @@
             jax.ShapeDtypeStruct((experts, copies, HALVES * SLOTS, quarter // HALVES), BF16)
         )
     if depth == 0:
+        outs.append(jax.ShapeDtypeStruct((128, quarter), BF16))
         outs.append(jax.ShapeDtypeStruct((depths - 1, nodes, quarter), F32))
     return pl.pallas_call(
         functools.partial(owner_kernel, depth, depths, experts, width, copies),
@@ -171,46 +175,35 @@
     )(*args)
 
 
-def expert_kernel(width, x_ref, gain_ref, gate_ref, up_ref, act_ref, pack, inv, total):
+def expert_kernel(width, x_ref, gain_ref, gate_ref, up_ref, act_ref, pack, square, total):
     step = pl.program_id(0)
-    sources, quarters, group, part = x_ref.shape
+    sources, _, group, part = x_ref.shape
     rows = sources * group
-
-    def block(index):
-        return x_ref[:, index].astype(F32).reshape(rows, part)
-
-    row_half = (iota((rows, 1), 0) // SLOTS) - (iota((rows, 1), 0) // group) * HALVES
-
-    @pl.when(step == 0)
-    def _():
-        pack[...] = pack_matrix(rows, True)
-        square = jnp.zeros((rows, part), F32)
-        for index in range(quarters):
-            value = block(index)
-            square = square + value * value
-        summed = jnp.broadcast_to(jnp.sum(square, axis=1, keepdims=True), (rows, 128))
-        other = jnp.where(
-            row_half == 0, pltpu.roll(summed, rows - SLOTS, 0), pltpu.roll(summed, SLOTS, 0)
-        )
-        inv[...] = 1.0 / jnp.sqrt((summed + other) / width + EPS)
-        total[...] = jnp.zeros_like(total)
-
-    gain = gain_ref[step]
-    scaled = block(step) * inv[:, :1]
-    scaled = (scaled * jnp.where(row_half == 0, gain[0:1, :], gain[1:2, :])).astype(BF16)
-    packed = jnp.dot(pack[...], scaled, preferred_element_type=F32).astype(BF16)
     per_half = rows // HALVES
     hidden = gate_ref.shape[1]
+
+    @pl.when(step == 0)
+    def _():
+        pack[...] = pack_matrix(rows, True)
+        square[...] = jnp.zeros_like(square)
+        total[...] = jnp.zeros_like(total)
+
+    mixed = x_ref[:, step].astype(F32).reshape(rows, part).astype(BF16)
+    packed = jnp.dot(pack[...], mixed, preferred_element_type=F32)
+    gain = gain_ref[step]
     for h in range(HALVES):
         piece = packed[h * per_half : (h + 1) * per_half]
+        square[...] += jnp.sum(piece * piece, axis=1, keepdims=True)
+        piece = (piece * gain[h : h + 1, :]).astype(BF16)
         span = slice(h * part, (h + 1) * part)
         total[:, :hidden] += jnp.dot(piece, gate_ref[span, :], preferred_element_type=F32)
         total[:, hidden:] += jnp.dot(piece, up_ref[span, :], preferred_element_type=F32)
 
     @pl.when(step == pl.num_programs(0) - 1)
     def _():
-        gate = total[:, :hidden]
-        act_ref[...] = (gate / (1.0 + jnp.exp(-gate)) * total[:, hidden:]).astype(BF16)
+        inv = 1.0 / jnp.sqrt(square[...] / width + EPS)
+        gate = total[:, :hidden] * inv
+        act_ref[...] = (gate / (1.0 + jnp.exp(-gate)) * (total[:, hidden:] * inv)).astype(BF16)
 
 
 def expert_call(width, x, gain, gate, up):
@@ -231,7 +224,7 @@
         out_shape=jax.ShapeDtypeStruct((rows // HALVES, hidden), BF16),
         scratch_shapes=[
             pltpu.VMEM((rows, rows), BF16),
-            pltpu.VMEM((rows, 128), F32),
+            pltpu.VMEM((rows // HALVES, 1), F32),
             pltpu.VMEM((rows // HALVES, 2 * hidden), F32),
         ],
         compiler_params=pltpu.CompilerParams(vmem_limit_bytes=VMEM_BYTES),
@@ -239,32 +232,43 @@
 
 
 def down_kernel(count, *refs):
-    acts, weights, out_ref = refs[:count], refs[count : 2 * count], refs[2 * count]
+    acts, weights, out_ref, stacked = refs[:count], refs[count : 2 * count], *refs[2 * count :]
+    step = pl.program_id(0)
     total = jnp.dot(acts[0][...], weights[0][...], preferred_element_type=F32)
     for index in range(1, count):
         total = total + jnp.dot(acts[index][...], weights[index][...], preferred_element_type=F32)
-    part = total.shape[1] // HALVES
-    stacked = jnp.concatenate(
-        [total[:, h * part : (h + 1) * part] for h in range(HALVES)], axis=0
-    ).astype(BF16)
-    unpack = pack_matrix(stacked.shape[0], False)
-    out_ref[...] = jnp.dot(unpack, stacked, preferred_element_type=F32).astype(BF16)
+    stacked[step] = total.astype(BF16)
+
+    @pl.when(step == HALVES - 1)
+    def _():
+        rows, part = out_ref.shape
+        unpack = pack_matrix(rows, False)
+        value = stacked[...].reshape(rows, part)
+        out_ref[...] = jnp.dot(unpack, value, preferred_element_type=F32).astype(BF16)
 
 
 def down_call(acts, weights):
     rows = acts[0].shape[0]
-    quarter = weights[0].shape[1]
+    hidden, quarter = weights[0].shape
+    part = quarter // HALVES
     return pl.pallas_call(
         functools.partial(down_kernel, len(acts)),
-        out_shape=jax.ShapeDtypeStruct((rows * HALVES, quarter // HALVES), BF16),
+        grid=(HALVES,),
+        in_specs=[pl.BlockSpec(acts[0].shape, lambda i: (0, 0)) for _ in acts]
+        + [pl.BlockSpec((hidden, part), lambda i: (0, i)) for _ in weights],
+        out_specs=pl.BlockSpec((rows * HALVES, part), lambda i: (0, 0)),
+        out_shape=jax.ShapeDtypeStruct((rows * HALVES, part), BF16),
+        scratch_shapes=[pltpu.VMEM((HALVES, rows, part), BF16)],
         compiler_params=pltpu.CompilerParams(vmem_limit_bytes=VMEM_BYTES),
     )(*acts, *weights)
 
 
-def project_kernel(rows_ref, weight_ref, out_ref):
-    columns = lax.dot_general(
-        rows_ref[...], weight_ref[...], (((1,), (1,)), ((), ())), preferred_element_type=F32
-    )
+def project_kernel(rows_ref, weight_ref, out_ref, turned):
+    @pl.when(pl.program_id(0) == 0)
+    def _():
+        turned[...] = weight_ref[...].T
+
+    columns = jnp.dot(rows_ref[...], turned[...], preferred_element_type=F32)
     out_ref[...] = columns.reshape(out_ref.shape).astype(BF16)
 
 
@@ -280,6 +284,7 @@
         ],
         out_specs=pl.BlockSpec((owners // steps, group, weight.shape[0]), lambda i: (i, 0, 0)),
         out_shape=jax.ShapeDtypeStruct((owners, group, weight.shape[0]), BF16),
+        scratch_shapes=[pltpu.VMEM(weight.shape[::-1], BF16)],
         compiler_params=pltpu.CompilerParams(vmem_limit_bytes=VMEM_BYTES),
     )(rows, weight)
 
@@ -312,20 +317,63 @@
     )(place, x)
 
 
+def attend_kernel(scale, length_ref, q_ref, cache_ref, out_ref, highest, summed, total):
+    step = pl.program_id(0)
+    rows, latent = out_ref.shape
+    chunk = cache_ref.shape[1]
+    keys = cache_ref[...]
+    values = keys[:latent].T
+    valid = step * chunk + iota((1, chunk), 1) < length_ref[0]
+    block = min(rows, 256)
+
+    @pl.when(step == 0)
+    def _():
+        highest[...] = jnp.full_like(highest, -1e30)
+        summed[...] = jnp.zeros_like(summed)
+        total[...] = jnp.zeros_like(total)
+
+    for at in range(0, rows, block):
+        span = slice(at, at + block)
+        scores = jnp.dot(q_ref[span, :], keys, preferred_element_type=F32)
+        scores = jnp.where(valid, scores, -1e30)
+        before = highest[span, :]
+        now = jnp.maximum(before, jnp.max(scores, axis=1, keepdims=True))
+        weights = jnp.exp2((scores - now) * scale)
+        fade = jnp.exp2((before - now) * scale)
+        highest[span, :] = now
+        summed[span, :] = summed[span, :] * fade + jnp.sum(weights, axis=1, keepdims=True)
+        total[span, :] = total[span, :] * fade + jnp.dot(
+            weights.astype(BF16), values, preferred_element_type=F32
+        )
+
+    @pl.when(step == pl.num_programs(0) - 1)
+    def _():
+        out_ref[...] = (total[...] / summed[...]).astype(BF16)
+
+
 def attend_request(query_block, cache_block, length, value_up, score_scale):
     depths, nodes, heads_dev, width_qk = query_block.shape
     latent = value_up.shape[1]
     query_rows = query_block.reshape(-1, width_qk)
-    scores = (
-        jnp.einsum("qk,ck->qc", query_rows, cache_block, preferred_element_type=F32)
-        * score_scale
-    )
-    valid = jnp.arange(cache_block.shape[0], dtype=jnp.int32) < length
-    scores = jnp.where(valid[None, :], scores, -jnp.inf)
-    highest = jnp.max(scores, axis=1, keepdims=True)
-    weights = jnp.exp(scores - highest)
-    probs = (weights / jnp.sum(weights, axis=1, keepdims=True)).astype(BF16)
-    latent_out = jnp.dot(probs, cache_block[:, :latent], preferred_element_type=F32).astype(BF16)
+    rows = query_rows.shape[0]
+    chunk = 2048
+    latent_out = pl.pallas_call(
+        functools.partial(attend_kernel, score_scale * math.log2(math.e)),
+        grid=(cache_block.shape[0] // chunk,),
+        in_specs=[
+            pl.BlockSpec(memory_space=pltpu.SMEM),
+            pl.BlockSpec((rows, width_qk), lambda i: (0, 0)),
+            pl.BlockSpec((width_qk, chunk), lambda i: (0, i)),
+        ],
+        out_specs=pl.BlockSpec((rows, latent), lambda i: (0, 0)),
+        out_shape=jax.ShapeDtypeStruct((rows, latent), BF16),
+        scratch_shapes=[
+            pltpu.VMEM((rows, 1), F32),
+            pltpu.VMEM((rows, 1), F32),
+            pltpu.VMEM((rows, latent), F32),
+        ],
+        compiler_params=pltpu.CompilerParams(vmem_limit_bytes=VMEM_BYTES),
+    )(length, query_rows, cache_block.T)
     latent_out = latent_out.reshape(depths * nodes, heads_dev, latent)
     mixed = jnp.einsum("nhl,hld->nhd", latent_out, value_up, preferred_element_type=F32)
     return mixed.astype(BF16).reshape(depths, nodes, -1)
@@ -365,7 +413,7 @@
     def deal(values):
         return [values[0]] + [lax.ppermute(values[k], "tp", shifts[k]) for k in range(1, tp)]
 
-    heads = attend_request(queries[:, 0], cache[0], cache_len[0], value_up, score_scale)
+    heads = attend_request(queries[:, 0], cache[0], cache_len, value_up, score_scale)
     heads = heads.reshape(depths * nodes, -1)
     gathered = lax.all_gather(heads, "dp", axis=0, tiled=True)
 
@@ -392,29 +440,29 @@
     normed = embed * (1.0 / jnp.sqrt(embed_sq / width + EPS))[..., None] * embed_gain
     gains = notes[(mine - jnp.arange(tp, dtype=jnp.int32)) % tp, :gain_rows].reshape(tp, HALVES, part)
     gathered, normed, gains, *down = lax.optimization_barrier((gathered, normed, gains, *down))
-
     columns = project(gathered, out_proj.T, groups)
     columns = lax.all_to_all(columns, "dp", split_axis=0, concat_axis=0, tiled=True)
     attn = deal(settle(mine.reshape(1).astype(jnp.int32), columns, tp))
 
+    names = jnp.pad(parents[:, 0, :, None], ((1, 0), (0, 0), (0, 0)))
+    tables = jnp.concatenate([expert_ids[:, 0], names], axis=2)
     drafted = []
     carried = None
-    ids = expert_ids[:, 0]
-    parent_columns = parents[:, 0, :, None]
     for depth in range(depths + 1):
-        args = [ids]
-        args += [root_hidden, normed, *attn] if depth == 0 else carried
-        if depth < depths:
-            args += [router.T, moe_gain[None]]
+        args = [tables]
+        if depth == 0:
+            args += [root_hidden, normed, *attn, router.T, moe_gain[None]]
+        else:
+            args += carried
         if 0 < depth < depths:
-            args += [parent_columns, base]
+            args += [routed, base]
         result = list(owner_call(depth, depths, experts, width, tp, args, nodes, quarter))
         if depth > 0:
             drafted.append(result.pop(0))
         if depth == depths:
             break
         if depth == 0:
-            base = result.pop()
+            routed, base = result.pop(-2), result.pop()
         state, stats, outgoing = result
         all_stats = share(stats)
         outgoing = outgoing.reshape(experts * tp, HALVES * SLOTS, part)

time: 327 us -> 317 us (0.969)
  blocking collectives: 118 us -> 98.1 us
  waiting for transfers between devices: 73.2 us -> 89 us
  Pallas kernels: 35.1 us -> 46.3 us
  matrix products: 12 us -> 1.1 us
  local copies, waits for them, and re-layouts: 19.9 us -> 11.3 us
  starting transfers between devices: 47.4 us -> 55 us
  other arithmetic: 4.91 us -> 1 us
    all_to_all x1 -> x0, blocking collectives: 18.2 us -> none  [local(): lax.all_to_all(columns, 'dp', split_axis=0, concat_axis=0, tiled=True)]
    pallas_call x3 -> x4, Pallas kernels: 9.75 us -> 23.3 us  [the longest x1 13.9 us: attend_request(): pl.pallas_call(functools.partial(attend_kernel, score_scale * math.log2(m...]
    dot_general x2 -> x0, matrix products: 10.9 us -> none  [the longest x1 7.21 us: attend_request(): jnp.einsum('qk,ck->qc', query_rows, cache_block, preferred_element_type=F32)]
    all_to_all x0 -> x1, waiting for transfers between devices: none -> 10.2 us  [local(): lax.all_to_all(columns, 'dp', split_axis=0, concat_axis=0, tiled=True)]
    all_to_all x0 -> x1, starting transfers between devices: none -> 9.23 us  [local(): lax.all_to_all(columns, 'dp', split_axis=0, concat_axis=0, tiled=True)]
    unnamed x72 -> x32, local copies, waits for them, and re-layouts: 13.4 us -> 5.97 us
  transfers between devices with their start and end apart: 31 -> 32, of which waited for: 26 -> 27; matrix products, arithmetic and copies ran while one was open for 2% -> 2% of each run, Pallas kernels for 0% -> 0%
where the time goes in v3:
time: 317 us; the launch traced here: 316 us
  blocking collectives  98.1 us (31%)
  waiting for transfers between devices  89 us (28%)
  starting transfers between devices  55 us (17%)
  Pallas kernels  46.3 us (15%)
  between operations  14.3 us (5%)
  local copies, waits for them, and re-layouts  11.3 us (4%)
    all_to_all x3, blocking collectives, local(): lax.all_to_all(outgoing, ('dp', 'tp'), split_axis=0, concat_axis=0, tiled...  98.1 us
    ppermute x6, waiting for transfers between devices, deal(): lax.ppermute(values[k], 'tp', shifts[k])  43.4 us
    ppermute x21, starting transfers between devices, share(): lax.ppermute(value, 'tp', shifts[k])  24.3 us
    ppermute x21, waiting for transfers between devices, share(): lax.ppermute(value, 'tp', shifts[k])  18.7 us
    all_to_all x3, waiting for transfers between devices, local(): lax.all_to_all(answer, 'dp', split_axis=0, concat_axis=0, tiled=True)  16 us
    all_to_all x3, starting transfers between devices, local(): lax.all_to_all(answer, 'dp', split_axis=0, concat_axis=0, tiled=True)  15.3 us
    pallas_call x1, Pallas kernels, attend_request(): pl.pallas_call(functools.partial(attend_kernel, score_scale * math.log2(m...  13.9 us
    pallas_call x3, Pallas kernels, expert_call(): pl.pallas_call(functools.partial(expert_kernel, width), grid=(quarters,),...  13.5 us
  transfers between devices with their start and end apart: 32, of which 27 were waited for; matrix products, arithmetic and copies ran while one was open for 2% of the time, Pallas kernels for 0%

profile of v3, /device:TPU:1, one launch (start us, length us, event | category | flops | bytes accessed | tf_op | source)
XLA Modules:
  0.0 316.2 jit_solution(1253500751166725956)
XLA Ops:
  8.4 13.9 %shard_map.145 = bf16[768,512]{1,0:T(8,128)(2,1)S(1)} custom-call(s32[1]{0:T(128)S(6)} %copy.39.length_ref, bf16[768,576]{1,0:T(8,128)(2,1)S(1)} %bitcast.79, bf16[576,4096]{1,0:T(8,128)(2,1)} %bitcast.87), custom_call_target="tpu_custom_call" | custom-call | tf_op jit(solution)/shard_map/pallas_call | solution.py:360
  24.4 2.2 collective-permute-start
  26.6 2.6 collective-permute-start.1
  30.2 3.7 %dynamic-slice_bitcast_fusion = (bf16[256,1792]{1,0:T(8,128)(2,1)}, bf16[256,1792]{1,0:T(8,128)(2,1)}, bf16[256,1792]{1,0:T(8,128)(2,1)}, bf16[256,1792]{1,0:T(8,128)(2,1)S(1)}) fusion(bf16[1,256,7168]{2,1,0:T(8,128)(2,1)} %param.29, s32[]{:T(128)S(6)} %select_n.63, s32[]{:T(128)S(6)} %select_n.61, s32[]{:T(128)S(6)} %select_n.59, s32[]{:T(128)S(6)} %select_n.57), kind=kLoop, calls=%fused_computation.3 | loop fusion | bytes 7340048 | tf_op jit(solution)/shard_map/dynamic_slice | solution.py:423
  37.7 19.2 %collective-permute-done.3.refs_5_ = bf16[256,1792]{1,0:T(8,128)(2,1)S(1)} collective-permute-done((bf16[256,1792]{1,0:T(8,128)(2,1)}, bf16[256,1792]{1,0:T(8,128)(2,1)S(1)}, u32[]{:S(2)}, u32[]{:S(2)}) %collective-permute-start.3) | collective-permute-done | bytes 917536 | tf_op jit(solution)/shard_map/ppermute | solution.py:414
  56.9 17.3 %collective-permute-done.4.refs_6_ = bf16[256,1792]{1,0:T(8,128)(2,1)S(1)} collective-permute-done((bf16[256,1792]{1,0:T(8,128)(2,1)}, bf16[256,1792]{1,0:T(8,128)(2,1)S(1)}, u32[]{:S(2)}, u32[]{:S(2)}) %collective-permute-start.4) | collective-permute-done | bytes 917536 | tf_op jit(solution)/shard_map/ppermute | solution.py:414
  74.2 2.4 collective-permute-done.5.refs_7_
  78.7 6.1 %shard_map.146 = bf16[32,24,224]{2,1,0:T(8,128)(2,1)} custom-call(bf16[768,4096]{1,0:T(8,128)(2,1)} %all-gather.2.cloned.1.call-done.rows_ref, bf16[224,4096]{1,0:T(8,128)(2,1)S(1)} %bitcast.78), custom_call_target="tpu_custom_call" | custom-call | tf_op jit(solution)/shard_map/pallas_call | solution.py:278
  84.8 9.2 %all-to-all-start = ((bf16[32,24,224]{2,1,0:T(8,128)(2,1)}), bf16[32,24,224]{2,1,0:T(8,128)(2,1)S(1)}, u32[]{:S(2)}, u32[]{:S(2)}) async-start(bf16[32,24,224]{2,1,0:T(8,128)(2,1)} %shard_map.146), calls=%async_computation | async-start | bytes 786432 | tf_op jit(solution)/shard_map/all_to_all | solution.py:444
  94.1 10.2 %all-to-all-done.x_ref = bf16[32,24,224]{2,1,0:T(8,128)(2,1)S(1)} async-done(((bf16[32,24,224]{2,1,0:T(8,128)(2,1)}), bf16[32,24,224]{2,1,0:T(8,128)(2,1)S(1)}, u32[]{:S(2)}, u32[]{:S(2)}) %all-to-all-start) | async-done | bytes 344096 | tf_op jit(solution)/shard_map/all_to_all | solution.py:444
  104.7 3.3 %collective-permute-start.7 = (bf16[24,1792]{1,0:T(8,128)(2,1)S(1)}, bf16[24,1792]{1,0:T(8,128)(2,1)S(1)}, u32[]{:S(2)}, u32[]{:S(2)}) collective-permute-start(bf16[24,1792]{1,0:T(8,128)(2,1)S(1)} %get-tuple-element.37), channel_id=1, source_target_pairs={{0,2},{1,3},{2,0},{3,1},{4,6},{5,7},{6,4},{7,5},{8,10},{9,11},{10,... | collective-permute-start | bytes 258056 | tf_op jit(solution)/shard_map/ppermute | solution.py:414
  110.0 2.5 collective-permute-done.7.refs_5_
  114.2 33.5 %all_to_all.35 = bf16[128,8,896]{2,1,0:T(8,128)(2,1)S(1)} all-to-all(bf16[128,8,896]{2,1,0:T(8,128)(2,1)S(1)} %bitcast.73), channel_id=1, replica_groups=mesh['dp'=32,'tp'=4] {'dp','tp'}, dimensions={0} | all-to-all | bytes 3670016 | tf_op jit(solution)/shard_map/all_to_all | solution.py:469
  147.7 4.5 %shard_map.149.refs_0_ = bf16[128,256]{1,0:T(8,128)(2,1)S(1)} custom-call(bf16[32,4,8,896]{3,2,1,0:T(8,128)(2,1)S(1)} %bitcast.69, f32[4,2,896]{2,1,0:T(2,128)S(1)} %reshape.123.gain_ref, bf16[7168,256]{1,0:T(8,128)(2,1)S(1)} %bitcast.65, bf16[7168,256]{1,0:T(8,128)(2,1)} %bitcast.84), custom_call_target="tpu_custom_call" | custom-call | tf_op jit(solution)/shard_map/pallas_call | solution.py:214
  152.3 2.7 collective-permute-start.11
  156.9 2.4 collective-permute-done.9.refs_1_
  159.3 3.1 shard_map.150
  162.5 5.5 %all-to-all-start.2 = ((bf16[32,8,896]{2,1,0:T(8,128)(2,1)}), bf16[32,8,896]{2,1,0:T(8,128)(2,1)S(1)}, u32[]{:S(2)}, u32[]{:S(2)}) async-start(bf16[32,8,896]{2,1,0:T(8,128)(2,1)} %bitcast.30), calls=%async_computation.2 | async-start | bytes 917504 | tf_op jit(solution)/shard_map/all_to_all | solution.py:474
  172.6 6.4 %all-to-all-done.2 = bf16[32,8,896]{2,1,0:T(8,128)(2,1)S(1)} async-done(((bf16[32,8,896]{2,1,0:T(8,128)(2,1)}), bf16[32,8,896]{2,1,0:T(8,128)(2,1)S(1)}, u32[]{:S(2)}, u32[]{:S(2)}) %all-to-all-start.2) | async-done | bytes 458784 | tf_op jit(solution)/shard_map/all_to_all | solution.py:474
  181.2 31.7 %all_to_all.36 = bf16[128,8,896]{2,1,0:T(8,128)(2,1)S(1)} all-to-all(bf16[128,8,896]{2,1,0:T(8,128)(2,1)S(1)} %bitcast.74), channel_id=1, replica_groups=mesh['dp'=32,'tp'=4] {'dp','tp'}, dimensions={0} | all-to-all | bytes 3670016 | tf_op jit(solution)/shard_map/all_to_all | solution.py:469
  212.9 4.5 %shard_map.152.refs_0_ = bf16[128,256]{1,0:T(8,128)(2,1)S(1)} custom-call(bf16[32,4,8,896]{3,2,1,0:T(8,128)(2,1)S(1)} %bitcast.70, f32[4,2,896]{2,1,0:T(2,128)S(1)} %reshape.123.gain_ref, bf16[7168,256]{1,0:T(8,128)(2,1)S(1)} %bitcast.66, bf16[7168,256]{1,0:T(8,128)(2,1)} %bitcast.85), custom_call_target="tpu_custom_call" | custom-call | tf_op jit(solution)/shard_map/pallas_call | solution.py:214
  223.8 3.2 %shard_map.153 = bf16[256,896]{1,0:T(8,128)(2,1)} custom-call(bf16[128,256]{1,0:T(8,128)(2,1)S(1)} %shard_map.152.refs_0_, bf16[128,256]{1,0:T(8,128)(2,1)S(1)} %collective-permute-done.15.refs_1_, bf16[128,256]{1,0:T(8,128)(2,1)S(1)} %collective-permute-done.16.refs_2_, bf16[128,256]{1,0:T(8,128)(2,1)S(1)} %collective-permute-done.17.refs_3_, ...), custom_call_target="tpu_custom_call" | custom-call | tf_op jit(solution)/shard_map/pallas_call | solution.py:254
  227.0 4.9 %all-to-all-start.4 = ((bf16[32,8,896]{2,1,0:T(8,128)(2,1)}), bf16[32,8,896]{2,1,0:T(8,128)(2,1)S(1)}, u32[]{:S(2)}, u32[]{:S(2)}) async-start(bf16[32,8,896]{2,1,0:T(8,128)(2,1)} %bitcast.35), calls=%async_computation.4 | async-start | bytes 917504 | tf_op jit(solution)/shard_map/all_to_all | solution.py:474
  232.6 2.8 collective-permute-start.19
  238.2 4.8 %all-to-all-done.4 = bf16[32,8,896]{2,1,0:T(8,128)(2,1)S(1)} async-done(((bf16[32,8,896]{2,1,0:T(8,128)(2,1)}), bf16[32,8,896]{2,1,0:T(8,128)(2,1)S(1)}, u32[]{:S(2)}, u32[]{:S(2)}) %all-to-all-start.4) | async-done | bytes 458784 | tf_op jit(solution)/shard_map/all_to_all | solution.py:474
  245.2 32.9 %all_to_all.37 = bf16[128,8,896]{2,1,0:T(8,128)(2,1)S(1)} all-to-all(bf16[128,8,896]{2,1,0:T(8,128)(2,1)S(1)} %bitcast.72), channel_id=1, replica_groups=mesh['dp'=32,'tp'=4] {'dp','tp'}, dimensions={0} | all-to-all | bytes 3670016 | tf_op jit(solution)/shard_map/all_to_all | solution.py:469
  278.1 4.5 %shard_map.155.refs_0_ = bf16[128,256]{1,0:T(8,128)(2,1)S(1)} custom-call(bf16[32,4,8,896]{3,2,1,0:T(8,128)(2,1)S(1)} %bitcast.68, f32[4,2,896]{2,1,0:T(2,128)S(1)} %reshape.123.gain_ref, bf16[7168,256]{1,0:T(8,128)(2,1)S(1)} %bitcast.67, bf16[7168,256]{1,0:T(8,128)(2,1)} %bitcast.86), custom_call_target="tpu_custom_call" | custom-call | tf_op jit(solution)/shard_map/pallas_call | solution.py:214
  285.5 2.0 collective-permute-done.21.refs_1_
  289.0 3.1 shard_map.156
  292.2 4.9 %all-to-all-start.6 = ((bf16[32,8,896]{2,1,0:T(8,128)(2,1)}), bf16[32,8,896]{2,1,0:T(8,128)(2,1)S(1)}, u32[]{:S(2)}, u32[]{:S(2)}) async-start(bf16[32,8,896]{2,1,0:T(8,128)(2,1)} %bitcast.40), calls=%async_computation.6 | async-start | bytes 917504 | tf_op jit(solution)/shard_map/all_to_all | solution.py:474
  297.8 2.8 collective-permute-start.25
  303.3 4.8 %all-to-all-done.6 = bf16[32,8,896]{2,1,0:T(8,128)(2,1)S(1)} async-done(((bf16[32,8,896]{2,1,0:T(8,128)(2,1)}), bf16[32,8,896]{2,1,0:T(8,128)(2,1)S(1)}, u32[]{:S(2)}, u32[]{:S(2)}) %all-to-all-start.6) | async-done | bytes 458784 | tf_op jit(solution)/shard_map/all_to_all | solution.py:474
  (100 shorter events, 44.1 us)
Async XLA Ops:
  6.5 70.7 %all-gather.2.cloned.1.call-start = ((), (), s32[]{:S(2)}) async-start(), calls=%async_computation.7 | async-start | bytes 6488064 | tf_op jit(solution)/shard_map/all_gather | solution.py:418
  24.4 10.8 %collective-permute-start = (f32[16,128]{1,0:T(8,128)S(1)}, f32[16,128]{1,0:T(8,128)S(1)}, u32[]{:S(2)}, u32[]{:S(2)}) collective-permute-start(f32[16,128]{1,0:T(8,128)S(1)} %select_maximum_fusion), channel_id=1, source_target_pairs={{0,1},{1,2},{2,3},{3,0},{4,5},{5,6},{6,7},{7,4},{8,9},{9,10},{10,1... | collective-permute-start | bytes 24584 | tf_op jit(solution)/shard_map/ppermute | solution.py:411
  26.6 10.2 %collective-permute-start.1 = (f32[16,128]{1,0:T(8,128)S(1)}, f32[16,128]{1,0:T(8,128)S(1)}, u32[]{:S(2)}, u32[]{:S(2)}) collective-permute-start(f32[16,128]{1,0:T(8,128)S(1)} %select_maximum_fusion), channel_id=1, source_target_pairs={{0,2},{1,3},{2,0},{3,1},{4,6},{5,7},{6,4},{7,5},{8,10},{9,11},{10,... | collective-permute-start | bytes 24584 | tf_op jit(solution)/shard_map/ppermute | solution.py:411
  29.2 7.6 %collective-permute-start.2 = (f32[16,128]{1,0:T(8,128)S(1)}, f32[16,128]{1,0:T(8,128)S(1)}, u32[]{:S(2)}, u32[]{:S(2)}) collective-permute-start(f32[16,128]{1,0:T(8,128)S(1)} %select_maximum_fusion), channel_id=1, source_target_pairs={{0,3},{1,0},{2,1},{3,2},{4,7},{5,4},{6,5},{7,6},{8,11},{9,8},{10,9... | collective-permute-start | bytes 24584 | tf_op jit(solution)/shard_map/ppermute | solution.py:411
  33.9 23.0 %collective-permute-start.3 = (bf16[256,1792]{1,0:T(8,128)(2,1)}, bf16[256,1792]{1,0:T(8,128)(2,1)S(1)}, u32[]{:S(2)}, u32[]{:S(2)}) collective-permute-start(bf16[256,1792]{1,0:T(8,128)(2,1)} %get-tuple-element.59), channel_id=1, source_target_pairs={{0,1},{1,2},{2,3},{3,0},{4,5},{5,6},{6,7},{7,4},{8,9},{9,10},{10,1... | collective-permute-start | bytes 2752520 | tf_op jit(solution)/shard_map/ppermute | solution.py:414
  34.3 39.9 %collective-permute-start.4 = (bf16[256,1792]{1,0:T(8,128)(2,1)}, bf16[256,1792]{1,0:T(8,128)(2,1)S(1)}, u32[]{:S(2)}, u32[]{:S(2)}) collective-permute-start(bf16[256,1792]{1,0:T(8,128)(2,1)} %get-tuple-element.58), channel_id=1, source_target_pairs={{0,2},{1,3},{2,0},{3,1},{4,6},{5,7},{6,4},{7,5},{8,10},{9,11},{10,... | collective-permute-start | bytes 2752520 | tf_op jit(solution)/shard_map/ppermute | solution.py:414
  35.1 41.5 %collective-permute-start.5 = (bf16[256,1792]{1,0:T(8,128)(2,1)}, bf16[256,1792]{1,0:T(8,128)(2,1)}, u32[]{:S(2)}, u32[]{:S(2)}) collective-permute-start(bf16[256,1792]{1,0:T(8,128)(2,1)} %get-tuple-element.57), channel_id=1, source_target_pairs={{0,3},{1,0},{2,1},{3,2},{4,7},{5,4},{6,5},{7,6},{8,11},{9,8},{10,9... | collective-permute-start | bytes 2752520 | tf_op jit(solution)/shard_map/ppermute | solution.py:414
  84.8 19.5 %all-to-all-start = ((bf16[32,24,224]{2,1,0:T(8,128)(2,1)}), bf16[32,24,224]{2,1,0:T(8,128)(2,1)S(1)}, u32[]{:S(2)}, u32[]{:S(2)}) async-start(bf16[32,24,224]{2,1,0:T(8,128)(2,1)} %shard_map.146), calls=%async_computation | async-start | bytes 786432 | tf_op jit(solution)/shard_map/all_to_all | solution.py:444
  104.5 5.5 %collective-permute-start.6 = (bf16[24,1792]{1,0:T(8,128)(2,1)S(1)}, bf16[24,1792]{1,0:T(8,128)(2,1)S(1)}, u32[]{:S(2)}, u32[]{:S(2)}) collective-permute-start(bf16[24,1792]{1,0:T(8,128)(2,1)S(1)} %get-tuple-element.36), channel_id=1, source_target_pairs={{0,1},{1,2},{2,3},{3,0},{4,5},{5,6},{6,7},{7,4},{8,9},{9,10},{10,1... | collective-permute-start | bytes 258056 | tf_op jit(solution)/shard_map/ppermute | solution.py:414
  104.7 7.9 %collective-permute-start.7 = (bf16[24,1792]{1,0:T(8,128)(2,1)S(1)}, bf16[24,1792]{1,0:T(8,128)(2,1)S(1)}, u32[]{:S(2)}, u32[]{:S(2)}) collective-permute-start(bf16[24,1792]{1,0:T(8,128)(2,1)S(1)} %get-tuple-element.37), channel_id=1, source_target_pairs={{0,2},{1,3},{2,0},{3,1},{4,6},{5,7},{6,4},{7,5},{8,10},{9,11},{10,... | collective-permute-start | bytes 258056 | tf_op jit(solution)/shard_map/ppermute | solution.py:414
  108.0 4.6 %collective-permute-start.8 = (bf16[24,1792]{1,0:T(8,128)(2,1)S(1)}, bf16[24,1792]{1,0:T(8,128)(2,1)S(1)}, u32[]{:S(2)}, u32[]{:S(2)}) collective-permute-start(bf16[24,1792]{1,0:T(8,128)(2,1)S(1)} %get-tuple-element.38), channel_id=1, source_target_pairs={{0,3},{1,0},{2,1},{3,2},{4,7},{5,4},{6,5},{7,6},{8,11},{9,8},{10,9... | collective-permute-start | bytes 258056 | tf_op jit(solution)/shard_map/ppermute | solution.py:414
  152.2 4.7 %collective-permute-start.10 = (bf16[128,256]{1,0:T(8,128)(2,1)S(1)}, bf16[128,256]{1,0:T(8,128)(2,1)S(1)}, u32[]{:S(2)}, u32[]{:S(2)}) collective-permute-start(bf16[128,256]{1,0:T(8,128)(2,1)S(1)} %shard_map.149.refs_0_), channel_id=1, source_target_pairs={{0,2},{1,3},{2,0},{3,1},{4,6},{5,7},{6,4},{7,5},{8,10},{9,11},{10,... | collective-permute-start | bytes 196616 | tf_op jit(solution)/shard_map/ppermute | solution.py:411
  152.3 4.6 %collective-permute-start.11 = (bf16[128,256]{1,0:T(8,128)(2,1)S(1)}, bf16[128,256]{1,0:T(8,128)(2,1)S(1)}, u32[]{:S(2)}, u32[]{:S(2)}) collective-permute-start(bf16[128,256]{1,0:T(8,128)(2,1)S(1)} %shard_map.149.refs_0_), channel_id=1, source_target_pairs={{0,3},{1,0},{2,1},{3,2},{4,7},{5,4},{6,5},{7,6},{8,11},{9,8},{10,9... | collective-permute-start | bytes 196616 | tf_op jit(solution)/shard_map/ppermute | solution.py:411
  155.0 4.3 %collective-permute-start.9 = (bf16[128,256]{1,0:T(8,128)(2,1)S(1)}, bf16[128,256]{1,0:T(8,128)(2,1)S(1)}, u32[]{:S(2)}, u32[]{:S(2)}) collective-permute-start(bf16[128,256]{1,0:T(8,128)(2,1)S(1)} %shard_map.149.refs_0_), channel_id=1, source_target_pairs={{0,1},{1,2},{2,3},{3,0},{4,5},{5,6},{6,7},{7,4},{8,9},{9,10},{10,1... | collective-permute-start | bytes 196616 | tf_op jit(solution)/shard_map/ppermute | solution.py:411
  162.5 16.6 %all-to-all-start.2 = ((bf16[32,8,896]{2,1,0:T(8,128)(2,1)}), bf16[32,8,896]{2,1,0:T(8,128)(2,1)S(1)}, u32[]{:S(2)}, u32[]{:S(2)}) async-start(bf16[32,8,896]{2,1,0:T(8,128)(2,1)} %bitcast.30), calls=%async_computation.2 | async-start | bytes 917504 | tf_op jit(solution)/shard_map/all_to_all | solution.py:474
  168.0 4.0 %collective-permute-start.12 = (f32[8,128]{1,0:T(8,128)S(1)}, f32[8,128]{1,0:T(8,128)S(1)}, u32[]{:S(2)}, u32[]{:S(2)}) collective-permute-start(f32[8,128]{1,0:T(8,128)S(1)} %get-tuple-element.46.refs_3_), channel_id=1, source_target_pairs={{0,1},{1,2},{2,3},{3,0},{4,5},{5,6},{6,7},{7,4},{8,9},{9,10},{10,1... | collective-permute-start | bytes 12296 | tf_op jit(solution)/shard_map/ppermute | solution.py:411
  168.0 4.3 %collective-permute-start.13 = (f32[8,128]{1,0:T(8,128)S(1)}, f32[8,128]{1,0:T(8,128)S(1)}, u32[]{:S(2)}, u32[]{:S(2)}) collective-permute-start(f32[8,128]{1,0:T(8,128)S(1)} %get-tuple-element.46.refs_3_), channel_id=1, source_target_pairs={{0,2},{1,3},{2,0},{3,1},{4,6},{5,7},{6,4},{7,5},{8,10},{9,11},{10,... | collective-permute-start | bytes 12296 | tf_op jit(solution)/shard_map/ppermute | solution.py:411
  168.9 3.7 %collective-permute-start.14 = (f32[8,128]{1,0:T(8,128)S(1)}, f32[8,128]{1,0:T(8,128)S(1)}, u32[]{:S(2)}, u32[]{:S(2)}) collective-permute-start(f32[8,128]{1,0:T(8,128)S(1)} %get-tuple-element.46.refs_3_), channel_id=1, source_target_pairs={{0,3},{1,0},{2,1},{3,2},{4,7},{5,4},{6,5},{7,6},{8,11},{9,8},{10,9... | collective-permute-start | bytes 12296 | tf_op jit(solution)/shard_map/ppermute | solution.py:411
  217.4 4.9 %collective-permute-start.15 = (bf16[128,256]{1,0:T(8,128)(2,1)S(1)}, bf16[128,256]{1,0:T(8,128)(2,1)S(1)}, u32[]{:S(2)}, u32[]{:S(2)}) collective-permute-start(bf16[128,256]{1,0:T(8,128)(2,1)S(1)} %shard_map.152.refs_0_), channel_id=1, source_target_pairs={{0,1},{1,2},{2,3},{3,0},{4,5},{5,6},{6,7},{7,4},{8,9},{9,10},{10,1... | collective-permute-start | bytes 196616 | tf_op jit(solution)/shard_map/ppermute | solution.py:411
  217.9 5.6 %collective-permute-start.16 = (bf16[128,256]{1,0:T(8,128)(2,1)S(1)}, bf16[128,256]{1,0:T(8,128)(2,1)S(1)}, u32[]{:S(2)}, u32[]{:S(2)}) collective-permute-start(bf16[128,256]{1,0:T(8,128)(2,1)S(1)} %shard_map.152.refs_0_), channel_id=1, source_target_pairs={{0,2},{1,3},{2,0},{3,1},{4,6},{5,7},{6,4},{7,5},{8,10},{9,11},{10,... | collective-permute-start | bytes 196616 | tf_op jit(solution)/shard_map/ppermute | solution.py:411
  218.8 5.1 %collective-permute-start.17 = (bf16[128,256]{1,0:T(8,128)(2,1)S(1)}, bf16[128,256]{1,0:T(8,128)(2,1)S(1)}, u32[]{:S(2)}, u32[]{:S(2)}) collective-permute-start(bf16[128,256]{1,0:T(8,128)(2,1)S(1)} %shard_map.152.refs_0_), channel_id=1, source_target_pairs={{0,3},{1,0},{2,1},{3,2},{4,7},{5,4},{6,5},{7,6},{8,11},{9,8},{10,9... | collective-permute-start | bytes 196616 | tf_op jit(solution)/shard_map/ppermute | solution.py:411
  227.0 16.0 %all-to-all-start.4 = ((bf16[32,8,896]{2,1,0:T(8,128)(2,1)}), bf16[32,8,896]{2,1,0:T(8,128)(2,1)S(1)}, u32[]{:S(2)}, u32[]{:S(2)}) async-start(bf16[32,8,896]{2,1,0:T(8,128)(2,1)} %bitcast.35), calls=%async_computation.4 | async-start | bytes 917504 | tf_op jit(solution)/shard_map/all_to_all | solution.py:474
  231.9 4.0 %collective-permute-start.18 = (f32[8,128]{1,0:T(8,128)S(1)}, f32[8,128]{1,0:T(8,128)S(1)}, u32[]{:S(2)}, u32[]{:S(2)}) collective-permute-start(f32[8,128]{1,0:T(8,128)S(1)} %get-tuple-element.52.refs_3_), channel_id=1, source_target_pairs={{0,1},{1,2},{2,3},{3,0},{4,5},{5,6},{6,7},{7,4},{8,9},{9,10},{10,1... | collective-permute-start | bytes 12296 | tf_op jit(solution)/shard_map/ppermute | solution.py:411
  232.6 4.0 %collective-permute-start.19 = (f32[8,128]{1,0:T(8,128)S(1)}, f32[8,128]{1,0:T(8,128)S(1)}, u32[]{:S(2)}, u32[]{:S(2)}) collective-permute-start(f32[8,128]{1,0:T(8,128)S(1)} %get-tuple-element.52.refs_3_), channel_id=1, source_target_pairs={{0,2},{1,3},{2,0},{3,1},{4,6},{5,7},{6,4},{7,5},{8,10},{9,11},{10,... | collective-permute-start | bytes 12296 | tf_op jit(solution)/shard_map/ppermute | solution.py:411
  235.4 2.8 collective-permute-start.20
  282.6 4.9 %collective-permute-start.21 = (bf16[128,256]{1,0:T(8,128)(2,1)S(1)}, bf16[128,256]{1,0:T(8,128)(2,1)S(1)}, u32[]{:S(2)}, u32[]{:S(2)}) collective-permute-start(bf16[128,256]{1,0:T(8,128)(2,1)S(1)} %shard_map.155.refs_0_), channel_id=1, source_target_pairs={{0,1},{1,2},{2,3},{3,0},{4,5},{5,6},{6,7},{7,4},{8,9},{9,10},{10,1... | collective-permute-start | bytes 196616 | tf_op jit(solution)/shard_map/ppermute | solution.py:411
  283.0 5.6 %collective-permute-start.22 = (bf16[128,256]{1,0:T(8,128)(2,1)S(1)}, bf16[128,256]{1,0:T(8,128)(2,1)S(1)}, u32[]{:S(2)}, u32[]{:S(2)}) collective-permute-start(bf16[128,256]{1,0:T(8,128)(2,1)S(1)} %shard_map.155.refs_0_), channel_id=1, source_target_pairs={{0,2},{1,3},{2,0},{3,1},{4,6},{5,7},{6,4},{7,5},{8,10},{9,11},{10,... | collective-permute-start | bytes 196616 | tf_op jit(solution)/shard_map/ppermute | solution.py:411
  284.0 5.1 %collective-permute-start.23 = (bf16[128,256]{1,0:T(8,128)(2,1)S(1)}, bf16[128,256]{1,0:T(8,128)(2,1)S(1)}, u32[]{:S(2)}, u32[]{:S(2)}) collective-permute-start(bf16[128,256]{1,0:T(8,128)(2,1)S(1)} %shard_map.155.refs_0_), channel_id=1, source_target_pairs={{0,3},{1,0},{2,1},{3,2},{4,7},{5,4},{6,5},{7,6},{8,11},{9,8},{10,9... | collective-permute-start | bytes 196616 | tf_op jit(solution)/shard_map/ppermute | solution.py:411
  292.2 16.0 %all-to-all-start.6 = ((bf16[32,8,896]{2,1,0:T(8,128)(2,1)}), bf16[32,8,896]{2,1,0:T(8,128)(2,1)S(1)}, u32[]{:S(2)}, u32[]{:S(2)}) async-start(bf16[32,8,896]{2,1,0:T(8,128)(2,1)} %bitcast.40), calls=%async_computation.6 | async-start | bytes 917504 | tf_op jit(solution)/shard_map/all_to_all | solution.py:474
  297.1 4.0 %collective-permute-start.24 = (f32[8,128]{1,0:T(8,128)S(1)}, f32[8,128]{1,0:T(8,128)S(1)}, u32[]{:S(2)}, u32[]{:S(2)}) collective-permute-start(f32[8,128]{1,0:T(8,128)S(1)} %get-tuple-element.56.refs_3_), channel_id=1, source_target_pairs={{0,1},{1,2},{2,3},{3,0},{4,5},{5,6},{6,7},{7,4},{8,9},{9,10},{10,1... | collective-permute-start | bytes 12296 | tf_op jit(solution)/shard_map/ppermute | solution.py:411
  297.8 4.0 %collective-permute-start.25 = (f32[8,128]{1,0:T(8,128)S(1)}, f32[8,128]{1,0:T(8,128)S(1)}, u32[]{:S(2)}, u32[]{:S(2)}) collective-permute-start(f32[8,128]{1,0:T(8,128)S(1)} %get-tuple-element.56.refs_3_), channel_id=1, source_target_pairs={{0,2},{1,3},{2,0},{3,1},{4,6},{5,7},{6,4},{7,5},{8,10},{9,11},{10,... | collective-permute-start | bytes 12296 | tf_op jit(solution)/shard_map/ppermute | solution.py:411
  300.6 2.8 collective-permute-start.26
  (16 other events, 260.0 us)
Sparse Core Ops, SparseCore 0:
  24.3 52.8 all-gather.1

commit v4 on v3

--- a/solution.py
+++ b/solution.py
@@ -263,12 +263,20 @@
     )(*acts, *weights)
 
 
-def project_kernel(rows_ref, weight_ref, out_ref, turned):
-    @pl.when(pl.program_id(0) == 0)
-    def _():
-        turned[...] = weight_ref[...].T
-
-    columns = jnp.dot(rows_ref[...], turned[...], preferred_element_type=F32)
+def turn_kernel(weight_ref, out_ref):
+    out_ref[...] = weight_ref[...].T
+
+
+def turn(weight):
+    return pl.pallas_call(
+        turn_kernel,
+        out_shape=jax.ShapeDtypeStruct(weight.shape[::-1], weight.dtype),
+        compiler_params=pltpu.CompilerParams(vmem_limit_bytes=VMEM_BYTES),
+    )(weight)
+
+
+def project_kernel(rows_ref, weight_ref, out_ref):
+    columns = jnp.dot(rows_ref[...], weight_ref[...], preferred_element_type=F32)
     out_ref[...] = columns.reshape(out_ref.shape).astype(BF16)
 
 
@@ -282,9 +290,8 @@
             pl.BlockSpec((rows.shape[0] // steps, rows.shape[1]), lambda i: (i, 0)),
             pl.BlockSpec(weight.shape, lambda i: (0, 0)),
         ],
-        out_specs=pl.BlockSpec((owners // steps, group, weight.shape[0]), lambda i: (i, 0, 0)),
-        out_shape=jax.ShapeDtypeStruct((owners, group, weight.shape[0]), BF16),
-        scratch_shapes=[pltpu.VMEM(weight.shape[::-1], BF16)],
+        out_specs=pl.BlockSpec((owners // steps, group, weight.shape[1]), lambda i: (i, 0, 0)),
+        out_shape=jax.ShapeDtypeStruct((owners, group, weight.shape[1]), BF16),
         compiler_params=pltpu.CompilerParams(vmem_limit_bytes=VMEM_BYTES),
     )(rows, weight)
 
@@ -332,10 +339,15 @@
         summed[...] = jnp.zeros_like(summed)
         total[...] = jnp.zeros_like(total)
 
+    def score(at):
+        return jnp.dot(q_ref[at : at + block, :], keys, preferred_element_type=F32)
+
+    ahead = score(0)
     for at in range(0, rows, block):
         span = slice(at, at + block)
-        scores = jnp.dot(q_ref[span, :], keys, preferred_element_type=F32)
-        scores = jnp.where(valid, scores, -1e30)
+        scores = jnp.where(valid, ahead, -1e30)
+        if at + block < rows:
+            ahead = score(at + block)
         before = highest[span, :]
         now = jnp.maximum(before, jnp.max(scores, axis=1, keepdims=True))
         weights = jnp.exp2((scores - now) * scale)
@@ -356,7 +368,7 @@
     latent = value_up.shape[1]
     query_rows = query_block.reshape(-1, width_qk)
     rows = query_rows.shape[0]
-    chunk = 2048
+    chunk = 1024
     latent_out = pl.pallas_call(
         functools.partial(attend_kernel, score_scale * math.log2(math.e)),
         grid=(cache_block.shape[0] // chunk,),
@@ -439,8 +451,12 @@
     embed_sq = jnp.sum(notes[:, gain_rows, : depths * nodes], axis=0).reshape(depths, nodes)
     normed = embed * (1.0 / jnp.sqrt(embed_sq / width + EPS))[..., None] * embed_gain
     gains = notes[(mine - jnp.arange(tp, dtype=jnp.int32)) % tp, :gain_rows].reshape(tp, HALVES, part)
-    gathered, normed, gains, *down = lax.optimization_barrier((gathered, normed, gains, *down))
-    columns = project(gathered, out_proj.T, groups)
+    turned, heads = lax.optimization_barrier((out_proj.T, heads))
+    turned = turn(turned)
+    gathered, normed, gains, turned, *down = lax.optimization_barrier(
+        (gathered, normed, gains, turned, *down)
+    )
+    columns = project(gathered, turned, groups)
     columns = lax.all_to_all(columns, "dp", split_axis=0, concat_axis=0, tiled=True)
     attn = deal(settle(mine.reshape(1).astype(jnp.int32), columns, tp))
 

time: 317 us -> 311 us (0.981)
  local copies, waits for them, and re-layouts: 11.3 us -> 6.62 us
    unnamed x32 -> x26, local copies, waits for them, and re-layouts: 5.97 us -> 1.24 us
where the time goes in v4:
time: 311 us; the launch traced here: 310 us
  blocking collectives  98.1 us (32%)
  waiting for transfers between devices  88.3 us (28%)
  starting transfers between devices  55.2 us (18%)
  Pallas kernels  45.2 us (15%)
  between operations  14.3 us (5%)
  local copies, waits for them, and re-layouts  6.62 us (2%)
    all_to_all x3, blocking collectives, local(): lax.all_to_all(outgoing, ('dp', 'tp'), split_axis=0, concat_axis=0, tiled...  98.1 us
    ppermute x6, waiting for transfers between devices, deal(): lax.ppermute(values[k], 'tp', shifts[k])  42.8 us
    ppermute x21, starting transfers between devices, share(): lax.ppermute(value, 'tp', shifts[k])  24.3 us
    ppermute x21, waiting for transfers between devices, share(): lax.ppermute(value, 'tp', shifts[k])  18.7 us
    all_to_all x3, waiting for transfers between devices, local(): lax.all_to_all(answer, 'dp', split_axis=0, concat_axis=0, tiled=True)  16 us
    all_to_all x3, starting transfers between devices, local(): lax.all_to_all(answer, 'dp', split_axis=0, concat_axis=0, tiled=True)  15.3 us
    pallas_call x3, Pallas kernels, expert_call(): pl.pallas_call(functools.partial(expert_kernel, width), grid=(quarters,),...  13.6 us
    pallas_call x1, Pallas kernels, attend_request(): pl.pallas_call(functools.partial(attend_kernel, score_scale * math.log2(m...  12 us
  transfers between devices with their start and end apart: 32, of which 27 were waited for; matrix products, arithmetic and copies ran while one was open for 2% of the time, Pallas kernels for 0%

profile of v4, /device:TPU:1, one launch (start us, length us, event | category | flops | bytes accessed | tf_op | source)
XLA Modules:
  0.0 309.8 jit_solution(17380224031023508863)
XLA Ops:
  8.4 12.0 %shard_map.145 = bf16[768,512]{1,0:T(8,128)(2,1)S(1)} custom-call(s32[1]{0:T(128)S(6)} %copy.39.length_ref, bf16[768,576]{1,0:T(8,128)(2,1)S(1)} %bitcast.79, bf16[576,4096]{1,0:T(8,128)(2,1)} %bitcast.87), custom_call_target="tpu_custom_call" | custom-call | tf_op jit(solution)/shard_map/pallas_call | solution.py:372
  22.5 2.2 collective-permute-start
  24.7 2.6 collective-permute-start.1
  28.4 3.8 %dynamic-slice_bitcast_fusion = (bf16[256,1792]{1,0:T(8,128)(2,1)}, bf16[256,1792]{1,0:T(8,128)(2,1)}, bf16[256,1792]{1,0:T(8,128)(2,1)}, bf16[256,1792]{1,0:T(8,128)(2,1)S(1)}) fusion(bf16[1,256,7168]{2,1,0:T(8,128)(2,1)} %param.29, s32[]{:T(128)S(6)} %select_n.63, s32[]{:T(128)S(6)} %select_n.61, s32[]{:T(128)S(6)} %select_n.59, s32[]{:T(128)S(6)} %select_n.57), kind=kLoop, calls=%fused_computation.3 | loop fusion | bytes 7340048 | tf_op jit(solution)/shard_map/dynamic_slice | solution.py:435
  36.5 18.7 %collective-permute-done.3.refs_5_ = bf16[256,1792]{1,0:T(8,128)(2,1)} collective-permute-done((bf16[256,1792]{1,0:T(8,128)(2,1)}, bf16[256,1792]{1,0:T(8,128)(2,1)}, u32[]{:S(2)}, u32[]{:S(2)}) %collective-permute-start.3) | collective-permute-done | bytes 917536 | tf_op jit(solution)/shard_map/ppermute | solution.py:426
  55.2 17.3 %collective-permute-done.4.refs_6_ = bf16[256,1792]{1,0:T(8,128)(2,1)} collective-permute-done((bf16[256,1792]{1,0:T(8,128)(2,1)}, bf16[256,1792]{1,0:T(8,128)(2,1)}, u32[]{:S(2)}, u32[]{:S(2)}) %collective-permute-start.4) | collective-permute-done | bytes 917536 | tf_op jit(solution)/shard_map/ppermute | solution.py:426
  72.5 2.3 collective-permute-done.5.refs_7_
  75.3 5.4 %shard_map.147 = bf16[32,24,224]{2,1,0:T(8,128)(2,1)} custom-call(bf16[768,4096]{1,0:T(8,128)(2,1)} %all-gather.2.cloned.1.call-done.rows_ref, bf16[4096,224]{1,0:T(8,128)(2,1)S(1)} %shard_map.146.weight_ref), custom_call_target="tpu_custom_call" | custom-call | tf_op jit(solution)/shard_map/pallas_call | solution.py:286
  80.7 9.4 %all-to-all-start = ((bf16[32,24,224]{2,1,0:T(8,128)(2,1)}), bf16[32,24,224]{2,1,0:T(8,128)(2,1)S(1)}, u32[]{:S(2)}, u32[]{:S(2)}) async-start(bf16[32,24,224]{2,1,0:T(8,128)(2,1)} %shard_map.147), calls=%async_computation | async-start | bytes 786432 | tf_op jit(solution)/shard_map/all_to_all | solution.py:460
  90.2 10.2 %all-to-all-done.x_ref = bf16[32,24,224]{2,1,0:T(8,128)(2,1)S(1)} async-done(((bf16[32,24,224]{2,1,0:T(8,128)(2,1)}), bf16[32,24,224]{2,1,0:T(8,128)(2,1)S(1)}, u32[]{:S(2)}, u32[]{:S(2)}) %all-to-all-start) | async-done | bytes 344096 | tf_op jit(solution)/shard_map/all_to_all | solution.py:460
  100.8 3.3 %collective-permute-start.7 = (bf16[24,1792]{1,0:T(8,128)(2,1)S(1)}, bf16[24,1792]{1,0:T(8,128)(2,1)S(1)}, u32[]{:S(2)}, u32[]{:S(2)}) collective-permute-start(bf16[24,1792]{1,0:T(8,128)(2,1)S(1)} %get-tuple-element.39), channel_id=1, source_target_pairs={{0,2},{1,3},{2,0},{3,1},{4,6},{5,7},{6,4},{7,5},{8,10},{9,11},{10,... | collective-permute-start | bytes 258056 | tf_op jit(solution)/shard_map/ppermute | solution.py:426
  106.1 2.5 collective-permute-done.7.refs_5_
  109.4 33.5 %all_to_all.35 = bf16[128,8,896]{2,1,0:T(8,128)(2,1)S(1)} all-to-all(bf16[128,8,896]{2,1,0:T(8,128)(2,1)S(1)} %bitcast.73), channel_id=1, replica_groups=mesh['dp'=32,'tp'=4] {'dp','tp'}, dimensions={0} | all-to-all | bytes 3670016 | tf_op jit(solution)/shard_map/all_to_all | solution.py:485
  142.9 4.5 %shard_map.150.refs_0_ = bf16[128,256]{1,0:T(8,128)(2,1)S(1)} custom-call(bf16[32,4,8,896]{3,2,1,0:T(8,128)(2,1)S(1)} %bitcast.69, f32[4,2,896]{2,1,0:T(2,128)S(1)} %reshape.123.gain_ref, bf16[7168,256]{1,0:T(8,128)(2,1)S(1)} %bitcast.65, bf16[7168,256]{1,0:T(8,128)(2,1)} %bitcast.84), custom_call_target="tpu_custom_call" | custom-call | tf_op jit(solution)/shard_map/pallas_call | solution.py:214
  147.5 2.7 collective-permute-start.11
  152.1 2.4 collective-permute-done.9.refs_1_
  154.6 3.3 %shard_map.151 = bf16[256,896]{1,0:T(8,128)(2,1)} custom-call(bf16[128,256]{1,0:T(8,128)(2,1)S(1)} %shard_map.150.refs_0_, bf16[128,256]{1,0:T(8,128)(2,1)S(1)} %collective-permute-done.9.refs_1_, bf16[128,256]{1,0:T(8,128)(2,1)S(1)} %collective-permute-done.10.refs_2_, bf16[128,256]{1,0:T(8,128)(2,1)S(1)} %collective-permute-done.11.refs_3_, ...), custom_call_target="tpu_custom_call" | custom-call | tf_op jit(solution)/shard_map/pallas_call | solution.py:254
  157.9 5.5 %all-to-all-start.2 = ((bf16[32,8,896]{2,1,0:T(8,128)(2,1)}), bf16[32,8,896]{2,1,0:T(8,128)(2,1)S(1)}, u32[]{:S(2)}, u32[]{:S(2)}) async-start(bf16[32,8,896]{2,1,0:T(8,128)(2,1)} %bitcast.30), calls=%async_computation.2 | async-start | bytes 917504 | tf_op jit(solution)/shard_map/all_to_all | solution.py:490
  168.1 6.4 %all-to-all-done.2 = bf16[32,8,896]{2,1,0:T(8,128)(2,1)S(1)} async-done(((bf16[32,8,896]{2,1,0:T(8,128)(2,1)}), bf16[32,8,896]{2,1,0:T(8,128)(2,1)S(1)}, u32[]{:S(2)}, u32[]{:S(2)}) %all-to-all-start.2) | async-done | bytes 458784 | tf_op jit(solution)/shard_map/all_to_all | solution.py:490
  175.5 31.7 %all_to_all.36 = bf16[128,8,896]{2,1,0:T(8,128)(2,1)S(1)} all-to-all(bf16[128,8,896]{2,1,0:T(8,128)(2,1)S(1)} %bitcast.74), channel_id=1, replica_groups=mesh['dp'=32,'tp'=4] {'dp','tp'}, dimensions={0} | all-to-all | bytes 3670016 | tf_op jit(solution)/shard_map/all_to_all | solution.py:485
  207.2 4.5 %shard_map.153.refs_0_ = bf16[128,256]{1,0:T(8,128)(2,1)S(1)} custom-call(bf16[32,4,8,896]{3,2,1,0:T(8,128)(2,1)S(1)} %bitcast.70, f32[4,2,896]{2,1,0:T(2,128)S(1)} %reshape.123.gain_ref, bf16[7168,256]{1,0:T(8,128)(2,1)S(1)} %bitcast.66, bf16[7168,256]{1,0:T(8,128)(2,1)} %bitcast.85), custom_call_target="tpu_custom_call" | custom-call | tf_op jit(solution)/shard_map/pallas_call | solution.py:214
  214.7 2.0 collective-permute-done.15.refs_1_
  218.2 3.3 %shard_map.154 = bf16[256,896]{1,0:T(8,128)(2,1)} custom-call(bf16[128,256]{1,0:T(8,128)(2,1)S(1)} %shard_map.153.refs_0_, bf16[128,256]{1,0:T(8,128)(2,1)S(1)} %collective-permute-done.15.refs_1_, bf16[128,256]{1,0:T(8,128)(2,1)S(1)} %collective-permute-done.16.refs_2_, bf16[128,256]{1,0:T(8,128)(2,1)S(1)} %collective-permute-done.17.refs_3_, ...), custom_call_target="tpu_custom_call" | custom-call | tf_op jit(solution)/shard_map/pallas_call | solution.py:254
  221.5 4.9 %all-to-all-start.4 = ((bf16[32,8,896]{2,1,0:T(8,128)(2,1)}), bf16[32,8,896]{2,1,0:T(8,128)(2,1)S(1)}, u32[]{:S(2)}, u32[]{:S(2)}) async-start(bf16[32,8,896]{2,1,0:T(8,128)(2,1)} %bitcast.35), calls=%async_computation.4 | async-start | bytes 917504 | tf_op jit(solution)/shard_map/all_to_all | solution.py:490
  227.1 2.8 collective-permute-start.19
  232.7 4.8 %all-to-all-done.4 = bf16[32,8,896]{2,1,0:T(8,128)(2,1)S(1)} async-done(((bf16[32,8,896]{2,1,0:T(8,128)(2,1)}), bf16[32,8,896]{2,1,0:T(8,128)(2,1)S(1)}, u32[]{:S(2)}, u32[]{:S(2)}) %all-to-all-start.4) | async-done | bytes 458784 | tf_op jit(solution)/shard_map/all_to_all | solution.py:490
  238.6 32.9 %all_to_all.37 = bf16[128,8,896]{2,1,0:T(8,128)(2,1)S(1)} all-to-all(bf16[128,8,896]{2,1,0:T(8,128)(2,1)S(1)} %bitcast.72), channel_id=1, replica_groups=mesh['dp'=32,'tp'=4] {'dp','tp'}, dimensions={0} | all-to-all | bytes 3670016 | tf_op jit(solution)/shard_map/all_to_all | solution.py:485
  271.5 4.5 %shard_map.156.refs_0_ = bf16[128,256]{1,0:T(8,128)(2,1)S(1)} custom-call(bf16[32,4,8,896]{3,2,1,0:T(8,128)(2,1)S(1)} %bitcast.68, f32[4,2,896]{2,1,0:T(2,128)S(1)} %reshape.123.gain_ref, bf16[7168,256]{1,0:T(8,128)(2,1)S(1)} %bitcast.67, bf16[7168,256]{1,0:T(8,128)(2,1)} %bitcast.86), custom_call_target="tpu_custom_call" | custom-call | tf_op jit(solution)/shard_map/pallas_call | solution.py:214
  282.5 3.3 %shard_map.157 = bf16[256,896]{1,0:T(8,128)(2,1)} custom-call(bf16[128,256]{1,0:T(8,128)(2,1)S(1)} %shard_map.156.refs_0_, bf16[128,256]{1,0:T(8,128)(2,1)S(1)} %collective-permute-done.21.refs_1_, bf16[128,256]{1,0:T(8,128)(2,1)S(1)} %collective-permute-done.22.refs_2_, bf16[128,256]{1,0:T(8,128)(2,1)S(1)} %collective-permute-done.23.refs_3_, ...), custom_call_target="tpu_custom_call" | custom-call | tf_op jit(solution)/shard_map/pallas_call | solution.py:254
  285.8 4.9 %all-to-all-start.6 = ((bf16[32,8,896]{2,1,0:T(8,128)(2,1)}), bf16[32,8,896]{2,1,0:T(8,128)(2,1)S(1)}, u32[]{:S(2)}, u32[]{:S(2)}) async-start(bf16[32,8,896]{2,1,0:T(8,128)(2,1)} %bitcast.40), calls=%async_computation.6 | async-start | bytes 917504 | tf_op jit(solution)/shard_map/all_to_all | solution.py:490
  291.4 2.8 collective-permute-start.25
  297.0 4.8 %all-to-all-done.6 = bf16[32,8,896]{2,1,0:T(8,128)(2,1)S(1)} async-done(((bf16[32,8,896]{2,1,0:T(8,128)(2,1)}), bf16[32,8,896]{2,1,0:T(8,128)(2,1)S(1)}, u32[]{:S(2)}, u32[]{:S(2)}) %all-to-all-start.6) | async-done | bytes 458784 | tf_op jit(solution)/shard_map/all_to_all | solution.py:490
  (95 shorter events, 39.9 us)
Async XLA Ops:
  6.5 68.8 %all-gather.2.cloned.1.call-start = ((), (), s32[]{:S(2)}) async-start(), calls=%async_computation.7 | async-start | bytes 6488064 | tf_op jit(solution)/shard_map/all_gather | solution.py:430
  22.5 10.8 %collective-permute-start = (f32[16,128]{1,0:T(8,128)S(1)}, f32[16,128]{1,0:T(8,128)S(1)}, u32[]{:S(2)}, u32[]{:S(2)}) collective-permute-start(f32[16,128]{1,0:T(8,128)S(1)} %select_maximum_fusion), channel_id=1, source_target_pairs={{0,1},{1,2},{2,3},{3,0},{4,5},{5,6},{6,7},{7,4},{8,9},{9,10},{10,1... | collective-permute-start | bytes 24584 | tf_op jit(solution)/shard_map/ppermute | solution.py:423
  24.7 10.9 %collective-permute-start.1 = (f32[16,128]{1,0:T(8,128)S(1)}, f32[16,128]{1,0:T(8,128)S(1)}, u32[]{:S(2)}, u32[]{:S(2)}) collective-permute-start(f32[16,128]{1,0:T(8,128)S(1)} %select_maximum_fusion), channel_id=1, source_target_pairs={{0,2},{1,3},{2,0},{3,1},{4,6},{5,7},{6,4},{7,5},{8,10},{9,11},{10,... | collective-permute-start | bytes 24584 | tf_op jit(solution)/shard_map/ppermute | solution.py:423
  27.3 8.3 %collective-permute-start.2 = (f32[16,128]{1,0:T(8,128)S(1)}, f32[16,128]{1,0:T(8,128)S(1)}, u32[]{:S(2)}, u32[]{:S(2)}) collective-permute-start(f32[16,128]{1,0:T(8,128)S(1)} %select_maximum_fusion), channel_id=1, source_target_pairs={{0,3},{1,0},{2,1},{3,2},{4,7},{5,4},{6,5},{7,6},{8,11},{9,8},{10,9... | collective-permute-start | bytes 24584 | tf_op jit(solution)/shard_map/ppermute | solution.py:423
  32.1 23.1 %collective-permute-start.3 = (bf16[256,1792]{1,0:T(8,128)(2,1)}, bf16[256,1792]{1,0:T(8,128)(2,1)}, u32[]{:S(2)}, u32[]{:S(2)}) collective-permute-start(bf16[256,1792]{1,0:T(8,128)(2,1)} %get-tuple-element.61), channel_id=1, source_target_pairs={{0,1},{1,2},{2,3},{3,0},{4,5},{5,6},{6,7},{7,4},{8,9},{9,10},{10,1... | collective-permute-start | bytes 2752520 | tf_op jit(solution)/shard_map/ppermute | solution.py:426
  32.5 40.0 %collective-permute-start.4 = (bf16[256,1792]{1,0:T(8,128)(2,1)}, bf16[256,1792]{1,0:T(8,128)(2,1)}, u32[]{:S(2)}, u32[]{:S(2)}) collective-permute-start(bf16[256,1792]{1,0:T(8,128)(2,1)} %get-tuple-element.60), channel_id=1, source_target_pairs={{0,2},{1,3},{2,0},{3,1},{4,6},{5,7},{6,4},{7,5},{8,10},{9,11},{10,... | collective-permute-start | bytes 2752520 | tf_op jit(solution)/shard_map/ppermute | solution.py:426
  33.3 41.5 %collective-permute-start.5 = (bf16[256,1792]{1,0:T(8,128)(2,1)}, bf16[256,1792]{1,0:T(8,128)(2,1)}, u32[]{:S(2)}, u32[]{:S(2)}) collective-permute-start(bf16[256,1792]{1,0:T(8,128)(2,1)} %get-tuple-element.59), channel_id=1, source_target_pairs={{0,3},{1,0},{2,1},{3,2},{4,7},{5,4},{6,5},{7,6},{8,11},{9,8},{10,9... | collective-permute-start | bytes 2752520 | tf_op jit(solution)/shard_map/ppermute | solution.py:426
  80.7 19.7 %all-to-all-start = ((bf16[32,24,224]{2,1,0:T(8,128)(2,1)}), bf16[32,24,224]{2,1,0:T(8,128)(2,1)S(1)}, u32[]{:S(2)}, u32[]{:S(2)}) async-start(bf16[32,24,224]{2,1,0:T(8,128)(2,1)} %shard_map.147), calls=%async_computation | async-start | bytes 786432 | tf_op jit(solution)/shard_map/all_to_all | solution.py:460
  100.7 5.5 %collective-permute-start.6 = (bf16[24,1792]{1,0:T(8,128)(2,1)S(1)}, bf16[24,1792]{1,0:T(8,128)(2,1)S(1)}, u32[]{:S(2)}, u32[]{:S(2)}) collective-permute-start(bf16[24,1792]{1,0:T(8,128)(2,1)S(1)} %get-tuple-element.38), channel_id=1, source_target_pairs={{0,1},{1,2},{2,3},{3,0},{4,5},{5,6},{6,7},{7,4},{8,9},{9,10},{10,1... | collective-permute-start | bytes 258056 | tf_op jit(solution)/shard_map/ppermute | solution.py:426
  100.8 7.9 %collective-permute-start.7 = (bf16[24,1792]{1,0:T(8,128)(2,1)S(1)}, bf16[24,1792]{1,0:T(8,128)(2,1)S(1)}, u32[]{:S(2)}, u32[]{:S(2)}) collective-permute-start(bf16[24,1792]{1,0:T(8,128)(2,1)S(1)} %get-tuple-element.39), channel_id=1, source_target_pairs={{0,2},{1,3},{2,0},{3,1},{4,6},{5,7},{6,4},{7,5},{8,10},{9,11},{10,... | collective-permute-start | bytes 258056 | tf_op jit(solution)/shard_map/ppermute | solution.py:426
  104.1 4.6 %collective-permute-start.8 = (bf16[24,1792]{1,0:T(8,128)(2,1)S(1)}, bf16[24,1792]{1,0:T(8,128)(2,1)S(1)}, u32[]{:S(2)}, u32[]{:S(2)}) collective-permute-start(bf16[24,1792]{1,0:T(8,128)(2,1)S(1)} %get-tuple-element.40), channel_id=1, source_target_pairs={{0,3},{1,0},{2,1},{3,2},{4,7},{5,4},{6,5},{7,6},{8,11},{9,8},{10,9... | collective-permute-start | bytes 258056 | tf_op jit(solution)/shard_map/ppermute | solution.py:426
  147.4 4.7 %collective-permute-start.10 = (bf16[128,256]{1,0:T(8,128)(2,1)S(1)}, bf16[128,256]{1,0:T(8,128)(2,1)S(1)}, u32[]{:S(2)}, u32[]{:S(2)}) collective-permute-start(bf16[128,256]{1,0:T(8,128)(2,1)S(1)} %shard_map.150.refs_0_), channel_id=1, source_target_pairs={{0,2},{1,3},{2,0},{3,1},{4,6},{5,7},{6,4},{7,5},{8,10},{9,11},{10,... | collective-permute-start | bytes 196616 | tf_op jit(solution)/shard_map/ppermute | solution.py:423
  147.5 4.6 %collective-permute-start.11 = (bf16[128,256]{1,0:T(8,128)(2,1)S(1)}, bf16[128,256]{1,0:T(8,128)(2,1)S(1)}, u32[]{:S(2)}, u32[]{:S(2)}) collective-permute-start(bf16[128,256]{1,0:T(8,128)(2,1)S(1)} %shard_map.150.refs_0_), channel_id=1, source_target_pairs={{0,3},{1,0},{2,1},{3,2},{4,7},{5,4},{6,5},{7,6},{8,11},{9,8},{10,9... | collective-permute-start | bytes 196616 | tf_op jit(solution)/shard_map/ppermute | solution.py:423
  150.3 4.3 %collective-permute-start.9 = (bf16[128,256]{1,0:T(8,128)(2,1)S(1)}, bf16[128,256]{1,0:T(8,128)(2,1)S(1)}, u32[]{:S(2)}, u32[]{:S(2)}) collective-permute-start(bf16[128,256]{1,0:T(8,128)(2,1)S(1)} %shard_map.150.refs_0_), channel_id=1, source_target_pairs={{0,1},{1,2},{2,3},{3,0},{4,5},{5,6},{6,7},{7,4},{8,9},{9,10},{10,1... | collective-permute-start | bytes 196616 | tf_op jit(solution)/shard_map/ppermute | solution.py:423
  157.9 16.6 %all-to-all-start.2 = ((bf16[32,8,896]{2,1,0:T(8,128)(2,1)}), bf16[32,8,896]{2,1,0:T(8,128)(2,1)S(1)}, u32[]{:S(2)}, u32[]{:S(2)}) async-start(bf16[32,8,896]{2,1,0:T(8,128)(2,1)} %bitcast.30), calls=%async_computation.2 | async-start | bytes 917504 | tf_op jit(solution)/shard_map/all_to_all | solution.py:490
  163.4 4.0 %collective-permute-start.12 = (f32[8,128]{1,0:T(8,128)S(1)}, f32[8,128]{1,0:T(8,128)S(1)}, u32[]{:S(2)}, u32[]{:S(2)}) collective-permute-start(f32[8,128]{1,0:T(8,128)S(1)} %get-tuple-element.48.refs_3_), channel_id=1, source_target_pairs={{0,1},{1,2},{2,3},{3,0},{4,5},{5,6},{6,7},{7,4},{8,9},{9,10},{10,1... | collective-permute-start | bytes 12296 | tf_op jit(solution)/shard_map/ppermute | solution.py:423
  163.5 4.3 %collective-permute-start.13 = (f32[8,128]{1,0:T(8,128)S(1)}, f32[8,128]{1,0:T(8,128)S(1)}, u32[]{:S(2)}, u32[]{:S(2)}) collective-permute-start(f32[8,128]{1,0:T(8,128)S(1)} %get-tuple-element.48.refs_3_), channel_id=1, source_target_pairs={{0,2},{1,3},{2,0},{3,1},{4,6},{5,7},{6,4},{7,5},{8,10},{9,11},{10,... | collective-permute-start | bytes 12296 | tf_op jit(solution)/shard_map/ppermute | solution.py:423
  164.4 3.7 %collective-permute-start.14 = (f32[8,128]{1,0:T(8,128)S(1)}, f32[8,128]{1,0:T(8,128)S(1)}, u32[]{:S(2)}, u32[]{:S(2)}) collective-permute-start(f32[8,128]{1,0:T(8,128)S(1)} %get-tuple-element.48.refs_3_), channel_id=1, source_target_pairs={{0,3},{1,0},{2,1},{3,2},{4,7},{5,4},{6,5},{7,6},{8,11},{9,8},{10,9... | collective-permute-start | bytes 12296 | tf_op jit(solution)/shard_map/ppermute | solution.py:423
  211.8 4.9 %collective-permute-start.15 = (bf16[128,256]{1,0:T(8,128)(2,1)S(1)}, bf16[128,256]{1,0:T(8,128)(2,1)S(1)}, u32[]{:S(2)}, u32[]{:S(2)}) collective-permute-start(bf16[128,256]{1,0:T(8,128)(2,1)S(1)} %shard_map.153.refs_0_), channel_id=1, source_target_pairs={{0,1},{1,2},{2,3},{3,0},{4,5},{5,6},{6,7},{7,4},{8,9},{9,10},{10,1... | collective-permute-start | bytes 196616 | tf_op jit(solution)/shard_map/ppermute | solution.py:423
  212.2 5.6 %collective-permute-start.16 = (bf16[128,256]{1,0:T(8,128)(2,1)S(1)}, bf16[128,256]{1,0:T(8,128)(2,1)S(1)}, u32[]{:S(2)}, u32[]{:S(2)}) collective-permute-start(bf16[128,256]{1,0:T(8,128)(2,1)S(1)} %shard_map.153.refs_0_), channel_id=1, source_target_pairs={{0,2},{1,3},{2,0},{3,1},{4,6},{5,7},{6,4},{7,5},{8,10},{9,11},{10,... | collective-permute-start | bytes 196616 | tf_op jit(solution)/shard_map/ppermute | solution.py:423
  213.1 5.1 %collective-permute-start.17 = (bf16[128,256]{1,0:T(8,128)(2,1)S(1)}, bf16[128,256]{1,0:T(8,128)(2,1)S(1)}, u32[]{:S(2)}, u32[]{:S(2)}) collective-permute-start(bf16[128,256]{1,0:T(8,128)(2,1)S(1)} %shard_map.153.refs_0_), channel_id=1, source_target_pairs={{0,3},{1,0},{2,1},{3,2},{4,7},{5,4},{6,5},{7,6},{8,11},{9,8},{10,9... | collective-permute-start | bytes 196616 | tf_op jit(solution)/shard_map/ppermute | solution.py:423
  221.5 16.0 %all-to-all-start.4 = ((bf16[32,8,896]{2,1,0:T(8,128)(2,1)}), bf16[32,8,896]{2,1,0:T(8,128)(2,1)S(1)}, u32[]{:S(2)}, u32[]{:S(2)}) async-start(bf16[32,8,896]{2,1,0:T(8,128)(2,1)} %bitcast.35), calls=%async_computation.4 | async-start | bytes 917504 | tf_op jit(solution)/shard_map/all_to_all | solution.py:490
  226.5 4.0 %collective-permute-start.18 = (f32[8,128]{1,0:T(8,128)S(1)}, f32[8,128]{1,0:T(8,128)S(1)}, u32[]{:S(2)}, u32[]{:S(2)}) collective-permute-start(f32[8,128]{1,0:T(8,128)S(1)} %get-tuple-element.54.refs_3_), channel_id=1, source_target_pairs={{0,1},{1,2},{2,3},{3,0},{4,5},{5,6},{6,7},{7,4},{8,9},{9,10},{10,1... | collective-permute-start | bytes 12296 | tf_op jit(solution)/shard_map/ppermute | solution.py:423
  227.1 4.0 %collective-permute-start.19 = (f32[8,128]{1,0:T(8,128)S(1)}, f32[8,128]{1,0:T(8,128)S(1)}, u32[]{:S(2)}, u32[]{:S(2)}) collective-permute-start(f32[8,128]{1,0:T(8,128)S(1)} %get-tuple-element.54.refs_3_), channel_id=1, source_target_pairs={{0,2},{1,3},{2,0},{3,1},{4,6},{5,7},{6,4},{7,5},{8,10},{9,11},{10,... | collective-permute-start | bytes 12296 | tf_op jit(solution)/shard_map/ppermute | solution.py:423
  230.0 2.8 collective-permute-start.20
  276.1 4.9 %collective-permute-start.21 = (bf16[128,256]{1,0:T(8,128)(2,1)S(1)}, bf16[128,256]{1,0:T(8,128)(2,1)S(1)}, u32[]{:S(2)}, u32[]{:S(2)}) collective-permute-start(bf16[128,256]{1,0:T(8,128)(2,1)S(1)} %shard_map.156.refs_0_), channel_id=1, source_target_pairs={{0,1},{1,2},{2,3},{3,0},{4,5},{5,6},{6,7},{7,4},{8,9},{9,10},{10,1... | collective-permute-start | bytes 196616 | tf_op jit(solution)/shard_map/ppermute | solution.py:423
  276.5 5.6 %collective-permute-start.22 = (bf16[128,256]{1,0:T(8,128)(2,1)S(1)}, bf16[128,256]{1,0:T(8,128)(2,1)S(1)}, u32[]{:S(2)}, u32[]{:S(2)}) collective-permute-start(bf16[128,256]{1,0:T(8,128)(2,1)S(1)} %shard_map.156.refs_0_), channel_id=1, source_target_pairs={{0,2},{1,3},{2,0},{3,1},{4,6},{5,7},{6,4},{7,5},{8,10},{9,11},{10,... | collective-permute-start | bytes 196616 | tf_op jit(solution)/shard_map/ppermute | solution.py:423
  277.4 5.1 %collective-permute-start.23 = (bf16[128,256]{1,0:T(8,128)(2,1)S(1)}, bf16[128,256]{1,0:T(8,128)(2,1)S(1)}, u32[]{:S(2)}, u32[]{:S(2)}) collective-permute-start(bf16[128,256]{1,0:T(8,128)(2,1)S(1)} %shard_map.156.refs_0_), channel_id=1, source_target_pairs={{0,3},{1,0},{2,1},{3,2},{4,7},{5,4},{6,5},{7,6},{8,11},{9,8},{10,9... | collective-permute-start | bytes 196616 | tf_op jit(solution)/shard_map/ppermute | solution.py:423
  285.8 16.0 %all-to-all-start.6 = ((bf16[32,8,896]{2,1,0:T(8,128)(2,1)}), bf16[32,8,896]{2,1,0:T(8,128)(2,1)S(1)}, u32[]{:S(2)}, u32[]{:S(2)}) async-start(bf16[32,8,896]{2,1,0:T(8,128)(2,1)} %bitcast.40), calls=%async_computation.6 | async-start | bytes 917504 | tf_op jit(solution)/shard_map/all_to_all | solution.py:490
  290.7 4.0 %collective-permute-start.24 = (f32[8,128]{1,0:T(8,128)S(1)}, f32[8,128]{1,0:T(8,128)S(1)}, u32[]{:S(2)}, u32[]{:S(2)}) collective-permute-start(f32[8,128]{1,0:T(8,128)S(1)} %get-tuple-element.58.refs_3_), channel_id=1, source_target_pairs={{0,1},{1,2},{2,3},{3,0},{4,5},{5,6},{6,7},{7,4},{8,9},{9,10},{10,1... | collective-permute-start | bytes 12296 | tf_op jit(solution)/shard_map/ppermute | solution.py:423
  291.4 4.0 %collective-permute-start.25 = (f32[8,128]{1,0:T(8,128)S(1)}, f32[8,128]{1,0:T(8,128)S(1)}, u32[]{:S(2)}, u32[]{:S(2)}) collective-permute-start(f32[8,128]{1,0:T(8,128)S(1)} %get-tuple-element.58.refs_3_), channel_id=1, source_target_pairs={{0,2},{1,3},{2,0},{3,1},{4,6},{5,7},{6,4},{7,5},{8,10},{9,11},{10,... | collective-permute-start | bytes 12296 | tf_op jit(solution)/shard_map/ppermute | solution.py:423
  294.2 2.8 collective-permute-start.26
  (13 other events, 247.6 us)
Sparse Core Ops, SparseCore 0:
  22.4 52.8 all-gather.1

commit v5 on v4

--- a/solution.py
+++ b/solution.py
@@ -177,7 +177,7 @@
 
 def expert_kernel(width, x_ref, gain_ref, gate_ref, up_ref, act_ref, pack, square, total):
     step = pl.program_id(0)
-    sources, _, group, part = x_ref.shape
+    sources, quarters, group, part = x_ref.shape
     rows = sources * group
     per_half = rows // HALVES
     hidden = gate_ref.shape[1]
@@ -188,16 +188,20 @@
         square[...] = jnp.zeros_like(square)
         total[...] = jnp.zeros_like(total)
 
-    mixed = x_ref[:, step].astype(F32).reshape(rows, part).astype(BF16)
-    packed = jnp.dot(pack[...], mixed, preferred_element_type=F32)
-    gain = gain_ref[step]
-    for h in range(HALVES):
-        piece = packed[h * per_half : (h + 1) * per_half]
-        square[...] += jnp.sum(piece * piece, axis=1, keepdims=True)
-        piece = (piece * gain[h : h + 1, :]).astype(BF16)
-        span = slice(h * part, (h + 1) * part)
-        total[:, :hidden] += jnp.dot(piece, gate_ref[span, :], preferred_element_type=F32)
-        total[:, hidden:] += jnp.dot(piece, up_ref[span, :], preferred_element_type=F32)
+    each = quarters // 2
+    for turn_index in range(each):
+        at = step * each + turn_index
+        mixed = x_ref[:, at].astype(F32).reshape(rows, part).astype(BF16)
+        packed = jnp.dot(pack[...], mixed, preferred_element_type=F32)
+        gain = gain_ref[at]
+        for h in range(HALVES):
+            piece = packed[h * per_half : (h + 1) * per_half]
+            square[...] += jnp.sum(piece * piece, axis=1, keepdims=True)
+            piece = (piece * gain[h : h + 1, :]).astype(BF16)
+            start = (turn_index * HALVES + h) * part
+            span = slice(start, start + part)
+            total[:, :hidden] += jnp.dot(piece, gate_ref[span, :], preferred_element_type=F32)
+            total[:, hidden:] += jnp.dot(piece, up_ref[span, :], preferred_element_type=F32)
 
     @pl.when(step == pl.num_programs(0) - 1)
     def _():
@@ -210,10 +214,10 @@
     sources, quarters, group, part = x.shape
     rows = sources * group
     hidden = gate.shape[1]
-    block = gate.shape[0] // quarters
+    block = gate.shape[0] // 2
     return pl.pallas_call(
         functools.partial(expert_kernel, width),
-        grid=(quarters,),
+        grid=(2,),
         in_specs=[
             pl.BlockSpec(x.shape, lambda i: (0, 0, 0, 0)),
             pl.BlockSpec(gain.shape, lambda i: (0, 0, 0)),

time: 311 us -> 308 us (level)
  no operation moved by 1% of the time
where the time goes in v5:
time: 308 us
  blocking collectives  98.1 us (32%)
  waiting for transfers between devices  88.3 us (29%)
  starting transfers between devices  55.2 us (18%)
  Pallas kernels  43 us (14%)
  between operations  14.3 us (5%)
  local copies, waits for them, and re-layouts  6.62 us (2%)
    all_to_all x3, blocking collectives, local(): lax.all_to_all(outgoing, ('dp', 'tp'), split_axis=0, concat_axis=0, tiled...  98.1 us
    ppermute x6, waiting for transfers between devices, deal(): lax.ppermute(values[k], 'tp', shifts[k])  42.8 us
    ppermute x21, starting transfers between devices, share(): lax.ppermute(value, 'tp', shifts[k])  24.3 us
    ppermute x21, waiting for transfers between devices, share(): lax.ppermute(value, 'tp', shifts[k])  18.7 us
    all_to_all x3, waiting for transfers between devices, local(): lax.all_to_all(answer, 'dp', split_axis=0, concat_axis=0, tiled=True)  16 us
    all_to_all x3, starting transfers between devices, local(): lax.all_to_all(answer, 'dp', split_axis=0, concat_axis=0, tiled=True)  15.3 us
    pallas_call x1, Pallas kernels, attend_request(): pl.pallas_call(functools.partial(attend_kernel, score_scale * math.log2(m...  12 us
    pallas_call x3, Pallas kernels, expert_call(): pl.pallas_call(functools.partial(expert_kernel, width), grid=(2,), in_spe...  11.5 us
  transfers between devices with their start and end apart: 32, of which 27 were waited for; matrix products, arithmetic and copies ran while one was open for 2% of the time, Pallas kernels for 0%

profile of v5, /device:TPU:1, one launch (start us, length us, event | category | flops | bytes accessed | tf_op | source)
XLA Modules:
  0.0 307.7 jit_solution(4190614134726434169)
XLA Ops:
  8.4 12.0 %shard_map.145 = bf16[768,512]{1,0:T(8,128)(2,1)S(1)} custom-call(s32[1]{0:T(128)S(6)} %copy.39.length_ref, bf16[768,576]{1,0:T(8,128)(2,1)S(1)} %bitcast.79, bf16[576,4096]{1,0:T(8,128)(2,1)} %bitcast.87), custom_call_target="tpu_custom_call" | custom-call | tf_op jit(solution)/shard_map/pallas_call | solution.py:376
  22.5 2.2 collective-permute-start
  24.7 2.6 collective-permute-start.1
  28.4 3.8 %dynamic-slice_bitcast_fusion = (bf16[256,1792]{1,0:T(8,128)(2,1)}, bf16[256,1792]{1,0:T(8,128)(2,1)}, bf16[256,1792]{1,0:T(8,128)(2,1)}, bf16[256,1792]{1,0:T(8,128)(2,1)S(1)}) fusion(bf16[1,256,7168]{2,1,0:T(8,128)(2,1)} %param.29, s32[]{:T(128)S(6)} %select_n.63, s32[]{:T(128)S(6)} %select_n.61, s32[]{:T(128)S(6)} %select_n.59, s32[]{:T(128)S(6)} %select_n.57), kind=kLoop, calls=%fused_computation.3 | loop fusion | bytes 7340048 | tf_op jit(solution)/shard_map/dynamic_slice | solution.py:439
  36.5 18.7 %collective-permute-done.3.refs_5_ = bf16[256,1792]{1,0:T(8,128)(2,1)} collective-permute-done((bf16[256,1792]{1,0:T(8,128)(2,1)}, bf16[256,1792]{1,0:T(8,128)(2,1)}, u32[]{:S(2)}, u32[]{:S(2)}) %collective-permute-start.3) | collective-permute-done | bytes 917536 | tf_op jit(solution)/shard_map/ppermute | solution.py:430
  55.2 17.3 %collective-permute-done.4.refs_6_ = bf16[256,1792]{1,0:T(8,128)(2,1)} collective-permute-done((bf16[256,1792]{1,0:T(8,128)(2,1)}, bf16[256,1792]{1,0:T(8,128)(2,1)}, u32[]{:S(2)}, u32[]{:S(2)}) %collective-permute-start.4) | collective-permute-done | bytes 917536 | tf_op jit(solution)/shard_map/ppermute | solution.py:430
  72.5 2.3 collective-permute-done.5.refs_7_
  75.3 5.4 %shard_map.147 = bf16[32,24,224]{2,1,0:T(8,128)(2,1)} custom-call(bf16[768,4096]{1,0:T(8,128)(2,1)} %all-gather.2.cloned.1.call-done.rows_ref, bf16[4096,224]{1,0:T(8,128)(2,1)S(1)} %shard_map.146.weight_ref), custom_call_target="tpu_custom_call" | custom-call | tf_op jit(solution)/shard_map/pallas_call | solution.py:290
  80.7 9.4 %all-to-all-start = ((bf16[32,24,224]{2,1,0:T(8,128)(2,1)}), bf16[32,24,224]{2,1,0:T(8,128)(2,1)S(1)}, u32[]{:S(2)}, u32[]{:S(2)}) async-start(bf16[32,24,224]{2,1,0:T(8,128)(2,1)} %shard_map.147), calls=%async_computation | async-start | bytes 786432 | tf_op jit(solution)/shard_map/all_to_all | solution.py:464
  90.2 10.2 %all-to-all-done.x_ref = bf16[32,24,224]{2,1,0:T(8,128)(2,1)S(1)} async-done(((bf16[32,24,224]{2,1,0:T(8,128)(2,1)}), bf16[32,24,224]{2,1,0:T(8,128)(2,1)S(1)}, u32[]{:S(2)}, u32[]{:S(2)}) %all-to-all-start) | async-done | bytes 344096 | tf_op jit(solution)/shard_map/all_to_all | solution.py:464
  100.8 3.3 %collective-permute-start.7 = (bf16[24,1792]{1,0:T(8,128)(2,1)S(1)}, bf16[24,1792]{1,0:T(8,128)(2,1)S(1)}, u32[]{:S(2)}, u32[]{:S(2)}) collective-permute-start(bf16[24,1792]{1,0:T(8,128)(2,1)S(1)} %get-tuple-element.39), channel_id=1, source_target_pairs={{0,2},{1,3},{2,0},{3,1},{4,6},{5,7},{6,4},{7,5},{8,10},{9,11},{10,... | collective-permute-start | bytes 258056 | tf_op jit(solution)/shard_map/ppermute | solution.py:430
  106.1 2.5 collective-permute-done.7.refs_5_
  109.4 33.5 %all_to_all.35 = bf16[128,8,896]{2,1,0:T(8,128)(2,1)S(1)} all-to-all(bf16[128,8,896]{2,1,0:T(8,128)(2,1)S(1)} %bitcast.73), channel_id=1, replica_groups=mesh['dp'=32,'tp'=4] {'dp','tp'}, dimensions={0} | all-to-all | bytes 3670016 | tf_op jit(solution)/shard_map/all_to_all | solution.py:489
  142.9 3.8 %shard_map.150.refs_0_ = bf16[128,256]{1,0:T(8,128)(2,1)S(1)} custom-call(bf16[32,4,8,896]{3,2,1,0:T(8,128)(2,1)S(1)} %bitcast.69, f32[4,2,896]{2,1,0:T(2,128)S(1)} %reshape.123.gain_ref, bf16[7168,256]{1,0:T(8,128)(2,1)S(1)} %bitcast.65, bf16[7168,256]{1,0:T(8,128)(2,1)} %bitcast.84), custom_call_target="tpu_custom_call" | custom-call | tf_op jit(solution)/shard_map/pallas_call | solution.py:218
  146.8 2.7 collective-permute-start.11
  151.4 2.4 collective-permute-done.9.refs_1_
  153.9 3.3 %shard_map.151 = bf16[256,896]{1,0:T(8,128)(2,1)} custom-call(bf16[128,256]{1,0:T(8,128)(2,1)S(1)} %shard_map.150.refs_0_, bf16[128,256]{1,0:T(8,128)(2,1)S(1)} %collective-permute-done.9.refs_1_, bf16[128,256]{1,0:T(8,128)(2,1)S(1)} %collective-permute-done.10.refs_2_, bf16[128,256]{1,0:T(8,128)(2,1)S(1)} %collective-permute-done.11.refs_3_, ...), custom_call_target="tpu_custom_call" | custom-call | tf_op jit(solution)/shard_map/pallas_call | solution.py:258
  157.2 5.5 %all-to-all-start.2 = ((bf16[32,8,896]{2,1,0:T(8,128)(2,1)}), bf16[32,8,896]{2,1,0:T(8,128)(2,1)S(1)}, u32[]{:S(2)}, u32[]{:S(2)}) async-start(bf16[32,8,896]{2,1,0:T(8,128)(2,1)} %bitcast.30), calls=%async_computation.2 | async-start | bytes 917504 | tf_op jit(solution)/shard_map/all_to_all | solution.py:494
  167.4 6.4 %all-to-all-done.2 = bf16[32,8,896]{2,1,0:T(8,128)(2,1)S(1)} async-done(((bf16[32,8,896]{2,1,0:T(8,128)(2,1)}), bf16[32,8,896]{2,1,0:T(8,128)(2,1)S(1)}, u32[]{:S(2)}, u32[]{:S(2)}) %all-to-all-start.2) | async-done | bytes 458784 | tf_op jit(solution)/shard_map/all_to_all | solution.py:494
  174.8 31.7 %all_to_all.36 = bf16[128,8,896]{2,1,0:T(8,128)(2,1)S(1)} all-to-all(bf16[128,8,896]{2,1,0:T(8,128)(2,1)S(1)} %bitcast.74), channel_id=1, replica_groups=mesh['dp'=32,'tp'=4] {'dp','tp'}, dimensions={0} | all-to-all | bytes 3670016 | tf_op jit(solution)/shard_map/all_to_all | solution.py:489
  206.5 3.8 %shard_map.153.refs_0_ = bf16[128,256]{1,0:T(8,128)(2,1)S(1)} custom-call(bf16[32,4,8,896]{3,2,1,0:T(8,128)(2,1)S(1)} %bitcast.70, f32[4,2,896]{2,1,0:T(2,128)S(1)} %reshape.123.gain_ref, bf16[7168,256]{1,0:T(8,128)(2,1)S(1)} %bitcast.66, bf16[7168,256]{1,0:T(8,128)(2,1)} %bitcast.85), custom_call_target="tpu_custom_call" | custom-call | tf_op jit(solution)/shard_map/pallas_call | solution.py:218
  216.8 3.3 %shard_map.154 = bf16[256,896]{1,0:T(8,128)(2,1)} custom-call(bf16[128,256]{1,0:T(8,128)(2,1)S(1)} %shard_map.153.refs_0_, bf16[128,256]{1,0:T(8,128)(2,1)S(1)} %collective-permute-done.15.refs_1_, bf16[128,256]{1,0:T(8,128)(2,1)S(1)} %collective-permute-done.16.refs_2_, bf16[128,256]{1,0:T(8,128)(2,1)S(1)} %collective-permute-done.17.refs_3_, ...), custom_call_target="tpu_custom_call" | custom-call | tf_op jit(solution)/shard_map/pallas_call | solution.py:258
  220.1 4.9 %all-to-all-start.4 = ((bf16[32,8,896]{2,1,0:T(8,128)(2,1)}), bf16[32,8,896]{2,1,0:T(8,128)(2,1)S(1)}, u32[]{:S(2)}, u32[]{:S(2)}) async-start(bf16[32,8,896]{2,1,0:T(8,128)(2,1)} %bitcast.35), calls=%async_computation.4 | async-start | bytes 917504 | tf_op jit(solution)/shard_map/all_to_all | solution.py:494
  225.7 2.8 collective-permute-start.19
  231.3 4.8 %all-to-all-done.4 = bf16[32,8,896]{2,1,0:T(8,128)(2,1)S(1)} async-done(((bf16[32,8,896]{2,1,0:T(8,128)(2,1)}), bf16[32,8,896]{2,1,0:T(8,128)(2,1)S(1)}, u32[]{:S(2)}, u32[]{:S(2)}) %all-to-all-start.4) | async-done | bytes 458784 | tf_op jit(solution)/shard_map/all_to_all | solution.py:494
  237.1 32.9 %all_to_all.37 = bf16[128,8,896]{2,1,0:T(8,128)(2,1)S(1)} all-to-all(bf16[128,8,896]{2,1,0:T(8,128)(2,1)S(1)} %bitcast.72), channel_id=1, replica_groups=mesh['dp'=32,'tp'=4] {'dp','tp'}, dimensions={0} | all-to-all | bytes 3670016 | tf_op jit(solution)/shard_map/all_to_all | solution.py:489
  270.1 3.8 %shard_map.156.refs_0_ = bf16[128,256]{1,0:T(8,128)(2,1)S(1)} custom-call(bf16[32,4,8,896]{3,2,1,0:T(8,128)(2,1)S(1)} %bitcast.68, f32[4,2,896]{2,1,0:T(2,128)S(1)} %reshape.123.gain_ref, bf16[7168,256]{1,0:T(8,128)(2,1)S(1)} %bitcast.67, bf16[7168,256]{1,0:T(8,128)(2,1)} %bitcast.86), custom_call_target="tpu_custom_call" | custom-call | tf_op jit(solution)/shard_map/pallas_call | solution.py:218
  276.8 2.0 collective-permute-done.21.refs_1_
  280.3 3.3 %shard_map.157 = bf16[256,896]{1,0:T(8,128)(2,1)} custom-call(bf16[128,256]{1,0:T(8,128)(2,1)S(1)} %shard_map.156.refs_0_, bf16[128,256]{1,0:T(8,128)(2,1)S(1)} %collective-permute-done.21.refs_1_, bf16[128,256]{1,0:T(8,128)(2,1)S(1)} %collective-permute-done.22.refs_2_, bf16[128,256]{1,0:T(8,128)(2,1)S(1)} %collective-permute-done.23.refs_3_, ...), custom_call_target="tpu_custom_call" | custom-call | tf_op jit(solution)/shard_map/pallas_call | solution.py:258
  283.7 4.9 %all-to-all-start.6 = ((bf16[32,8,896]{2,1,0:T(8,128)(2,1)}), bf16[32,8,896]{2,1,0:T(8,128)(2,1)S(1)}, u32[]{:S(2)}, u32[]{:S(2)}) async-start(bf16[32,8,896]{2,1,0:T(8,128)(2,1)} %bitcast.40), calls=%async_computation.6 | async-start | bytes 917504 | tf_op jit(solution)/shard_map/all_to_all | solution.py:494
  289.3 2.8 collective-permute-start.25
  294.9 4.8 %all-to-all-done.6 = bf16[32,8,896]{2,1,0:T(8,128)(2,1)S(1)} async-done(((bf16[32,8,896]{2,1,0:T(8,128)(2,1)}), bf16[32,8,896]{2,1,0:T(8,128)(2,1)S(1)}, u32[]{:S(2)}, u32[]{:S(2)}) %all-to-all-start.6) | async-done | bytes 458784 | tf_op jit(solution)/shard_map/all_to_all | solution.py:494
  (95 shorter events, 39.9 us)
Async XLA Ops:
  6.5 68.8 %all-gather.2.cloned.1.call-start = ((), (), s32[]{:S(2)}) async-start(), calls=%async_computation.7 | async-start | bytes 6488064 | tf_op jit(solution)/shard_map/all_gather | solution.py:434
  22.5 10.8 %collective-permute-start = (f32[16,128]{1,0:T(8,128)S(1)}, f32[16,128]{1,0:T(8,128)S(1)}, u32[]{:S(2)}, u32[]{:S(2)}) collective-permute-start(f32[16,128]{1,0:T(8,128)S(1)} %select_maximum_fusion), channel_id=1, source_target_pairs={{0,1},{1,2},{2,3},{3,0},{4,5},{5,6},{6,7},{7,4},{8,9},{9,10},{10,1... | collective-permute-start | bytes 24584 | tf_op jit(solution)/shard_map/ppermute | solution.py:427
  24.7 10.9 %collective-permute-start.1 = (f32[16,128]{1,0:T(8,128)S(1)}, f32[16,128]{1,0:T(8,128)S(1)}, u32[]{:S(2)}, u32[]{:S(2)}) collective-permute-start(f32[16,128]{1,0:T(8,128)S(1)} %select_maximum_fusion), channel_id=1, source_target_pairs={{0,2},{1,3},{2,0},{3,1},{4,6},{5,7},{6,4},{7,5},{8,10},{9,11},{10,... | collective-permute-start | bytes 24584 | tf_op jit(solution)/shard_map/ppermute | solution.py:427
  27.3 8.3 %collective-permute-start.2 = (f32[16,128]{1,0:T(8,128)S(1)}, f32[16,128]{1,0:T(8,128)S(1)}, u32[]{:S(2)}, u32[]{:S(2)}) collective-permute-start(f32[16,128]{1,0:T(8,128)S(1)} %select_maximum_fusion), channel_id=1, source_target_pairs={{0,3},{1,0},{2,1},{3,2},{4,7},{5,4},{6,5},{7,6},{8,11},{9,8},{10,9... | collective-permute-start | bytes 24584 | tf_op jit(solution)/shard_map/ppermute | solution.py:427
  32.1 23.1 %collective-permute-start.3 = (bf16[256,1792]{1,0:T(8,128)(2,1)}, bf16[256,1792]{1,0:T(8,128)(2,1)}, u32[]{:S(2)}, u32[]{:S(2)}) collective-permute-start(bf16[256,1792]{1,0:T(8,128)(2,1)} %get-tuple-element.61), channel_id=1, source_target_pairs={{0,1},{1,2},{2,3},{3,0},{4,5},{5,6},{6,7},{7,4},{8,9},{9,10},{10,1... | collective-permute-start | bytes 2752520 | tf_op jit(solution)/shard_map/ppermute | solution.py:430
  32.5 40.0 %collective-permute-start.4 = (bf16[256,1792]{1,0:T(8,128)(2,1)}, bf16[256,1792]{1,0:T(8,128)(2,1)}, u32[]{:S(2)}, u32[]{:S(2)}) collective-permute-start(bf16[256,1792]{1,0:T(8,128)(2,1)} %get-tuple-element.60), channel_id=1, source_target_pairs={{0,2},{1,3},{2,0},{3,1},{4,6},{5,7},{6,4},{7,5},{8,10},{9,11},{10,... | collective-permute-start | bytes 2752520 | tf_op jit(solution)/shard_map/ppermute | solution.py:430
  33.3 41.5 %collective-permute-start.5 = (bf16[256,1792]{1,0:T(8,128)(2,1)}, bf16[256,1792]{1,0:T(8,128)(2,1)}, u32[]{:S(2)}, u32[]{:S(2)}) collective-permute-start(bf16[256,1792]{1,0:T(8,128)(2,1)} %get-tuple-element.59), channel_id=1, source_target_pairs={{0,3},{1,0},{2,1},{3,2},{4,7},{5,4},{6,5},{7,6},{8,11},{9,8},{10,9... | collective-permute-start | bytes 2752520 | tf_op jit(solution)/shard_map/ppermute | solution.py:430
  80.7 19.7 %all-to-all-start = ((bf16[32,24,224]{2,1,0:T(8,128)(2,1)}), bf16[32,24,224]{2,1,0:T(8,128)(2,1)S(1)}, u32[]{:S(2)}, u32[]{:S(2)}) async-start(bf16[32,24,224]{2,1,0:T(8,128)(2,1)} %shard_map.147), calls=%async_computation | async-start | bytes 786432 | tf_op jit(solution)/shard_map/all_to_all | solution.py:464
  100.7 5.5 %collective-permute-start.6 = (bf16[24,1792]{1,0:T(8,128)(2,1)S(1)}, bf16[24,1792]{1,0:T(8,128)(2,1)S(1)}, u32[]{:S(2)}, u32[]{:S(2)}) collective-permute-start(bf16[24,1792]{1,0:T(8,128)(2,1)S(1)} %get-tuple-element.38), channel_id=1, source_target_pairs={{0,1},{1,2},{2,3},{3,0},{4,5},{5,6},{6,7},{7,4},{8,9},{9,10},{10,1... | collective-permute-start | bytes 258056 | tf_op jit(solution)/shard_map/ppermute | solution.py:430
  100.8 7.9 %collective-permute-start.7 = (bf16[24,1792]{1,0:T(8,128)(2,1)S(1)}, bf16[24,1792]{1,0:T(8,128)(2,1)S(1)}, u32[]{:S(2)}, u32[]{:S(2)}) collective-permute-start(bf16[24,1792]{1,0:T(8,128)(2,1)S(1)} %get-tuple-element.39), channel_id=1, source_target_pairs={{0,2},{1,3},{2,0},{3,1},{4,6},{5,7},{6,4},{7,5},{8,10},{9,11},{10,... | collective-permute-start | bytes 258056 | tf_op jit(solution)/shard_map/ppermute | solution.py:430
  104.1 4.6 %collective-permute-start.8 = (bf16[24,1792]{1,0:T(8,128)(2,1)S(1)}, bf16[24,1792]{1,0:T(8,128)(2,1)S(1)}, u32[]{:S(2)}, u32[]{:S(2)}) collective-permute-start(bf16[24,1792]{1,0:T(8,128)(2,1)S(1)} %get-tuple-element.40), channel_id=1, source_target_pairs={{0,3},{1,0},{2,1},{3,2},{4,7},{5,4},{6,5},{7,6},{8,11},{9,8},{10,9... | collective-permute-start | bytes 258056 | tf_op jit(solution)/shard_map/ppermute | solution.py:430
  146.7 4.7 %collective-permute-start.10 = (bf16[128,256]{1,0:T(8,128)(2,1)S(1)}, bf16[128,256]{1,0:T(8,128)(2,1)S(1)}, u32[]{:S(2)}, u32[]{:S(2)}) collective-permute-start(bf16[128,256]{1,0:T(8,128)(2,1)S(1)} %shard_map.150.refs_0_), channel_id=1, source_target_pairs={{0,2},{1,3},{2,0},{3,1},{4,6},{5,7},{6,4},{7,5},{8,10},{9,11},{10,... | collective-permute-start | bytes 196616 | tf_op jit(solution)/shard_map/ppermute | solution.py:427
  146.8 4.6 %collective-permute-start.11 = (bf16[128,256]{1,0:T(8,128)(2,1)S(1)}, bf16[128,256]{1,0:T(8,128)(2,1)S(1)}, u32[]{:S(2)}, u32[]{:S(2)}) collective-permute-start(bf16[128,256]{1,0:T(8,128)(2,1)S(1)} %shard_map.150.refs_0_), channel_id=1, source_target_pairs={{0,3},{1,0},{2,1},{3,2},{4,7},{5,4},{6,5},{7,6},{8,11},{9,8},{10,9... | collective-permute-start | bytes 196616 | tf_op jit(solution)/shard_map/ppermute | solution.py:427
  149.6 4.3 %collective-permute-start.9 = (bf16[128,256]{1,0:T(8,128)(2,1)S(1)}, bf16[128,256]{1,0:T(8,128)(2,1)S(1)}, u32[]{:S(2)}, u32[]{:S(2)}) collective-permute-start(bf16[128,256]{1,0:T(8,128)(2,1)S(1)} %shard_map.150.refs_0_), channel_id=1, source_target_pairs={{0,1},{1,2},{2,3},{3,0},{4,5},{5,6},{6,7},{7,4},{8,9},{9,10},{10,1... | collective-permute-start | bytes 196616 | tf_op jit(solution)/shard_map/ppermute | solution.py:427
  157.2 16.6 %all-to-all-start.2 = ((bf16[32,8,896]{2,1,0:T(8,128)(2,1)}), bf16[32,8,896]{2,1,0:T(8,128)(2,1)S(1)}, u32[]{:S(2)}, u32[]{:S(2)}) async-start(bf16[32,8,896]{2,1,0:T(8,128)(2,1)} %bitcast.30), calls=%async_computation.2 | async-start | bytes 917504 | tf_op jit(solution)/shard_map/all_to_all | solution.py:494
  162.7 4.0 %collective-permute-start.12 = (f32[8,128]{1,0:T(8,128)S(1)}, f32[8,128]{1,0:T(8,128)S(1)}, u32[]{:S(2)}, u32[]{:S(2)}) collective-permute-start(f32[8,128]{1,0:T(8,128)S(1)} %get-tuple-element.48.refs_3_), channel_id=1, source_target_pairs={{0,1},{1,2},{2,3},{3,0},{4,5},{5,6},{6,7},{7,4},{8,9},{9,10},{10,1... | collective-permute-start | bytes 12296 | tf_op jit(solution)/shard_map/ppermute | solution.py:427
  162.8 4.3 %collective-permute-start.13 = (f32[8,128]{1,0:T(8,128)S(1)}, f32[8,128]{1,0:T(8,128)S(1)}, u32[]{:S(2)}, u32[]{:S(2)}) collective-permute-start(f32[8,128]{1,0:T(8,128)S(1)} %get-tuple-element.48.refs_3_), channel_id=1, source_target_pairs={{0,2},{1,3},{2,0},{3,1},{4,6},{5,7},{6,4},{7,5},{8,10},{9,11},{10,... | collective-permute-start | bytes 12296 | tf_op jit(solution)/shard_map/ppermute | solution.py:427
  163.7 3.7 %collective-permute-start.14 = (f32[8,128]{1,0:T(8,128)S(1)}, f32[8,128]{1,0:T(8,128)S(1)}, u32[]{:S(2)}, u32[]{:S(2)}) collective-permute-start(f32[8,128]{1,0:T(8,128)S(1)} %get-tuple-element.48.refs_3_), channel_id=1, source_target_pairs={{0,3},{1,0},{2,1},{3,2},{4,7},{5,4},{6,5},{7,6},{8,11},{9,8},{10,9... | collective-permute-start | bytes 12296 | tf_op jit(solution)/shard_map/ppermute | solution.py:427
  210.4 4.9 %collective-permute-start.15 = (bf16[128,256]{1,0:T(8,128)(2,1)S(1)}, bf16[128,256]{1,0:T(8,128)(2,1)S(1)}, u32[]{:S(2)}, u32[]{:S(2)}) collective-permute-start(bf16[128,256]{1,0:T(8,128)(2,1)S(1)} %shard_map.153.refs_0_), channel_id=1, source_target_pairs={{0,1},{1,2},{2,3},{3,0},{4,5},{5,6},{6,7},{7,4},{8,9},{9,10},{10,1... | collective-permute-start | bytes 196616 | tf_op jit(solution)/shard_map/ppermute | solution.py:427
  210.8 5.6 %collective-permute-start.16 = (bf16[128,256]{1,0:T(8,128)(2,1)S(1)}, bf16[128,256]{1,0:T(8,128)(2,1)S(1)}, u32[]{:S(2)}, u32[]{:S(2)}) collective-permute-start(bf16[128,256]{1,0:T(8,128)(2,1)S(1)} %shard_map.153.refs_0_), channel_id=1, source_target_pairs={{0,2},{1,3},{2,0},{3,1},{4,6},{5,7},{6,4},{7,5},{8,10},{9,11},{10,... | collective-permute-start | bytes 196616 | tf_op jit(solution)/shard_map/ppermute | solution.py:427
  211.7 5.1 %collective-permute-start.17 = (bf16[128,256]{1,0:T(8,128)(2,1)S(1)}, bf16[128,256]{1,0:T(8,128)(2,1)S(1)}, u32[]{:S(2)}, u32[]{:S(2)}) collective-permute-start(bf16[128,256]{1,0:T(8,128)(2,1)S(1)} %shard_map.153.refs_0_), channel_id=1, source_target_pairs={{0,3},{1,0},{2,1},{3,2},{4,7},{5,4},{6,5},{7,6},{8,11},{9,8},{10,9... | collective-permute-start | bytes 196616 | tf_op jit(solution)/shard_map/ppermute | solution.py:427
  220.1 16.0 %all-to-all-start.4 = ((bf16[32,8,896]{2,1,0:T(8,128)(2,1)}), bf16[32,8,896]{2,1,0:T(8,128)(2,1)S(1)}, u32[]{:S(2)}, u32[]{:S(2)}) async-start(bf16[32,8,896]{2,1,0:T(8,128)(2,1)} %bitcast.35), calls=%async_computation.4 | async-start | bytes 917504 | tf_op jit(solution)/shard_map/all_to_all | solution.py:494
  225.0 4.0 %collective-permute-start.18 = (f32[8,128]{1,0:T(8,128)S(1)}, f32[8,128]{1,0:T(8,128)S(1)}, u32[]{:S(2)}, u32[]{:S(2)}) collective-permute-start(f32[8,128]{1,0:T(8,128)S(1)} %get-tuple-element.54.refs_3_), channel_id=1, source_target_pairs={{0,1},{1,2},{2,3},{3,0},{4,5},{5,6},{6,7},{7,4},{8,9},{9,10},{10,1... | collective-permute-start | bytes 12296 | tf_op jit(solution)/shard_map/ppermute | solution.py:427
  225.7 4.0 %collective-permute-start.19 = (f32[8,128]{1,0:T(8,128)S(1)}, f32[8,128]{1,0:T(8,128)S(1)}, u32[]{:S(2)}, u32[]{:S(2)}) collective-permute-start(f32[8,128]{1,0:T(8,128)S(1)} %get-tuple-element.54.refs_3_), channel_id=1, source_target_pairs={{0,2},{1,3},{2,0},{3,1},{4,6},{5,7},{6,4},{7,5},{8,10},{9,11},{10,... | collective-permute-start | bytes 12296 | tf_op jit(solution)/shard_map/ppermute | solution.py:427
  228.5 2.8 collective-permute-start.20
  273.9 4.9 %collective-permute-start.21 = (bf16[128,256]{1,0:T(8,128)(2,1)S(1)}, bf16[128,256]{1,0:T(8,128)(2,1)S(1)}, u32[]{:S(2)}, u32[]{:S(2)}) collective-permute-start(bf16[128,256]{1,0:T(8,128)(2,1)S(1)} %shard_map.156.refs_0_), channel_id=1, source_target_pairs={{0,1},{1,2},{2,3},{3,0},{4,5},{5,6},{6,7},{7,4},{8,9},{9,10},{10,1... | collective-permute-start | bytes 196616 | tf_op jit(solution)/shard_map/ppermute | solution.py:427
  274.4 5.6 %collective-permute-start.22 = (bf16[128,256]{1,0:T(8,128)(2,1)S(1)}, bf16[128,256]{1,0:T(8,128)(2,1)S(1)}, u32[]{:S(2)}, u32[]{:S(2)}) collective-permute-start(bf16[128,256]{1,0:T(8,128)(2,1)S(1)} %shard_map.156.refs_0_), channel_id=1, source_target_pairs={{0,2},{1,3},{2,0},{3,1},{4,6},{5,7},{6,4},{7,5},{8,10},{9,11},{10,... | collective-permute-start | bytes 196616 | tf_op jit(solution)/shard_map/ppermute | solution.py:427
  275.3 5.1 %collective-permute-start.23 = (bf16[128,256]{1,0:T(8,128)(2,1)S(1)}, bf16[128,256]{1,0:T(8,128)(2,1)S(1)}, u32[]{:S(2)}, u32[]{:S(2)}) collective-permute-start(bf16[128,256]{1,0:T(8,128)(2,1)S(1)} %shard_map.156.refs_0_), channel_id=1, source_target_pairs={{0,3},{1,0},{2,1},{3,2},{4,7},{5,4},{6,5},{7,6},{8,11},{9,8},{10,9... | collective-permute-start | bytes 196616 | tf_op jit(solution)/shard_map/ppermute | solution.py:427
  283.7 16.0 %all-to-all-start.6 = ((bf16[32,8,896]{2,1,0:T(8,128)(2,1)}), bf16[32,8,896]{2,1,0:T(8,128)(2,1)S(1)}, u32[]{:S(2)}, u32[]{:S(2)}) async-start(bf16[32,8,896]{2,1,0:T(8,128)(2,1)} %bitcast.40), calls=%async_computation.6 | async-start | bytes 917504 | tf_op jit(solution)/shard_map/all_to_all | solution.py:494
  288.6 4.0 %collective-permute-start.24 = (f32[8,128]{1,0:T(8,128)S(1)}, f32[8,128]{1,0:T(8,128)S(1)}, u32[]{:S(2)}, u32[]{:S(2)}) collective-permute-start(f32[8,128]{1,0:T(8,128)S(1)} %get-tuple-element.58.refs_3_), channel_id=1, source_target_pairs={{0,1},{1,2},{2,3},{3,0},{4,5},{5,6},{6,7},{7,4},{8,9},{9,10},{10,1... | collective-permute-start | bytes 12296 | tf_op jit(solution)/shard_map/ppermute | solution.py:427
  289.3 4.0 %collective-permute-start.25 = (f32[8,128]{1,0:T(8,128)S(1)}, f32[8,128]{1,0:T(8,128)S(1)}, u32[]{:S(2)}, u32[]{:S(2)}) collective-permute-start(f32[8,128]{1,0:T(8,128)S(1)} %get-tuple-element.58.refs_3_), channel_id=1, source_target_pairs={{0,2},{1,3},{2,0},{3,1},{4,6},{5,7},{6,4},{7,5},{8,10},{9,11},{10,... | collective-permute-start | bytes 12296 | tf_op jit(solution)/shard_map/ppermute | solution.py:427
  292.1 2.8 collective-permute-start.26
  (13 other events, 247.6 us)
Sparse Core Ops, SparseCore 0:
  22.4 52.8 all-gather.1

commit v6 on v5

--- a/solution.py
+++ b/solution.py
@@ -236,33 +236,24 @@
 
 
 def down_kernel(count, *refs):
-    acts, weights, out_ref, stacked = refs[:count], refs[count : 2 * count], *refs[2 * count :]
-    step = pl.program_id(0)
+    acts, weights, out_ref = refs[:count], refs[count : 2 * count], refs[2 * count]
     total = jnp.dot(acts[0][...], weights[0][...], preferred_element_type=F32)
     for index in range(1, count):
         total = total + jnp.dot(acts[index][...], weights[index][...], preferred_element_type=F32)
-    stacked[step] = total.astype(BF16)
-
-    @pl.when(step == HALVES - 1)
-    def _():
-        rows, part = out_ref.shape
-        unpack = pack_matrix(rows, False)
-        value = stacked[...].reshape(rows, part)
-        out_ref[...] = jnp.dot(unpack, value, preferred_element_type=F32).astype(BF16)
+    part = total.shape[1] // HALVES
+    stacked = jnp.concatenate(
+        [total[:, h * part : (h + 1) * part] for h in range(HALVES)], axis=0
+    ).astype(BF16)
+    unpack = pack_matrix(stacked.shape[0], False)
+    out_ref[...] = jnp.dot(unpack, stacked, preferred_element_type=F32).astype(BF16)
 
 
 def down_call(acts, weights):
     rows = acts[0].shape[0]
-    hidden, quarter = weights[0].shape
-    part = quarter // HALVES
+    quarter = weights[0].shape[1]
     return pl.pallas_call(
         functools.partial(down_kernel, len(acts)),
-        grid=(HALVES,),
-        in_specs=[pl.BlockSpec(acts[0].shape, lambda i: (0, 0)) for _ in acts]
-        + [pl.BlockSpec((hidden, part), lambda i: (0, i)) for _ in weights],
-        out_specs=pl.BlockSpec((rows * HALVES, part), lambda i: (0, 0)),
-        out_shape=jax.ShapeDtypeStruct((rows * HALVES, part), BF16),
-        scratch_shapes=[pltpu.VMEM((HALVES, rows, part), BF16)],
+        out_shape=jax.ShapeDtypeStruct((rows * HALVES, quarter // HALVES), BF16),
         compiler_params=pltpu.CompilerParams(vmem_limit_bytes=VMEM_BYTES),
     )(*acts, *weights)
 
@@ -285,7 +276,7 @@
 
 
 def project(rows, weight, owners):
-    steps = 4
+    steps = 2
     group = rows.shape[0] // owners
     return pl.pallas_call(
         project_kernel,

time: 308 us -> 308 us (level)
  no operation moved by 1% of the time
where the time goes in v6:
time: 308 us
  blocking collectives  98.1 us (32%)
  waiting for transfers between devices  88.3 us (29%)
  starting transfers between devices  55.3 us (18%)
  Pallas kernels  42.7 us (14%)
  between operations  14.3 us (5%)
  local copies, waits for them, and re-layouts  6.62 us (2%)
    all_to_all x3, blocking collectives, local(): lax.all_to_all(outgoing, ('dp', 'tp'), split_axis=0, concat_axis=0, tiled...  98.1 us
    ppermute x6, waiting for transfers between devices, deal(): lax.ppermute(values[k], 'tp', shifts[k])  42.8 us
    ppermute x21, starting transfers between devices, share(): lax.ppermute(value, 'tp', shifts[k])  24.5 us
    ppermute x21, waiting for transfers between devices, share(): lax.ppermute(value, 'tp', shifts[k])  18.7 us
    all_to_all x3, waiting for transfers between devices, local(): lax.all_to_all(answer, 'dp', split_axis=0, concat_axis=0, tiled=True)  16 us
    all_to_all x3, starting transfers between devices, local(): lax.all_to_all(answer, 'dp', split_axis=0, concat_axis=0, tiled=True)  15.3 us
    pallas_call x1, Pallas kernels, attend_request(): pl.pallas_call(functools.partial(attend_kernel, score_scale * math.log2(m...  12 us
    pallas_call x3, Pallas kernels, expert_call(): pl.pallas_call(functools.partial(expert_kernel, width), grid=(2,), in_spe...  11.5 us
  transfers between devices with their start and end apart: 32, of which 27 were waited for; matrix products, arithmetic and copies ran while one was open for 2% of the time, Pallas kernels for 0%

profile of v6, /device:TPU:1, one launch (start us, length us, event | category | flops | bytes accessed | tf_op | source)
XLA Modules:
  0.0 307.5 jit_solution(6702936047855357800)
XLA Ops:
  8.4 12.0 %shard_map.145 = bf16[768,512]{1,0:T(8,128)(2,1)S(1)} custom-call(s32[1]{0:T(128)S(6)} %copy.39.length_ref, bf16[768,576]{1,0:T(8,128)(2,1)S(1)} %bitcast.79, bf16[576,4096]{1,0:T(8,128)(2,1)} %bitcast.87), custom_call_target="tpu_custom_call" | custom-call | tf_op jit(solution)/shard_map/pallas_call | solution.py:367
  22.5 2.2 collective-permute-start
  24.7 2.6 collective-permute-start.1
  28.4 3.8 %dynamic-slice_bitcast_fusion = (bf16[256,1792]{1,0:T(8,128)(2,1)}, bf16[256,1792]{1,0:T(8,128)(2,1)}, bf16[256,1792]{1,0:T(8,128)(2,1)}, bf16[256,1792]{1,0:T(8,128)(2,1)S(1)}) fusion(bf16[1,256,7168]{2,1,0:T(8,128)(2,1)} %param.29, s32[]{:T(128)S(6)} %select_n.63, s32[]{:T(128)S(6)} %select_n.61, s32[]{:T(128)S(6)} %select_n.59, s32[]{:T(128)S(6)} %select_n.57), kind=kLoop, calls=%fused_computation.3 | loop fusion | bytes 7340048 | tf_op jit(solution)/shard_map/dynamic_slice | solution.py:430
  36.5 18.7 %collective-permute-done.3.refs_5_ = bf16[256,1792]{1,0:T(8,128)(2,1)} collective-permute-done((bf16[256,1792]{1,0:T(8,128)(2,1)}, bf16[256,1792]{1,0:T(8,128)(2,1)}, u32[]{:S(2)}, u32[]{:S(2)}) %collective-permute-start.3) | collective-permute-done | bytes 917536 | tf_op jit(solution)/shard_map/ppermute | solution.py:421
  55.2 17.3 %collective-permute-done.4.refs_6_ = bf16[256,1792]{1,0:T(8,128)(2,1)} collective-permute-done((bf16[256,1792]{1,0:T(8,128)(2,1)}, bf16[256,1792]{1,0:T(8,128)(2,1)}, u32[]{:S(2)}, u32[]{:S(2)}) %collective-permute-start.4) | collective-permute-done | bytes 917536 | tf_op jit(solution)/shard_map/ppermute | solution.py:421
  72.5 2.3 collective-permute-done.5.refs_7_
  75.3 4.6 %shard_map.147 = bf16[32,24,224]{2,1,0:T(8,128)(2,1)} custom-call(bf16[768,4096]{1,0:T(8,128)(2,1)} %all-gather.2.cloned.1.call-done.rows_ref, bf16[4096,224]{1,0:T(8,128)(2,1)S(1)} %shard_map.146.weight_ref), custom_call_target="tpu_custom_call" | custom-call | tf_op jit(solution)/shard_map/pallas_call | solution.py:281
  79.9 9.4 %all-to-all-start = ((bf16[32,24,224]{2,1,0:T(8,128)(2,1)}), bf16[32,24,224]{2,1,0:T(8,128)(2,1)S(1)}, u32[]{:S(2)}, u32[]{:S(2)}) async-start(bf16[32,24,224]{2,1,0:T(8,128)(2,1)} %shard_map.147), calls=%async_computation | async-start | bytes 786432 | tf_op jit(solution)/shard_map/all_to_all | solution.py:455
  89.4 10.2 %all-to-all-done.x_ref = bf16[32,24,224]{2,1,0:T(8,128)(2,1)S(1)} async-done(((bf16[32,24,224]{2,1,0:T(8,128)(2,1)}), bf16[32,24,224]{2,1,0:T(8,128)(2,1)S(1)}, u32[]{:S(2)}, u32[]{:S(2)}) %all-to-all-start) | async-done | bytes 344096 | tf_op jit(solution)/shard_map/all_to_all | solution.py:455
  99.9 3.3 %collective-permute-start.7 = (bf16[24,1792]{1,0:T(8,128)(2,1)S(1)}, bf16[24,1792]{1,0:T(8,128)(2,1)S(1)}, u32[]{:S(2)}, u32[]{:S(2)}) collective-permute-start(bf16[24,1792]{1,0:T(8,128)(2,1)S(1)} %get-tuple-element.39), channel_id=1, source_target_pairs={{0,2},{1,3},{2,0},{3,1},{4,6},{5,7},{6,4},{7,5},{8,10},{9,11},{10,... | collective-permute-start | bytes 258056 | tf_op jit(solution)/shard_map/ppermute | solution.py:421
  105.3 2.5 collective-permute-done.7.refs_5_
  108.5 33.5 %all_to_all.35 = bf16[128,8,896]{2,1,0:T(8,128)(2,1)S(1)} all-to-all(bf16[128,8,896]{2,1,0:T(8,128)(2,1)S(1)} %bitcast.73), channel_id=1, replica_groups=mesh['dp'=32,'tp'=4] {'dp','tp'}, dimensions={0} | all-to-all | bytes 3670016 | tf_op jit(solution)/shard_map/all_to_all | solution.py:480
  142.0 3.8 %shard_map.150.refs_0_ = bf16[128,256]{1,0:T(8,128)(2,1)S(1)} custom-call(bf16[32,4,8,896]{3,2,1,0:T(8,128)(2,1)S(1)} %bitcast.69, f32[4,2,896]{2,1,0:T(2,128)S(1)} %reshape.123.gain_ref, bf16[7168,256]{1,0:T(8,128)(2,1)S(1)} %bitcast.65, bf16[7168,256]{1,0:T(8,128)(2,1)} %bitcast.84), custom_call_target="tpu_custom_call" | custom-call | tf_op jit(solution)/shard_map/pallas_call | solution.py:218
  146.1 2.7 collective-permute-start.11
  150.8 2.4 collective-permute-done.9.refs_1_
  153.2 3.5 %shard_map.151 = bf16[256,896]{1,0:T(8,128)(2,1)} custom-call(bf16[128,256]{1,0:T(8,128)(2,1)S(1)} %shard_map.150.refs_0_, bf16[128,256]{1,0:T(8,128)(2,1)S(1)} %collective-permute-done.9.refs_1_, bf16[128,256]{1,0:T(8,128)(2,1)S(1)} %collective-permute-done.10.refs_2_, bf16[128,256]{1,0:T(8,128)(2,1)S(1)} %collective-permute-done.11.refs_3_, ...), custom_call_target="tpu_custom_call" | custom-call | tf_op jit(solution)/shard_map/pallas_call | solution.py:254
  156.7 5.5 %all-to-all-start.2 = ((bf16[32,8,896]{2,1,0:T(8,128)(2,1)}), bf16[32,8,896]{2,1,0:T(8,128)(2,1)S(1)}, u32[]{:S(2)}, u32[]{:S(2)}) async-start(bf16[32,8,896]{2,1,0:T(8,128)(2,1)} %bitcast.30), calls=%async_computation.2 | async-start | bytes 917504 | tf_op jit(solution)/shard_map/all_to_all | solution.py:485
  166.9 6.4 %all-to-all-done.2 = bf16[32,8,896]{2,1,0:T(8,128)(2,1)S(1)} async-done(((bf16[32,8,896]{2,1,0:T(8,128)(2,1)}), bf16[32,8,896]{2,1,0:T(8,128)(2,1)S(1)}, u32[]{:S(2)}, u32[]{:S(2)}) %all-to-all-start.2) | async-done | bytes 458784 | tf_op jit(solution)/shard_map/all_to_all | solution.py:485
  174.3 31.7 %all_to_all.36 = bf16[128,8,896]{2,1,0:T(8,128)(2,1)S(1)} all-to-all(bf16[128,8,896]{2,1,0:T(8,128)(2,1)S(1)} %bitcast.74), channel_id=1, replica_groups=mesh['dp'=32,'tp'=4] {'dp','tp'}, dimensions={0} | all-to-all | bytes 3670016 | tf_op jit(solution)/shard_map/all_to_all | solution.py:480
  206.0 3.8 %shard_map.153.refs_0_ = bf16[128,256]{1,0:T(8,128)(2,1)S(1)} custom-call(bf16[32,4,8,896]{3,2,1,0:T(8,128)(2,1)S(1)} %bitcast.70, f32[4,2,896]{2,1,0:T(2,128)S(1)} %reshape.123.gain_ref, bf16[7168,256]{1,0:T(8,128)(2,1)S(1)} %bitcast.66, bf16[7168,256]{1,0:T(8,128)(2,1)} %bitcast.85), custom_call_target="tpu_custom_call" | custom-call | tf_op jit(solution)/shard_map/pallas_call | solution.py:218
  212.8 2.0 collective-permute-done.15.refs_1_
  216.3 3.5 %shard_map.154 = bf16[256,896]{1,0:T(8,128)(2,1)} custom-call(bf16[128,256]{1,0:T(8,128)(2,1)S(1)} %shard_map.153.refs_0_, bf16[128,256]{1,0:T(8,128)(2,1)S(1)} %collective-permute-done.15.refs_1_, bf16[128,256]{1,0:T(8,128)(2,1)S(1)} %collective-permute-done.16.refs_2_, bf16[128,256]{1,0:T(8,128)(2,1)S(1)} %collective-permute-done.17.refs_3_, ...), custom_call_target="tpu_custom_call" | custom-call | tf_op jit(solution)/shard_map/pallas_call | solution.py:254
  219.8 4.9 %all-to-all-start.4 = ((bf16[32,8,896]{2,1,0:T(8,128)(2,1)}), bf16[32,8,896]{2,1,0:T(8,128)(2,1)S(1)}, u32[]{:S(2)}, u32[]{:S(2)}) async-start(bf16[32,8,896]{2,1,0:T(8,128)(2,1)} %bitcast.35), calls=%async_computation.4 | async-start | bytes 917504 | tf_op jit(solution)/shard_map/all_to_all | solution.py:485
  225.4 2.8 collective-permute-start.19
  231.0 4.8 %all-to-all-done.4 = bf16[32,8,896]{2,1,0:T(8,128)(2,1)S(1)} async-done(((bf16[32,8,896]{2,1,0:T(8,128)(2,1)}), bf16[32,8,896]{2,1,0:T(8,128)(2,1)S(1)}, u32[]{:S(2)}, u32[]{:S(2)}) %all-to-all-start.4) | async-done | bytes 458784 | tf_op jit(solution)/shard_map/all_to_all | solution.py:485
  236.8 32.9 %all_to_all.37 = bf16[128,8,896]{2,1,0:T(8,128)(2,1)S(1)} all-to-all(bf16[128,8,896]{2,1,0:T(8,128)(2,1)S(1)} %bitcast.72), channel_id=1, replica_groups=mesh['dp'=32,'tp'=4] {'dp','tp'}, dimensions={0} | all-to-all | bytes 3670016 | tf_op jit(solution)/shard_map/all_to_all | solution.py:480
  269.8 3.8 %shard_map.156.refs_0_ = bf16[128,256]{1,0:T(8,128)(2,1)S(1)} custom-call(bf16[32,4,8,896]{3,2,1,0:T(8,128)(2,1)S(1)} %bitcast.68, f32[4,2,896]{2,1,0:T(2,128)S(1)} %reshape.123.gain_ref, bf16[7168,256]{1,0:T(8,128)(2,1)S(1)} %bitcast.67, bf16[7168,256]{1,0:T(8,128)(2,1)} %bitcast.86), custom_call_target="tpu_custom_call" | custom-call | tf_op jit(solution)/shard_map/pallas_call | solution.py:218
  280.0 3.5 %shard_map.157 = bf16[256,896]{1,0:T(8,128)(2,1)} custom-call(bf16[128,256]{1,0:T(8,128)(2,1)S(1)} %shard_map.156.refs_0_, bf16[128,256]{1,0:T(8,128)(2,1)S(1)} %collective-permute-done.21.refs_1_, bf16[128,256]{1,0:T(8,128)(2,1)S(1)} %collective-permute-done.22.refs_2_, bf16[128,256]{1,0:T(8,128)(2,1)S(1)} %collective-permute-done.23.refs_3_, ...), custom_call_target="tpu_custom_call" | custom-call | tf_op jit(solution)/shard_map/pallas_call | solution.py:254
  283.6 4.9 %all-to-all-start.6 = ((bf16[32,8,896]{2,1,0:T(8,128)(2,1)}), bf16[32,8,896]{2,1,0:T(8,128)(2,1)S(1)}, u32[]{:S(2)}, u32[]{:S(2)}) async-start(bf16[32,8,896]{2,1,0:T(8,128)(2,1)} %bitcast.40), calls=%async_computation.6 | async-start | bytes 917504 | tf_op jit(solution)/shard_map/all_to_all | solution.py:485
  289.2 2.8 collective-permute-start.25
  294.7 4.8 %all-to-all-done.6 = bf16[32,8,896]{2,1,0:T(8,128)(2,1)S(1)} async-done(((bf16[32,8,896]{2,1,0:T(8,128)(2,1)}), bf16[32,8,896]{2,1,0:T(8,128)(2,1)S(1)}, u32[]{:S(2)}, u32[]{:S(2)}) %all-to-all-start.6) | async-done | bytes 458784 | tf_op jit(solution)/shard_map/all_to_all | solution.py:485
  (95 shorter events, 40.1 us)
Async XLA Ops:
  6.5 68.8 %all-gather.2.cloned.1.call-start = ((), (), s32[]{:S(2)}) async-start(), calls=%async_computation.7 | async-start | bytes 6488064 | tf_op jit(solution)/shard_map/all_gather | solution.py:425
  22.5 10.8 %collective-permute-start = (f32[16,128]{1,0:T(8,128)S(1)}, f32[16,128]{1,0:T(8,128)S(1)}, u32[]{:S(2)}, u32[]{:S(2)}) collective-permute-start(f32[16,128]{1,0:T(8,128)S(1)} %select_maximum_fusion), channel_id=1, source_target_pairs={{0,1},{1,2},{2,3},{3,0},{4,5},{5,6},{6,7},{7,4},{8,9},{9,10},{10,1... | collective-permute-start | bytes 24584 | tf_op jit(solution)/shard_map/ppermute | solution.py:418
  24.7 10.9 %collective-permute-start.1 = (f32[16,128]{1,0:T(8,128)S(1)}, f32[16,128]{1,0:T(8,128)S(1)}, u32[]{:S(2)}, u32[]{:S(2)}) collective-permute-start(f32[16,128]{1,0:T(8,128)S(1)} %select_maximum_fusion), channel_id=1, source_target_pairs={{0,2},{1,3},{2,0},{3,1},{4,6},{5,7},{6,4},{7,5},{8,10},{9,11},{10,... | collective-permute-start | bytes 24584 | tf_op jit(solution)/shard_map/ppermute | solution.py:418
  27.3 8.3 %collective-permute-start.2 = (f32[16,128]{1,0:T(8,128)S(1)}, f32[16,128]{1,0:T(8,128)S(1)}, u32[]{:S(2)}, u32[]{:S(2)}) collective-permute-start(f32[16,128]{1,0:T(8,128)S(1)} %select_maximum_fusion), channel_id=1, source_target_pairs={{0,3},{1,0},{2,1},{3,2},{4,7},{5,4},{6,5},{7,6},{8,11},{9,8},{10,9... | collective-permute-start | bytes 24584 | tf_op jit(solution)/shard_map/ppermute | solution.py:418
  32.1 23.1 %collective-permute-start.3 = (bf16[256,1792]{1,0:T(8,128)(2,1)}, bf16[256,1792]{1,0:T(8,128)(2,1)}, u32[]{:S(2)}, u32[]{:S(2)}) collective-permute-start(bf16[256,1792]{1,0:T(8,128)(2,1)} %get-tuple-element.61), channel_id=1, source_target_pairs={{0,1},{1,2},{2,3},{3,0},{4,5},{5,6},{6,7},{7,4},{8,9},{9,10},{10,1... | collective-permute-start | bytes 2752520 | tf_op jit(solution)/shard_map/ppermute | solution.py:421
  32.5 40.0 %collective-permute-start.4 = (bf16[256,1792]{1,0:T(8,128)(2,1)}, bf16[256,1792]{1,0:T(8,128)(2,1)}, u32[]{:S(2)}, u32[]{:S(2)}) collective-permute-start(bf16[256,1792]{1,0:T(8,128)(2,1)} %get-tuple-element.60), channel_id=1, source_target_pairs={{0,2},{1,3},{2,0},{3,1},{4,6},{5,7},{6,4},{7,5},{8,10},{9,11},{10,... | collective-permute-start | bytes 2752520 | tf_op jit(solution)/shard_map/ppermute | solution.py:421
  33.3 41.5 %collective-permute-start.5 = (bf16[256,1792]{1,0:T(8,128)(2,1)}, bf16[256,1792]{1,0:T(8,128)(2,1)}, u32[]{:S(2)}, u32[]{:S(2)}) collective-permute-start(bf16[256,1792]{1,0:T(8,128)(2,1)} %get-tuple-element.59), channel_id=1, source_target_pairs={{0,3},{1,0},{2,1},{3,2},{4,7},{5,4},{6,5},{7,6},{8,11},{9,8},{10,9... | collective-permute-start | bytes 2752520 | tf_op jit(solution)/shard_map/ppermute | solution.py:421
  79.9 19.7 %all-to-all-start = ((bf16[32,24,224]{2,1,0:T(8,128)(2,1)}), bf16[32,24,224]{2,1,0:T(8,128)(2,1)S(1)}, u32[]{:S(2)}, u32[]{:S(2)}) async-start(bf16[32,24,224]{2,1,0:T(8,128)(2,1)} %shard_map.147), calls=%async_computation | async-start | bytes 786432 | tf_op jit(solution)/shard_map/all_to_all | solution.py:455
  99.8 5.5 %collective-permute-start.6 = (bf16[24,1792]{1,0:T(8,128)(2,1)S(1)}, bf16[24,1792]{1,0:T(8,128)(2,1)S(1)}, u32[]{:S(2)}, u32[]{:S(2)}) collective-permute-start(bf16[24,1792]{1,0:T(8,128)(2,1)S(1)} %get-tuple-element.38), channel_id=1, source_target_pairs={{0,1},{1,2},{2,3},{3,0},{4,5},{5,6},{6,7},{7,4},{8,9},{9,10},{10,1... | collective-permute-start | bytes 258056 | tf_op jit(solution)/shard_map/ppermute | solution.py:421
  99.9 7.9 %collective-permute-start.7 = (bf16[24,1792]{1,0:T(8,128)(2,1)S(1)}, bf16[24,1792]{1,0:T(8,128)(2,1)S(1)}, u32[]{:S(2)}, u32[]{:S(2)}) collective-permute-start(bf16[24,1792]{1,0:T(8,128)(2,1)S(1)} %get-tuple-element.39), channel_id=1, source_target_pairs={{0,2},{1,3},{2,0},{3,1},{4,6},{5,7},{6,4},{7,5},{8,10},{9,11},{10,... | collective-permute-start | bytes 258056 | tf_op jit(solution)/shard_map/ppermute | solution.py:421
  103.2 4.6 %collective-permute-start.8 = (bf16[24,1792]{1,0:T(8,128)(2,1)S(1)}, bf16[24,1792]{1,0:T(8,128)(2,1)S(1)}, u32[]{:S(2)}, u32[]{:S(2)}) collective-permute-start(bf16[24,1792]{1,0:T(8,128)(2,1)S(1)} %get-tuple-element.40), channel_id=1, source_target_pairs={{0,3},{1,0},{2,1},{3,2},{4,7},{5,4},{6,5},{7,6},{8,11},{9,8},{10,9... | collective-permute-start | bytes 258056 | tf_op jit(solution)/shard_map/ppermute | solution.py:421
  145.9 4.9 %collective-permute-start.10 = (bf16[128,256]{1,0:T(8,128)(2,1)S(1)}, bf16[128,256]{1,0:T(8,128)(2,1)S(1)}, u32[]{:S(2)}, u32[]{:S(2)}) collective-permute-start(bf16[128,256]{1,0:T(8,128)(2,1)S(1)} %shard_map.150.refs_0_), channel_id=1, source_target_pairs={{0,2},{1,3},{2,0},{3,1},{4,6},{5,7},{6,4},{7,5},{8,10},{9,11},{10,... | collective-permute-start | bytes 196616 | tf_op jit(solution)/shard_map/ppermute | solution.py:418
  146.1 4.6 %collective-permute-start.11 = (bf16[128,256]{1,0:T(8,128)(2,1)S(1)}, bf16[128,256]{1,0:T(8,128)(2,1)S(1)}, u32[]{:S(2)}, u32[]{:S(2)}) collective-permute-start(bf16[128,256]{1,0:T(8,128)(2,1)S(1)} %shard_map.150.refs_0_), channel_id=1, source_target_pairs={{0,3},{1,0},{2,1},{3,2},{4,7},{5,4},{6,5},{7,6},{8,11},{9,8},{10,9... | collective-permute-start | bytes 196616 | tf_op jit(solution)/shard_map/ppermute | solution.py:418
  148.9 4.3 %collective-permute-start.9 = (bf16[128,256]{1,0:T(8,128)(2,1)S(1)}, bf16[128,256]{1,0:T(8,128)(2,1)S(1)}, u32[]{:S(2)}, u32[]{:S(2)}) collective-permute-start(bf16[128,256]{1,0:T(8,128)(2,1)S(1)} %shard_map.150.refs_0_), channel_id=1, source_target_pairs={{0,1},{1,2},{2,3},{3,0},{4,5},{5,6},{6,7},{7,4},{8,9},{9,10},{10,1... | collective-permute-start | bytes 196616 | tf_op jit(solution)/shard_map/ppermute | solution.py:418
  156.7 16.6 %all-to-all-start.2 = ((bf16[32,8,896]{2,1,0:T(8,128)(2,1)}), bf16[32,8,896]{2,1,0:T(8,128)(2,1)S(1)}, u32[]{:S(2)}, u32[]{:S(2)}) async-start(bf16[32,8,896]{2,1,0:T(8,128)(2,1)} %bitcast.30), calls=%async_computation.2 | async-start | bytes 917504 | tf_op jit(solution)/shard_map/all_to_all | solution.py:485
  162.2 4.0 %collective-permute-start.12 = (f32[8,128]{1,0:T(8,128)S(1)}, f32[8,128]{1,0:T(8,128)S(1)}, u32[]{:S(2)}, u32[]{:S(2)}) collective-permute-start(f32[8,128]{1,0:T(8,128)S(1)} %get-tuple-element.48.refs_3_), channel_id=1, source_target_pairs={{0,1},{1,2},{2,3},{3,0},{4,5},{5,6},{6,7},{7,4},{8,9},{9,10},{10,1... | collective-permute-start | bytes 12296 | tf_op jit(solution)/shard_map/ppermute | solution.py:418
  162.3 4.3 %collective-permute-start.13 = (f32[8,128]{1,0:T(8,128)S(1)}, f32[8,128]{1,0:T(8,128)S(1)}, u32[]{:S(2)}, u32[]{:S(2)}) collective-permute-start(f32[8,128]{1,0:T(8,128)S(1)} %get-tuple-element.48.refs_3_), channel_id=1, source_target_pairs={{0,2},{1,3},{2,0},{3,1},{4,6},{5,7},{6,4},{7,5},{8,10},{9,11},{10,... | collective-permute-start | bytes 12296 | tf_op jit(solution)/shard_map/ppermute | solution.py:418
  163.2 3.7 %collective-permute-start.14 = (f32[8,128]{1,0:T(8,128)S(1)}, f32[8,128]{1,0:T(8,128)S(1)}, u32[]{:S(2)}, u32[]{:S(2)}) collective-permute-start(f32[8,128]{1,0:T(8,128)S(1)} %get-tuple-element.48.refs_3_), channel_id=1, source_target_pairs={{0,3},{1,0},{2,1},{3,2},{4,7},{5,4},{6,5},{7,6},{8,11},{9,8},{10,9... | collective-permute-start | bytes 12296 | tf_op jit(solution)/shard_map/ppermute | solution.py:418
  209.9 4.9 %collective-permute-start.15 = (bf16[128,256]{1,0:T(8,128)(2,1)S(1)}, bf16[128,256]{1,0:T(8,128)(2,1)S(1)}, u32[]{:S(2)}, u32[]{:S(2)}) collective-permute-start(bf16[128,256]{1,0:T(8,128)(2,1)S(1)} %shard_map.153.refs_0_), channel_id=1, source_target_pairs={{0,1},{1,2},{2,3},{3,0},{4,5},{5,6},{6,7},{7,4},{8,9},{9,10},{10,1... | collective-permute-start | bytes 196616 | tf_op jit(solution)/shard_map/ppermute | solution.py:418
  210.3 5.6 %collective-permute-start.16 = (bf16[128,256]{1,0:T(8,128)(2,1)S(1)}, bf16[128,256]{1,0:T(8,128)(2,1)S(1)}, u32[]{:S(2)}, u32[]{:S(2)}) collective-permute-start(bf16[128,256]{1,0:T(8,128)(2,1)S(1)} %shard_map.153.refs_0_), channel_id=1, source_target_pairs={{0,2},{1,3},{2,0},{3,1},{4,6},{5,7},{6,4},{7,5},{8,10},{9,11},{10,... | collective-permute-start | bytes 196616 | tf_op jit(solution)/shard_map/ppermute | solution.py:418
  211.2 5.1 %collective-permute-start.17 = (bf16[128,256]{1,0:T(8,128)(2,1)S(1)}, bf16[128,256]{1,0:T(8,128)(2,1)S(1)}, u32[]{:S(2)}, u32[]{:S(2)}) collective-permute-start(bf16[128,256]{1,0:T(8,128)(2,1)S(1)} %shard_map.153.refs_0_), channel_id=1, source_target_pairs={{0,3},{1,0},{2,1},{3,2},{4,7},{5,4},{6,5},{7,6},{8,11},{9,8},{10,9... | collective-permute-start | bytes 196616 | tf_op jit(solution)/shard_map/ppermute | solution.py:418
  219.8 16.0 %all-to-all-start.4 = ((bf16[32,8,896]{2,1,0:T(8,128)(2,1)}), bf16[32,8,896]{2,1,0:T(8,128)(2,1)S(1)}, u32[]{:S(2)}, u32[]{:S(2)}) async-start(bf16[32,8,896]{2,1,0:T(8,128)(2,1)} %bitcast.35), calls=%async_computation.4 | async-start | bytes 917504 | tf_op jit(solution)/shard_map/all_to_all | solution.py:485
  224.7 4.0 %collective-permute-start.18 = (f32[8,128]{1,0:T(8,128)S(1)}, f32[8,128]{1,0:T(8,128)S(1)}, u32[]{:S(2)}, u32[]{:S(2)}) collective-permute-start(f32[8,128]{1,0:T(8,128)S(1)} %get-tuple-element.54.refs_3_), channel_id=1, source_target_pairs={{0,1},{1,2},{2,3},{3,0},{4,5},{5,6},{6,7},{7,4},{8,9},{9,10},{10,1... | collective-permute-start | bytes 12296 | tf_op jit(solution)/shard_map/ppermute | solution.py:418
  225.4 4.0 %collective-permute-start.19 = (f32[8,128]{1,0:T(8,128)S(1)}, f32[8,128]{1,0:T(8,128)S(1)}, u32[]{:S(2)}, u32[]{:S(2)}) collective-permute-start(f32[8,128]{1,0:T(8,128)S(1)} %get-tuple-element.54.refs_3_), channel_id=1, source_target_pairs={{0,2},{1,3},{2,0},{3,1},{4,6},{5,7},{6,4},{7,5},{8,10},{9,11},{10,... | collective-permute-start | bytes 12296 | tf_op jit(solution)/shard_map/ppermute | solution.py:418
  228.2 2.8 collective-permute-start.20
  273.6 4.9 %collective-permute-start.21 = (bf16[128,256]{1,0:T(8,128)(2,1)S(1)}, bf16[128,256]{1,0:T(8,128)(2,1)S(1)}, u32[]{:S(2)}, u32[]{:S(2)}) collective-permute-start(bf16[128,256]{1,0:T(8,128)(2,1)S(1)} %shard_map.156.refs_0_), channel_id=1, source_target_pairs={{0,1},{1,2},{2,3},{3,0},{4,5},{5,6},{6,7},{7,4},{8,9},{9,10},{10,1... | collective-permute-start | bytes 196616 | tf_op jit(solution)/shard_map/ppermute | solution.py:418
  274.0 5.6 %collective-permute-start.22 = (bf16[128,256]{1,0:T(8,128)(2,1)S(1)}, bf16[128,256]{1,0:T(8,128)(2,1)S(1)}, u32[]{:S(2)}, u32[]{:S(2)}) collective-permute-start(bf16[128,256]{1,0:T(8,128)(2,1)S(1)} %shard_map.156.refs_0_), channel_id=1, source_target_pairs={{0,2},{1,3},{2,0},{3,1},{4,6},{5,7},{6,4},{7,5},{8,10},{9,11},{10,... | collective-permute-start | bytes 196616 | tf_op jit(solution)/shard_map/ppermute | solution.py:418
  275.0 5.1 %collective-permute-start.23 = (bf16[128,256]{1,0:T(8,128)(2,1)S(1)}, bf16[128,256]{1,0:T(8,128)(2,1)S(1)}, u32[]{:S(2)}, u32[]{:S(2)}) collective-permute-start(bf16[128,256]{1,0:T(8,128)(2,1)S(1)} %shard_map.156.refs_0_), channel_id=1, source_target_pairs={{0,3},{1,0},{2,1},{3,2},{4,7},{5,4},{6,5},{7,6},{8,11},{9,8},{10,9... | collective-permute-start | bytes 196616 | tf_op jit(solution)/shard_map/ppermute | solution.py:418
  283.6 16.0 %all-to-all-start.6 = ((bf16[32,8,896]{2,1,0:T(8,128)(2,1)}), bf16[32,8,896]{2,1,0:T(8,128)(2,1)S(1)}, u32[]{:S(2)}, u32[]{:S(2)}) async-start(bf16[32,8,896]{2,1,0:T(8,128)(2,1)} %bitcast.40), calls=%async_computation.6 | async-start | bytes 917504 | tf_op jit(solution)/shard_map/all_to_all | solution.py:485
  288.5 4.0 %collective-permute-start.24 = (f32[8,128]{1,0:T(8,128)S(1)}, f32[8,128]{1,0:T(8,128)S(1)}, u32[]{:S(2)}, u32[]{:S(2)}) collective-permute-start(f32[8,128]{1,0:T(8,128)S(1)} %get-tuple-element.58.refs_3_), channel_id=1, source_target_pairs={{0,1},{1,2},{2,3},{3,0},{4,5},{5,6},{6,7},{7,4},{8,9},{9,10},{10,1... | collective-permute-start | bytes 12296 | tf_op jit(solution)/shard_map/ppermute | solution.py:418
  289.2 4.0 %collective-permute-start.25 = (f32[8,128]{1,0:T(8,128)S(1)}, f32[8,128]{1,0:T(8,128)S(1)}, u32[]{:S(2)}, u32[]{:S(2)}) collective-permute-start(f32[8,128]{1,0:T(8,128)S(1)} %get-tuple-element.58.refs_3_), channel_id=1, source_target_pairs={{0,2},{1,3},{2,0},{3,1},{4,6},{5,7},{6,4},{7,5},{8,10},{9,11},{10,... | collective-permute-start | bytes 12296 | tf_op jit(solution)/shard_map/ppermute | solution.py:418
  292.0 2.8 collective-permute-start.26
  (13 other events, 244.1 us)
Sparse Core Ops, SparseCore 0:
  22.4 52.8 all-gather.1
